TPU v7x, 32 devices: a whole 2x2x4 slice. The times are simulated.
32 devices in a mesh: seq: 4 (over y, x), tp: 8 (over z, core).
Axes of the slice: x: 2, y: 2, z: 4, core: 2. Of those that a mesh axis runs over, the one named last changes fastest.
Arguments:
- inputs: bfloat16 [8, 1024, 1280], P(None, 'seq'), may hold values from -6 to 6
- starts: int32 [8, 1024], P(None, 'seq'), may hold values from 0 to 1, as said below
- first_proj: bfloat16 [1280, 640], P(None, 'tp'), may hold values from -0.15625 to 0.15625
- dilated_conv: bfloat16 [5, 640, 640], P(None, None, 'tp'), may hold values from -0.109375 to 0.109375
- last_proj: bfloat16 [640, 1280], P('tp'), may hold values from -0.25 to 0.25
- first_norm_gain: float32 [1280], replicated, may hold values from 0.25 to 1.75
- second_norm_gain: float32 [640], P('tp'), may hold values from 0.25 to 1.75
- third_norm_gain: float32 [640], P('tp'), may hold values from 0.25 to 1.75
- cotangent: bfloat16 [8, 1024, 1280], P(None, 'seq', 'tp'), may hold values from -6 to 6
Outputs:
- outputs: bfloat16 [8, 1024, 1280], P(None, 'seq', 'tp')
- grad_inputs: bfloat16 [8, 1024, 1280], P(None, 'seq')
- grad_first: float32 [1280, 640], P(None, 'tp')
- grad_conv: float32 [5, 640, 640], P(None, None, 'tp')
- grad_last: float32 [640, 1280], P('tp')
- grad_gain_outer: float32 [1280], P('tp')
- second_gain_gradient: float32 [640], P('tp')
- third_gain_gradient: float32 [640], P('tp')
Inputs may be any that keep to these rules, and one draw needn't show every extreme that they name: `starts`: 1 where a new document begins in its packed row; in one packed row, drawn from the seed, no document begins; the other rows begin about 8 documents each.
All inputs are finite; a program needn't handle non-finite values.
Results may differ from a plain program's by a relative error of at most 0.0073.
Values may be sent and summed in bfloat16 or wider, within the bound.
A program may use at most 256 MiB of HBM per device.

v0:
```python
import jax
import jax.numpy as jnp
from jax import lax
from jax.sharding import PartitionSpec as P

TAP_COUNT = 5
DILATION_STEP = 2
TAP_REACH = 4


EPS = 1e-05


def extended(cells, sides, width):
    for axis, dim in sides:
        count = lax.axis_size(axis)
        ends = count - 1
        head = lax.slice_in_dim(cells, 0, width, axis=dim)
        tail = lax.slice_in_dim(cells, cells.shape[dim] - width, cells.shape[dim], axis=dim)
        cells = jnp.concatenate(
            [
                lax.ppermute(tail, axis, [(i, (i + 1) % count) for i in range(ends)]),
                cells,
                lax.ppermute(head, axis, [((i + 1) % count, i) for i in range(ends)]),
            ],
            axis=dim,
        )
    return cells


def exact_gelu_fn(values):
    return jax.nn.gelu(values, approximate=False)


def gelu_back(values, grad):
    unused, pullback = jax.vjp(exact_gelu_fn, values)
    return pullback(grad)[0]


def norm_stats(total, squares, width):
    centre_tap = total[..., None] / width
    spread = squares[..., None] / width - centre_tap * centre_tap
    return (centre_tap, lax.rsqrt(spread + EPS))


def first_norm_fn(values, norm_gain):
    input_as_float = values.astype(jnp.float32)
    centre_tap = jnp.mean(input_as_float, axis=-1, keepdims=True)
    spread = (
        jnp.mean(input_as_float * input_as_float, axis=-1, keepdims=True) - centre_tap * centre_tap
    )
    inverse_deviation = lax.rsqrt(spread + EPS)
    normed_input = (input_as_float - centre_tap) * inverse_deviation
    pre_norm_input = normed_input * norm_gain
    return (
        input_as_float,
        inverse_deviation,
        normed_input,
        pre_norm_input,
        exact_gelu_fn(pre_norm_input).astype(jnp.bfloat16),
    )


def build_taps(wide_active, rim_flags, positions, tap_offsets):
    counts = jnp.cumsum(rim_flags.astype(jnp.float32), axis=1)
    centre_counts = counts[:, TAP_REACH : TAP_REACH + positions]
    keep_masks = [
        (
            counts[:, TAP_REACH + tap_offset : TAP_REACH + tap_offset + positions] == centre_counts
        ).astype(jnp.bfloat16)
        for tap_offset in tap_offsets
    ]
    taps = jnp.concatenate(
        [
            wide_active[
                :,
                TAP_REACH
                + tap_offsets[tap_position_index] : TAP_REACH
                + tap_offsets[tap_position_index]
                + positions,
                :,
            ]
            * keep_masks[tap_position_index][..., None]
            for tap_position_index in range(TAP_COUNT)
        ],
        axis=2,
    )
    return (taps, keep_masks)


def back_stack(rim_grad, keep_masks, positions, tap_offsets):
    return jnp.stack(
        [
            rim_grad[
                :,
                TAP_REACH
                - tap_offsets[tap_position_index] : TAP_REACH
                - tap_offsets[tap_position_index]
                + positions,
                :,
            ]
            * keep_masks[TAP_COUNT - 1 - tap_position_index][..., None]
            for tap_position_index in range(TAP_COUNT)
        ],
        axis=2,
    )


def shards(
    inputs,
    starts,
    first_proj,
    dilated_conv,
    last_proj,
    first_norm_gain,
    second_norm_gain,
    third_norm_gain,
    cotangent,
):
    slot = lax.axis_index("tp")
    share = cotangent.shape[2]
    positions = inputs.shape[1]
    inner_local = first_proj.shape[1]
    inner_block = dilated_conv.shape[1]
    tap_offsets = [
        DILATION_STEP * tap_position_index - TAP_REACH for tap_position_index in range(TAP_COUNT)
    ]
    input_as_float, first_inverse_deviation, first_normed, first_pre_norm, outer_activation = (
        first_norm_fn(inputs, first_norm_gain)
    )
    second_hidden = jnp.einsum(
        "bpd,dh->bph", outer_activation, first_proj, preferred_element_type=jnp.float32
    )
    total_mid, squares_mid = lax.psum(
        (jnp.sum(second_hidden, -1), jnp.sum(second_hidden * second_hidden, -1)), "tp"
    )
    second_mean, second_inverse_deviation = norm_stats(total_mid, squares_mid, inner_block)
    second_normed = (second_hidden - second_mean) * second_inverse_deviation
    second_pre_norm = second_normed * second_norm_gain
    active_mid = exact_gelu_fn(second_pre_norm).astype(jnp.bfloat16)
    rim_active, rim_flags = (
        extended(active_mid, (("seq", 1),), TAP_REACH),
        extended(starts.astype(jnp.bfloat16), (("seq", 1),), TAP_REACH),
    )
    wide_active = lax.all_gather(rim_active, "tp", axis=2, tiled=True)
    taps, keep_masks = build_taps(wide_active, rim_flags, positions, tap_offsets)
    kernel = dilated_conv.reshape(TAP_COUNT * inner_block, inner_local)
    third_hidden = jnp.einsum("bpc,ch->bph", taps, kernel, preferred_element_type=jnp.float32)
    total_last, squares_last = lax.psum(
        (jnp.sum(third_hidden, -1), jnp.sum(third_hidden * third_hidden, -1)), "tp"
    )
    third_mean, third_inverse_deviation = norm_stats(total_last, squares_last, inner_block)
    third_normed = (third_hidden - third_mean) * third_inverse_deviation
    third_pre_norm = third_normed * third_norm_gain
    active_last = exact_gelu_fn(third_pre_norm).astype(jnp.bfloat16)
    partial_out = jnp.einsum(
        "bph,hd->bpd", active_last, last_proj, preferred_element_type=jnp.float32
    )
    mixed = lax.psum_scatter(partial_out, "tp", scatter_dimension=2, tiled=True)
    residual = lax.dynamic_slice_in_dim(input_as_float, slot * share, share, 2)
    outputs = (residual + mixed).astype(jnp.bfloat16)
    grad_full = lax.all_gather(cotangent, "tp", axis=2, tiled=True)
    grad_last = jnp.einsum(
        "bph,bpd->hd", active_last, grad_full, preferred_element_type=jnp.float32
    )
    dact_last = jnp.einsum("bpd,hd->bph", grad_full, last_proj, preferred_element_type=jnp.float32)
    third_pre_gradient = gelu_back(third_pre_norm, dact_last)
    third_gain_gradient = jnp.sum(third_pre_gradient * third_normed, axis=(0, 1))
    third_normed_gradient = third_pre_gradient * third_norm_gain
    plain_sum_total, cross_sum_total = lax.psum(
        (jnp.sum(third_normed_gradient, -1), jnp.sum(third_normed_gradient * third_normed, -1)),
        "tp",
    )
    dhidden_last = (
        third_inverse_deviation
        * (
            third_normed_gradient
            - plain_sum_total[..., None] / inner_block
            - third_normed * cross_sum_total[..., None] / inner_block
        )
    ).astype(jnp.bfloat16)
    rim_grad = extended(dhidden_last, (("seq", 1),), TAP_REACH)
    grad_conv = jnp.einsum(
        "bpc,bph->ch", taps, dhidden_last, preferred_element_type=jnp.float32
    ).reshape(TAP_COUNT, inner_block, inner_local)
    back_taps = back_stack(rim_grad, keep_masks, positions, tap_offsets)
    dwide = jnp.einsum("bpks,kcs->bpc", back_taps, dilated_conv, preferred_element_type=jnp.float32)
    dact_mid = lax.psum_scatter(dwide, "tp", scatter_dimension=2, tiled=True)
    second_pre_gradient = gelu_back(second_pre_norm, dact_mid)
    second_gain_gradient = jnp.sum(second_pre_gradient * second_normed, axis=(0, 1))
    second_normed_gradient = second_pre_gradient * second_norm_gain
    second_plain_sum, second_cross_sum = (
        lax.psum(jnp.sum(second_normed_gradient, -1).astype(jnp.bfloat16), "tp").astype(
            jnp.float32
        ),
        lax.psum(
            jnp.sum(second_normed_gradient * second_normed, -1).astype(jnp.bfloat16), "tp"
        ).astype(jnp.float32),
    )
    dhidden_mid = (
        second_inverse_deviation
        * (
            second_normed_gradient
            - second_plain_sum[..., None] / inner_block
            - second_normed * second_cross_sum[..., None] / inner_block
        )
    ).astype(jnp.bfloat16)
    grad_first = jnp.einsum(
        "bpd,bph->dh", outer_activation, dhidden_mid, preferred_element_type=jnp.float32
    )
    dact_outer = jnp.einsum(
        "bph,dh->bpd", dhidden_mid, first_proj, preferred_element_type=jnp.float32
    )
    dact_full = lax.psum(dact_outer, "tp")
    first_pre_gradient = gelu_back(first_pre_norm, dact_full)
    gain_gradient_whole = jnp.sum(first_pre_gradient * first_normed, axis=(0, 1))
    grad_gain_outer = lax.dynamic_slice_in_dim(gain_gradient_whole, slot * share, share, 0)
    first_normed_gradient = first_pre_gradient * first_norm_gain
    dinput_norm = first_inverse_deviation * (
        first_normed_gradient
        - jnp.mean(first_normed_gradient, -1, keepdims=True)
        - first_normed * jnp.mean(first_normed_gradient * first_normed, -1, keepdims=True)
    )
    grad_inputs = (grad_full.astype(jnp.float32) + dinput_norm).astype(jnp.bfloat16)
    summed = lax.psum(
        (
            grad_first,
            grad_conv,
            grad_last,
            grad_gain_outer,
            second_gain_gradient,
            third_gain_gradient,
        ),
        "seq",
    )
    return (outputs, grad_inputs, summed[0], summed[1], summed[2], summed[3], summed[4], summed[5])


def solution(mesh):
    placed = (
        P(None, "seq", None),
        P(None, "seq"),
        P(None, "tp"),
        P(None, None, "tp"),
        P("tp", None),
        P(),
        P("tp"),
        P("tp"),
        P(None, "seq", "tp"),
    )
    return jax.shard_map(
        shards,
        mesh=mesh,
        in_specs=placed,
        out_specs=(
            P(None, "seq", "tp"),
            P(None, "seq", None),
            P(None, "tp"),
            P(None, None, "tp"),
            P("tp", None),
            P("tp"),
            P("tp"),
            P("tp"),
        ),
        check_vma=False,
    )
```

profile of v0, /device:TPU:0, one launch (start us, length us, event | category | flops | bytes accessed | tf_op | source)
XLA Modules:
  0.0 736.8 jit_solution(8736009576201899195)
XLA Ops:
  7.2 7.8 %copy.26 = bf16[8,256,1280]{1,2,0:T(8,128)(2,1)} copy(bf16[8,256,1280]{2,1,0:T(8,128)(2,1)} %param.9) | data formatting | bytes 10485760 | tf_op args[0]
  15.0 3.9 convert_reduce_fusion
  18.9 27.5 %multiply_convert_fusion = (bf16[8,256,1280]{1,2,0:T(8,128)(2,1)S(1)}, f32[8,256,1280]{1,2,0:T(8,128)}) fusion(bf16[8,256,1280]{1,2,0:T(8,128)(2,1)} %copy.26, f32[1280]{0:T(1024)S(1)} %copy-done.10, f32[8,256]{1,0:T(8,128)S(1)} %get-tuple-element.73, f32[8,256]{1,0:T(8,128)S(1)} %get-tuple-element.72), kind=kLoop, calls=%fused_computation.6 | loop fusion | flops 180879360 | bytes 20993024 | tf_op jit(solution)/shard_map/convert_element_type | solution.py:60
  46.4 2.3 copy-done.2
  49.8 30.3 %all-reduce.3 = (f32[8,256]{1,0:T(8,128)S(1)}, f32[8,256]{1,0:T(8,128)S(1)}) all-reduce(f32[8,256]{1,0:T(8,128)S(1)} %get-tuple-element.38, f32[8,256]{1,0:T(8,128)S(1)} %get-tuple-element.37), channel_id=1, replica_groups=mesh['seq'=4,'tp'=8] {'tp'}, use_global_device_ids=true, to_apply=%region_5.0 | all-reduce | flops 4096 | bytes 32768 | tf_op jit(solution)/shard_map/psum | solution.py:134
  80.1 1.6 multiply_convert_fusion.4
  81.7 3.4 collective-permute-start
  85.2 1.3 collective-permute-start.1
  86.5 1.5 collective-permute-done
  88.0 4.4 collective-permute-done.1
  94.4 4.3 collective-permute-start.2
  98.7 1.5 collective-permute-start.3
  100.3 1.4 reshape.95
  101.7 2.4 collective-permute-done.3
  105.4 31.1 %all-gather.3.cloned.1.call-done = bf16[8,264,640]{1,2,0:T(8,128)(2,1)} async-done(((bf16[8,264,80]{1,2,0:T(8,128)(2,1)}), bf16[8,264,640]{1,2,0:T(8,128)(2,1)}) %all-gather.3.cloned.1.call-update) | async-done | bytes 2703376 | tf_op jit(solution)/shard_map/all_gather | solution.py:145
  136.5 2.3 fusion.10
  138.9 3.7 fusion.9
  142.6 1.5 fusion.8
  144.1 1.5 fusion.7
  145.7 1.5 fusion.6
  147.2 4.6 copy-done.1
  151.8 2.4 fusion.56
  154.2 28.4 %all-reduce.2 = (f32[8,256]{1,0:T(8,128)S(1)}, f32[8,256]{1,0:T(8,128)S(1)}) all-reduce(f32[8,256]{1,0:T(8,128)S(1)} %get-tuple-element.36, f32[8,256]{1,0:T(8,128)S(1)} %get-tuple-element.35), channel_id=1, replica_groups=mesh['seq'=4,'tp'=8] {'tp'}, use_global_device_ids=true, to_apply=%region_11.12 | all-reduce | flops 4096 | bytes 32768 | tf_op jit(solution)/shard_map/psum | solution.py:149
  182.7 10.9 %all-gather.5.cloned.1.call-done = bf16[8,256,1280]{1,2,0:T(8,128)(2,1)} async-done(((bf16[8,256,160]{1,2,0:T(8,128)(2,1)}), bf16[8,256,1280]{1,2,0:T(8,128)(2,1)}) %all-gather.5.cloned.1.call-update) | async-done | bytes 5242896 | tf_op jit(solution)/shard_map/all_gather | solution.py:162
  193.5 5.5 multiply_reduce_fusion.4
  199.0 26.8 %all-reduce.1 = (f32[8,256]{1,0:T(8,128)S(1)}, f32[8,256]{1,0:T(8,128)S(1)}) all-reduce(f32[8,256]{1,0:T(8,128)S(1)} %get-tuple-element.30, f32[8,256]{1,0:T(8,128)S(1)} %get-tuple-element.34), channel_id=1, replica_groups=mesh['seq'=4,'tp'=8] {'tp'}, use_global_device_ids=true, to_apply=%region_16.17 | all-reduce | flops 4096 | bytes 32768 | tf_op jit(solution)/shard_map/psum | solution.py:170
  227.5 4.6 collective-permute-start.5
  232.0 2.8 collective-permute-done.4
  235.7 5.0 convolution_bitcast_fusion.1
  240.8 8.8 %convolution_bitcast_fusion = f32[3200,80]{0,1:T(8,128)S(1)} fusion(bf16[8,256,3200]{1,2,0:T(8,128)(2,1)} %copy-done.1, bf16[8,256,80]{1,2,0:T(8,128)(2,1)S(1)} %multiply_convert_fusion.2), kind=kOutput, calls=%fused_computation.24 | convolution fusion | flops 1048576000 | bytes 14458880 | tf_op jit(solution)/shard_map/bpc,bph->ch/dot_general | solution.py:183
  249.6 1.4 reshape.92
  250.9 6.1 convolution_bitcast_fusion.2
  257.0 43.6 %reduce-scatter.5.cloned.1.call-done = f32[8,256,80]{1,2,0:T(8,128)} async-done(((f32[8,256,640]{1,2,0:T(8,128)}), f32[8,256,80]{1,2,0:T(8,128)}) %reduce-scatter.5.cloned.1.call-update) | async-done | bytes 655376 | tf_op jit(solution)/shard_map/reduce_scatter | solution.py:188
  300.6 1.8 multiply_reduce_fusion.5
  302.4 13.9 %all-reduce.6 = (bf16[8,256]{1,0:T(8,128)(2,1)S(1)}, bf16[8,256]{1,0:T(8,128)(2,1)S(1)}) all-reduce(bf16[8,256]{1,0:T(8,128)(2,1)S(1)} %get-tuple-element.32, bf16[8,256]{1,0:T(8,128)(2,1)S(1)} %get-tuple-element.33), channel_id=1, replica_groups=mesh['seq'=4,'tp'=8] {'tp'}, use_global_device_ids=true, to_apply=%region_21.22 | all-reduce | flops 4096 | bytes 16384 | tf_op jit(solution)/shard_map/psum | solution.py:196
  316.6 4.9 convolution_bitcast_fusion.3
  321.7 5.9 fusion.41
  327.9 6.4 fusion.39
  334.3 7.6 %convert_element_type.58 = f32[8,256,1280]{1,2,0:T(8,128)} convert(bf16[8,256,1280]{1,2,0:T(8,128)(2,1)} %copy.26) | non-fusion elementwise | flops 2621440 | bytes 15728640 | tf_op jit(solution)/shard_map/convert_element_type | solution.py:47
  341.9 54.3 %all-reduce.12.cloned.1.call-done = (f32[1280,80]{0,1:T(8,128)}, f32[5,640,80]{1,0,2:T(8,128)}, f32[80,1280]{1,0:T(8,128)}) async-done(((f32[1280,80]{0,1:T(8,128)}, f32[5,640,80]{1,0,2:T(8,128)}, f32[80,1280]{1,0:T(8,128)}), (f32[1280,80]{0,1:T(8,128)}, f32[5,640,80]{1,0,2:T(8,128)}, f32[80,1280]{1,0:T(8,128)})) %all-reduce.12.cloned.1.call-update) | async-done | bytes 1843216 | tf_op jit(solution)/shard_map/psum | solution.py:225
  396.2 2.6 copy.35
  398.8 214.7 %all-reduce.10.cloned.1.call-done = f32[8,256,1280]{1,2,0:T(8,128)} async-done(((f32[8,256,1280]{1,2,0:T(8,128)}), f32[8,256,1280]{1,2,0:T(8,128)}) %all-reduce.10.cloned.1.call-update) | async-done | bytes 10485776 | tf_op jit(solution)/shard_map/psum | solution.py:214
  613.5 13.8 %multiply_reduce_fusion = (f32[1280]{0:T(1024)S(1)}, f32[8,256]{1,0:T(8,128)S(1)}, f32[8,256]{1,0:T(8,128)S(1)}, f32[8,256,1280]{1,2,0:T(8,128)S(1)}) fusion(bf16[8,256,1280]{1,2,0:T(8,128)(2,1)} %copy.26, f32[8,256]{1,0:T(8,128)S(1)} %get-tuple-element.73, f32[8,256]{1,0:T(8,128)S(1)} %get-tuple-element.72, f32[1280]{0:T(1024)S(1)} %copy-done.11, ...), kind=kLoop, calls=%fused_computation.2 | loop fusion | flops 60287744 | bytes 36743168 | tf_op jit(solution)/shard_map/reduce_sum | solution.py:216
  627.4 7.8 %add_convert_fusion = bf16[8,256,1280]{1,2,0:T(8,128)(2,1)} fusion(bf16[8,256,1280]{1,2,0:T(8,128)(2,1)} %all-gather.5.cloned.1.call-done, f32[8,256,1280]{1,2,0:T(8,128)S(1)} %get-tuple-element.53, bf16[8,256,1280]{1,2,0:T(8,128)(2,1)S(1)} %bitcast.69, f32[8,256]{1,0:T(8,128)S(1)} %get-tuple-element.79, f32[8,256]{1,0:T(8,128)S(1)} %get-tuple-element.80, ...), kind=kLoop, calls=%fused_computation.3 | loop fusion | flops 28835840 | bytes 26252288 | tf_op jit(solution)/shard_map/convert_element_type | solution.py:224
  635.3 7.9 %copy.34 = bf16[8,256,1280]{2,1,0:T(8,128)(2,1)} copy(bf16[8,256,1280]{1,2,0:T(8,128)(2,1)} %add_convert_fusion) | data formatting | bytes 10485760
  643.3 10.7 %all-reduce.4 = (f32[160]{0:T(256)}, f32[80]{0:T(128)}, f32[80]{0:T(128)}) all-reduce(f32[160]{0:T(256)S(1)} %dynamic_slice.7, f32[80]{0:T(128)S(1)} %get-tuple-element.31, f32[80]{0:T(128)S(1)} %copy-done.22), channel_id=1, replica_groups=mesh['seq'=4,'tp'=8] {'seq'}, use_global_device_ids=true, to_apply=%region_29.30 | all-reduce | flops 320 | bytes 2560 | tf_op jit(solution)/shard_map/psum | solution.py:225
  654.0 71.3 %reduce-scatter.3.cloned.1.call-done = f32[8,256,160]{1,2,0:T(8,128)} async-done(((f32[8,256,1280]{1,2,0:T(8,128)}), f32[8,256,160]{1,2,0:T(8,128)}) %reduce-scatter.3.cloned.1.call-update) | async-done | bytes 1310736 | tf_op jit(solution)/shard_map/reduce_scatter | solution.py:159
  725.3 2.7 add_convert_fusion.1
  (94 shorter events, 9.5 us)
Async XLA Ops:
  7.2 186.4 %copy-start = (bf16[80,1280]{1,0:T(8,128)(2,1)S(1)}, bf16[80,1280]{1,0:T(8,128)(2,1)}, u32[]{:S(2)}) copy-start(bf16[80,1280]{1,0:T(8,128)(2,1)} %param.13) | copy-start | bytes 614404
  7.2 11.7 %copy-start.10 = (f32[1280]{0:T(1024)S(1)}, f32[1280]{0:T(1024)}, u32[]{:S(2)}) copy-start(f32[1280]{0:T(1024)} %param.14) | copy-start | bytes 15364
  7.2 129.3 %all-gather.3.cloned.1.call-start = ((), (), s32[]{:S(2)}) async-start(), calls=%async_computation.2 | async-start | bytes 4423680 | tf_op jit(solution)/shard_map/all_gather | solution.py:145
  18.9 29.8 %copy-start.5 = (bf16[1280,80]{0,1:T(8,128)(2,1)S(1)}, bf16[1280,80]{0,1:T(8,128)(2,1)}, u32[]{:S(2)}) copy-start(bf16[1280,80]{0,1:T(8,128)(2,1)} %param.11) | copy-start | bytes 614404
  18.9 61.2 %copy-start.17 = (f32[80]{0:T(128)S(1)}, f32[80]{0:T(128)}, u32[]{:S(2)}) copy-start(f32[80]{0:T(128)} %param.15) | copy-start | bytes 964
  46.4 2.3 copy-start.2
  46.4 47.9 %copy-start.16 = (s32[8,256]{1,0:T(8,128)S(1)}, s32[8,256]{1,0:T(8,128)}, u32[]{:S(2)}) copy-start(s32[8,256]{1,0:T(8,128)} %param.10) | copy-start | bytes 24580
  46.4 53.7 %copy-start.7 = (bf16[5,640,80]{1,2,0:T(8,128)(2,1)S(1)}, bf16[5,640,80]{1,2,0:T(8,128)(2,1)}, u32[]{:S(2)}) copy-start(bf16[5,640,80]{1,2,0:T(8,128)(2,1)} %param.12) | copy-start | bytes 1536004
  81.7 6.2 collective-permute-start
  85.2 7.2 collective-permute-start.1
  93.5 100.0 %all-gather.5.cloned.1.call-start = ((), (), s32[]{:S(2)}) async-start(), calls=%async_computation.4 | async-start | bytes 5898240 | tf_op jit(solution)/shard_map/all_gather | solution.py:162
  94.2 206.4 %reduce-scatter.5.cloned.1.call-start = ((), (), s32[]{:S(2)}) async-start(), calls=%async_computation.5 | async-start | bytes 5898240 | tf_op jit(solution)/shard_map/reduce_scatter | solution.py:188
  94.4 7.4 collective-permute-start.2
  98.7 5.5 collective-permute-start.3
  136.5 6.1 copy-start.3
  138.9 12.9 %copy-start.4 = (bf16[3200,80,1]{0,1,2:T(8,128)(2,1)S(1)}, bf16[3200,80,1]{0,1,2:T(8,128)(2,1)}, u32[]{:S(2)}) copy-start(bf16[3200,80,1]{0,1,2:T(8,128)(2,1)} %reshape.95) | copy-start | bytes 1536004
  145.7 47.9 %copy-start.20 = (f32[80]{0:T(128)S(1)}, f32[80]{0:T(128)}, u32[]{:S(2)}) copy-start(f32[80]{0:T(128)} %param.16) | copy-start | bytes 964
  147.2 4.6 copy-start.1
  182.6 43.1 %copy-start.12 = (f32[8,256]{1,0:T(8,128)}, f32[8,256]{1,0:T(8,128)S(1)}, u32[]{:S(2)}) copy-start(f32[8,256]{1,0:T(8,128)S(1)} %get-tuple-element.68) | copy-start | bytes 24580
  182.6 43.1 %copy-start.14 = (f32[8,256]{1,0:T(8,128)}, f32[8,256]{1,0:T(8,128)S(1)}, u32[]{:S(2)}) copy-start(f32[8,256]{1,0:T(8,128)S(1)} %get-tuple-element.69) | copy-start | bytes 24580
  226.2 8.7 %collective-permute-start.4 = (bf16[8,4,80]{1,2,0:T(8,128)(2,1)S(1)}, bf16[8,4,80]{1,2,0:T(8,128)(2,1)S(1)}, u32[]{:S(2)}, u32[]{:S(2)}) collective-permute-start(bf16[8,4,80]{1,2,0:T(8,128)(2,1)S(1)} %get-tuple-element.60), channel_id=1, source_target_pairs={{8,0},{16,8},{24,16},{9,1},{17,9},{25,17},{10,2},{18,10},{26,18},{... | collective-permute-start | bytes 15368 | tf_op jit(solution)/shard_map/ppermute | solution.py:24
  227.5 7.9 %collective-permute-start.5 = (bf16[8,4,80]{1,2,0:T(8,128)(2,1)S(1)}, bf16[8,4,80]{1,2,0:T(8,128)(2,1)S(1)}, u32[]{:S(2)}, u32[]{:S(2)}) collective-permute-start(bf16[8,4,80]{1,2,0:T(8,128)(2,1)S(1)} %get-tuple-element.59), channel_id=1, source_target_pairs={{0,8},{8,16},{16,24},{1,9},{9,17},{17,25},{2,10},{10,18},{18,26},{... | collective-permute-start | bytes 15368 | tf_op jit(solution)/shard_map/ppermute | solution.py:22
  240.7 155.5 %all-reduce.12.cloned.1.call-start = ((), (), s32[]{:S(2)}) async-start(), calls=%async_computation.7 | async-start | bytes 4915200 | tf_op jit(solution)/shard_map/psum | solution.py:225
  249.5 51.1 %copy-start.18 = (f32[80]{0:T(128)S(1)}, f32[80]{0:T(128)}, u32[]{:S(2)}) copy-start(f32[80]{0:T(128)} %param.15) | copy-start | bytes 964
  250.9 65.4 %copy-start.19 = (f32[80]{0:T(128)S(1)}, f32[80]{0:T(128)}, u32[]{:S(2)}) copy-start(f32[80]{0:T(128)} %param.15) | copy-start | bytes 964
  257.0 64.7 %copy-start.6 = (bf16[1280,80]{0,1:T(8,128)(2,1)S(1)}, bf16[1280,80]{0,1:T(8,128)(2,1)}, u32[]{:S(2)}) copy-start(bf16[1280,80]{0,1:T(8,128)(2,1)} %param.11) | copy-start | bytes 614404
  321.6 6.3 copy-start.13
  321.6 6.3 copy-start.15
  321.6 6.3 copy-start.21
  321.6 291.9 %all-reduce.10.cloned.1.call-start = ((), (), s32[]{:S(2)}) async-start(), calls=%async_computation.6 | async-start | bytes 20971520 | tf_op jit(solution)/shard_map/psum | solution.py:214
  327.5 397.8 %reduce-scatter.3.cloned.1.call-start = ((), (), s32[]{:S(2)}) async-start(), calls=%async_computation.3 | async-start | bytes 11796480 | tf_op jit(solution)/shard_map/reduce_scatter | solution.py:159
  334.3 279.2 %copy-start.11 = (f32[1280]{0:T(1024)S(1)}, f32[1280]{0:T(1024)}, u32[]{:S(2)}) copy-start(f32[1280]{0:T(1024)} %param.14) | copy-start | bytes 15364
  334.3 293.1 %slice-start = ((s8[5242880]{0:T(1024)(128)(4,1)}), s8[1048576]{0:T(1024)(128)(4,1)S(1)}, s32[]{:S(2)}) async-start(s8[5242880]{0:T(1024)(128)(4,1)} %bitcast.68), calls=%async_computation.8 | async-start | bytes 2097152
  613.5 13.9 %slice-start.1 = ((s8[5242880]{0:T(1024)(128)(4,1)}), s8[4194304]{0:T(1024)(128)(4,1)S(1)}, s32[]{:S(2)}) async-start(s8[5242880]{0:T(1024)(128)(4,1)} %bitcast.68), calls=%async_computation.9 | async-start | bytes 8388608
  635.3 8.0 %copy-start.22 = (f32[80]{0:T(128)S(1)}, f32[80]{0:T(128)}, u32[]{:S(2)}) copy-start(f32[80]{0:T(128)} %get-tuple-element.29) | copy-start | bytes 964
  635.3 92.7 %copy-start.9 = (f32[1280,80]{0,1:T(8,128)S(1)}, f32[1280,80]{0,1:T(8,128)}, u32[]{:S(2)}) copy-start(f32[1280,80]{0,1:T(8,128)} %get-tuple-element.83) | copy-start | bytes 1228804
  635.3 93.5 %copy-start.8 = (f32[80,1280]{1,0:T(8,128)S(1)}, f32[80,1280]{1,0:T(8,128)}, u32[]{:S(2)}) copy-start(f32[80,1280]{1,0:T(8,128)} %get-tuple-element.85) | copy-start | bytes 1228804
Sparse Core Ops, SparseCore 0:
  93.6 42.9 all-gather.2
  138.1 55.3 all-gather.4
  240.9 59.7 reduce-scatter.4
  321.7 74.4 all-reduce.11
  398.4 215.0 all-reduce.9
  615.7 109.5 reduce-scatter.2
where the time goes:
time: 743 us; the launch traced here: 737 us
  waiting for transfers between devices  438 us (59%)
  blocking collectives  110 us (15%)
  other arithmetic  80.8 us (11%)
  matrix products  45.9 us (6%)
  local copies, waits for them, and re-layouts  30.3 us (4%)
  starting transfers between devices  16.8 us (2%)
  between operations  15 us (2%)
    psum x1, waiting for transfers between devices, shards(): dact_full = lax.psum(dact_outer, 'tp')  215 us
    reduce_scatter x1, waiting for transfers between devices, shards(): mixed = lax.psum_scatter(partial_out, 'tp', scatter_dimension=2, tiled=True)  71.3 us
    psum x1, waiting for transfers between devices, shards(): lax.psum((grad_first, grad_conv, grad_last, grad_gain_outer, second_gain_...  54.3 us
    reduce_scatter x1, waiting for transfers between devices, shards(): dact_mid = lax.psum_scatter(dwide, 'tp', scatter_dimension=2, tiled=True)  43.6 us
    all_gather x1, waiting for transfers between devices, shards(): wide_active = lax.all_gather(rim_active, 'tp', axis=2, tiled=True)  31.1 us
    psum x1, blocking collectives, shards(): lax.psum((jnp.sum(second_hidden, -1), jnp.sum(second_hidden * second_hidd...  30.3 us
    psum x1, blocking collectives, shards(): lax.psum((jnp.sum(third_hidden, -1), jnp.sum(third_hidden * third_hidden,...  28.4 us
    convert_element_type x1, other arithmetic, first_norm_fn(): exact_gelu_fn(pre_norm_input).astype(jnp.bfloat16)  27.5 us
  transfers between devices with their start and end apart: 12, of which 10 were waited for; matrix products, arithmetic and copies ran while one was open for 11% of the time, Pallas kernels for 0%

commit v1 on v0

v1 whole, which is shorter than its diff:
```python
import functools
from types import SimpleNamespace

import jax
import jax.numpy as jnp
from jax import lax
from jax.experimental import pallas as pl
from jax.experimental.pallas import tpu as pltpu
from jax.sharding import PartitionSpec as P

MESH = pl.DeviceIdType.MESH
F32 = jnp.float32
BF16 = jnp.bfloat16

TAPS = 5
STEP = 2
REACH = 4
EPS = 1e-05
LANES = 128
RIM = 16
PAD = 8
STAGES = 4
HALF_ROOT = 0.7071067811865476
PEAK = 0.3989422804014327

NT = (((1,), (1,)), ((), ()))
OFFSETS = [STEP * k - REACH for k in range(TAPS)]


class Sizes:
    def __init__(self, mesh, inputs, starts, first_proj, cotangent):
        self.S = mesh.shape["seq"]
        self.T = mesh.shape["tp"]
        self.Z = self.T // 2
        self.R, self.N, self.D = inputs.shape
        assert self.R == self.T and self.N % LANES == 0
        self.Hs = first_proj.shape[1]
        self.H = self.Hs * self.T
        self.Hp = -(-self.Hs // 16) * 16
        self.HP = self.Hp * self.T
        assert self.HP % LANES == 0 and self.D % LANES == 0
        self.E = self.N + 2 * RIM
        self.nd = self.D // LANES
        self.nh = self.HP // LANES
        self.units = 2 * self.nd + TAPS * self.nh
        self.NR = -(-self.units // self.S)
        self.Dt = cotangent.shape[2]
        self.wide = self.Dt // LANES * LANES
        self.rem = self.Dt - self.wide
        self.fold = LANES // self.rem if self.rem else 1
        cuts = [round(i * self.NR / STAGES) for i in range(STAGES + 1)]
        self.chunks = list(zip(cuts[:-1], cuts[1:]))
        self.square = self.S == 4


def cells(ref, row, count):
    return ref[pl.ds(row, count), :]


def gelu_parts(v):
    whole = 0.5 * (1.0 + lax.erf(v * HALF_ROOT))
    slope = whole + v * (PEAK * jnp.exp(-0.5 * v * v))
    return v * whole, slope


def fold_narrow(z, part):
    rows = z.N // z.fold
    return jnp.concatenate([part[i * rows : (i + 1) * rows] for i in range(z.fold)], axis=1)


def unfold_narrow(z, part):
    return jnp.concatenate([part[:, i * z.rem : (i + 1) * z.rem] for i in range(z.fold)], axis=0)


def kernel(z, names, *refs):
    r = SimpleNamespace(**dict(zip(names, refs, strict=True)))
    S, T, Z, N, D, E, H, Hp, HP, NR = z.S, z.T, z.Z, z.N, z.D, z.E, z.H, z.Hp, z.HP, z.NR
    s, t = lax.axis_index("seq"), lax.axis_index("tp")
    core, layer = lax.rem(t, 2), t // 2
    slot = core * Z + layer
    mine = core * Z
    theirs = (1 - core) * Z
    partner = (s, t + 1 - 2 * core)

    send, recv, local = r.send, r.recv, r.local
    counts = {"remote": 0, "local": 0}
    sent = []

    def remote(src, dst, device):
        i = counts["remote"]
        counts["remote"] += 1
        return pltpu.make_async_remote_copy(
            src_ref=src,
            dst_ref=dst,
            send_sem=send.at[i],
            recv_sem=recv.at[i],
            device_id=device,
            device_id_type=MESH,
        )

    def push(src, dst, device):
        copy = remote(src, dst, device)
        copy.start()
        sent.append(copy)
        return copy

    def move(src, dst):
        i = counts["local"]
        counts["local"] += 1
        copy = pltpu.make_async_copy(src, dst, local.at[i])
        copy.start()
        return copy

    def z_at(i):
        return lax.rem(layer + i + Z, Z)

    def dev_z(i):
        return (s, 2 * z_at(i) + core)

    def seq_at(i):
        return lax.rem(s + i + S, S)

    right, left = (seq_at(1), t), (seq_at(-1), t)
    if z.square:
        sx, sy, sd = s ^ 1, s ^ 2, s ^ 3
        x_side, y_side = (sx, t), (sy, t)

    barrier = pltpu.get_barrier_semaphore()
    for i in range(1, T):
        pl.semaphore_signal(barrier, inc=1, device_id=(s, lax.rem(t + i, T)), device_id_type=MESH)
    for i in range(1, S):
        pl.semaphore_signal(barrier, inc=1, device_id=(seq_at(i), t), device_id_type=MESH)
    pl.semaphore_wait(barrier, T + S - 2)

    pack, wg = r.pack, r.wg
    along = {}
    own_core = {}
    own_local = {}
    for k, (a, b) in enumerate(z.chunks):
        for i in range(1, Z):
            along[k, i] = push(
                pack.at[s, pl.ds(a, b - a)], wg.at[s, pl.ds(a, b - a), slot], dev_z(i)
            )
        own_local[k] = move(pack.at[:, pl.ds(a, b - a)], wg.at[:, pl.ds(a, b - a), slot])
        own_core[k] = push(pack.at[:, pl.ds(a, b - a)], wg.at[:, pl.ds(a, b - a), slot], partner)
        if k == 0:
            xe = r.xe
            row_in = move(r.x.at[t], xe.at[pl.ds(RIM, N)])
            rim_r = push(r.x.at[t, pl.ds(N - RIM, RIM)], xe.at[pl.ds(0, RIM)], right)
            rim_l = push(r.x.at[t, pl.ds(0, RIM)], xe.at[pl.ds(RIM + N, RIM)], left)
            flags_r = push(r.starts, r.flags_left, right)
            flags_l = push(r.starts, r.flags_right, left)
            gain_copies = [
                push(r.gl, r.gslots.at[slot], (s, lax.rem(t + i, T))) for i in range(1, T)
            ]
            gain_own = move(r.gl, r.gslots.at[slot])

    cot = r.cot
    cot_copies, cot_local = [], []
    if z.rem:
        for row in range(T):
            r.cot_fold[row] = fold_narrow(z, cot[row, :, z.wide : z.Dt])
    for i in range(1, T):
        to = lax.rem(t + i, T)
        if z.wide:
            cot_copies.append(
                push(cot.at[to, :, pl.ds(0, z.wide)], r.cot_wide.at[t], (s, to))
            )
        if z.rem:
            cot_copies.append(push(r.cot_fold.at[to], r.cot_narrow.at[t], (s, to)))
    if z.wide:
        cot_local.append(move(cot.at[t, :, pl.ds(0, z.wide)], r.cot_wide.at[t]))
    if z.rem:
        cot_local.append(move(r.cot_fold.at[t], r.cot_narrow.at[t]))

    plane_x, plane_y, plane_d, plane_any = {}, {}, {}, {}
    across = {}

    def weights_along(k):
        a, b = z.chunks[k]
        span = pl.ds(a, b - a)
        for i in range(1, Z):
            along[k, i].wait_recv()
            place = wg.at[s, span, mine + z_at(-i)]
            if z.square:
                plane_x[k, i] = push(place, place, x_side)
                plane_y[k, i] = push(place, place, y_side)
            else:
                for j in range(1, S):
                    plane_any[k, i, j] = push(place, place, (seq_at(j), t))

    def weights_corner(k):
        a, b = z.chunks[k]
        span = pl.ds(a, b - a)
        if not z.square:
            return
        for i in range(1, Z):
            plane_x[k, i].wait_recv()
            plane_y[k, i].wait_recv()
            if (k * (Z - 1) + i) % 2:
                place = wg.at[sx, span, mine + z_at(-i)]
                plane_d[k, i] = push(place, place, y_side)
            else:
                place = wg.at[sy, span, mine + z_at(-i)]
                plane_d[k, i] = push(place, place, x_side)

    def weights_across(k):
        a, b = z.chunks[k]
        span = pl.ds(a, b - a)
        for i in range(1, Z):
            if z.square:
                plane_d[k, i].wait_recv()
            else:
                for j in range(1, S):
                    plane_any[k, i, j].wait_recv()
            place = wg.at[:, span, mine + z_at(-i)]
            across[k, i] = push(place, place, partner)

    def weights_ready(k):
        own_local[k].wait()
        own_core[k].wait_recv()
        for i in range(1, Z):
            across[k, i].wait_recv()

    def unit(ref, u):
        return ref[u % S, u // S].reshape(HP, LANES)

    def weights(first, count):
        return jnp.concatenate([unit(wg, u) for u in range(first, first + count)], axis=1)

    def first_weight():
        return weights(0, z.nd)

    def tap_weight(k):
        return weights(z.nd + k * z.nh, z.nh)

    def last_weight():
        return weights(z.nd + TAPS * z.nh, z.nd)

    flags_r.wait_recv()
    flags_l.wait_recv()
    here = r.starts[pl.ds(t, 1), :]
    before = r.flags_left[pl.ds(t, 1), :]
    after = r.flags_right[pl.ds(t, 1), :]
    window = jnp.concatenate([before[:, N - LANES :], here, after[:, :LANES]], axis=1).astype(F32)
    window = jnp.broadcast_to(window, (E, N + 2 * LANES))
    at = lax.broadcasted_iota(jnp.int32, window.shape, 1) - LANES
    place = lax.broadcasted_iota(jnp.int32, window.shape, 0) - RIM
    rows = lax.broadcasted_iota(jnp.int32, (E, 1), 0) - RIM + s * N
    for k, offset in enumerate(OFFSETS):
        low, high = min(offset, 0), max(offset, 0)
        begun = jnp.sum(
            jnp.where((at > place + low) & (at <= place + high), window, 0.0), axis=1, keepdims=True
        )
        moved = rows + offset
        inside = (begun == 0.0) & (moved >= 0) & (moved < S * N)
        r.mask[:, k : k + 1] = inside.astype(F32)

    gain_own.wait()
    for copy in gain_copies:
        copy.wait_recv()
    for j in range(T):
        r.gains[0:2, j * Hp : (j + 1) * Hp] = r.gslots[j, 0:2, :Hp]

    row_in.wait()
    rim_r.wait_recv()
    rim_l.wait_recv()

    def first_norm(i, carry):
        row = pl.multiple_of(i * 16, 16)
        v = cells(xe, row, 16).astype(F32)
        mean = jnp.sum(v, axis=1, keepdims=True) / D
        spread = jnp.sum(v * v, axis=1, keepdims=True) / D - mean * mean
        scale = lax.rsqrt(spread + EPS)
        act, slope = gelu_parts((v - mean) * scale * r.g1[0:1, :])
        r.act0[pl.ds(row, 16), :] = act.astype(BF16)
        r.slope0[pl.ds(row, 16), :] = slope
        r.mean0[pl.ds(row, 16), :] = mean
        r.scale0[pl.ds(row, 16), :] = scale
        return carry

    lax.fori_loop(0, E // 16, first_norm, 0)

    weights_along(0)
    weights_along(1)
    weights_corner(0)
    weights_along(2)
    weights_corner(1)
    weights_across(0)

    weights_ready(0)
    r.hid[...] = lax.dot_general(
        r.act0[...], first_weight(), NT, preferred_element_type=F32
    )

    weights_along(3)
    weights_corner(2)
    weights_across(1)

    def inner_norm(which, act_store):
        gain = r.gains[which : which + 1, :]
        xhat_ref, slope_ref, scale_ref = (
            (r.xhat1, r.slope1, r.scale1),
            (r.xhat2, r.slope2, r.scale2),
        )[which]

        def body(i, carry):
            row = pl.multiple_of(i * 16, 16)
            v = cells(r.hid, row, 16)
            mean = jnp.sum(v, axis=1, keepdims=True) / H
            spread = jnp.sum(v * v, axis=1, keepdims=True) / H - mean * mean
            scale = lax.rsqrt(spread + EPS)
            xhat = (v - mean) * scale
            act, slope = gelu_parts(xhat * gain)
            act_store(row, act)
            xhat_ref[pl.ds(row, 16), :] = xhat
            slope_ref[pl.ds(row, 16), :] = slope
            scale_ref[pl.ds(row, 16), :] = scale
            return carry

        lax.fori_loop(0, E // 16, body, 0)

    act1, taps = r.act1, r.taps
    act1[0:PAD, :] = jnp.zeros((PAD, HP), F32)
    act1[PAD + E :, :] = jnp.zeros((PAD, HP), F32)

    def keep_act1(row, act):
        act1[pl.ds(pl.multiple_of(row + PAD, 8), 16), :] = act.astype(BF16).astype(F32)

    inner_norm(0, keep_act1)
    for k, offset in enumerate(OFFSETS):
        taps[:, k * HP : (k + 1) * HP] = (
            act1[PAD + offset : PAD + offset + E, :] * r.mask[:, k : k + 1]
        ).astype(BF16)

    weights_corner(3)
    weights_across(2)

    weights_ready(1)
    weights_ready(2)
    total = None
    for k in range(TAPS):
        term = lax.dot_general(
            taps[:, k * HP : (k + 1) * HP], tap_weight(k), NT, preferred_element_type=F32
        )
        total = term if total is None else total + term
    r.hid[...] = total

    act2 = r.act2

    def keep_act2(row, act):
        act2[pl.ds(row, 16), :] = act.astype(BF16)

    inner_norm(1, keep_act2)
    weights_across(3)

    for copy in cot_local:
        copy.wait()
    for copy in cot_copies:
        copy.wait_recv()
    cote = r.cote
    for j in range(T):
        base = j * z.Dt
        if z.wide:
            cote[RIM : RIM + N, base : base + z.wide] = r.cot_wide[j]
        if z.rem:
            cote[RIM : RIM + N, base + z.wide : base + z.Dt] = unfold_narrow(z, r.cot_narrow[j])
    edge_r = push(cote.at[pl.ds(N, RIM)], cote.at[pl.ds(0, RIM)], right)
    edge_l = push(cote.at[pl.ds(RIM, RIM)], cote.at[pl.ds(RIM + N, RIM)], left)

    weights_ready(3)
    big = r.big
    big[...] = jnp.dot(act2[RIM : RIM + N, :], last_weight(), preferred_element_type=F32)
    big[...] = big[...] + xe[RIM : RIM + N, :].astype(F32)
    out_copies, out_local = [], []
    for j in range(T):
        base = j * z.Dt
        if z.wide:
            r.out_wide[j] = big[:, base : base + z.wide].astype(BF16)
        if z.rem:
            r.out_fold[j] = fold_narrow(z, big[:, base + z.wide : base + z.Dt]).astype(BF16)
    for i in range(1, T):
        to = lax.rem(t + i, T)
        if z.wide:
            out_copies.append(push(r.out_wide.at[to], r.got_wide.at[t], (s, to)))
        if z.rem:
            out_copies.append(push(r.out_fold.at[to], r.got_fold.at[t], (s, to)))
    if z.wide:
        out_local.append(move(r.out_wide.at[t], r.got_wide.at[t]))
    if z.rem:
        out_local.append(move(r.out_fold.at[t], r.got_fold.at[t]))

    edge_r.wait_recv()
    edge_l.wait_recv()
    r.hid[...] = lax.dot_general(cote[...], last_weight(), NT, preferred_element_type=F32)
    r.acc1[...] = jnp.zeros_like(r.acc1)
    r.acc2[...] = jnp.zeros_like(r.acc2)
    r.acc0[...] = jnp.zeros_like(r.acc0)

    def inner_norm_back(which, first, count, grad_store, acc_ref, own):
        gain = r.gains[which : which + 1, :]
        xhat_ref, slope_ref, scale_ref = (
            (r.xhat1, r.slope1, r.scale1),
            (r.xhat2, r.slope2, r.scale2),
        )[which]

        def body(i, carry):
            row = pl.multiple_of(i * 16, 16)
            xhat = cells(xhat_ref, row, 16)
            dpre = cells(r.hid, row, 16) * cells(slope_ref, row, 16)
            if own:
                dgain = dpre * xhat
                acc_ref[...] += dgain[0:8] + dgain[8:16]
            dx = dpre * gain
            plain = jnp.sum(dx, axis=1, keepdims=True) / H
            cross = jnp.sum(dx * xhat, axis=1, keepdims=True) / H
            grad_store(row, cells(scale_ref, row, 16) * (dx - plain - xhat * cross))
            return carry

        lax.fori_loop(first, first + count, body, 0)

    dhid2 = r.dhid2
    dhid2[0:PAD, :] = jnp.zeros((PAD, HP), F32)
    dhid2[PAD + E :, :] = jnp.zeros((PAD, HP), F32)

    def keep_dhid2(row, grad):
        dhid2[pl.ds(pl.multiple_of(row + PAD, 8), 16), :] = grad.astype(BF16).astype(F32)

    n16 = N // 16
    inner_norm_back(1, 0, 1, keep_dhid2, r.acc2, False)
    inner_norm_back(1, 1, n16, keep_dhid2, r.acc2, True)
    inner_norm_back(1, 1 + n16, 1, keep_dhid2, r.acc2, False)

    back = r.back
    for j, offset in enumerate(OFFSETS):
        first = PAD + RIM + offset
        back[:, j * HP : (j + 1) * HP] = (
            dhid2[first : first + N, :] * r.mask[RIM : RIM + N, j : j + 1]
        ).astype(BF16)
    total = None
    for j in range(TAPS):
        term = jnp.dot(
            back[:, j * HP : (j + 1) * HP], tap_weight(TAPS - 1 - j), preferred_element_type=F32
        )
        total = term if total is None else total + term
    r.hid[RIM : RIM + N, :] = total

    dhid1 = r.dhid1

    def keep_dhid1(row, grad):
        dhid1[pl.ds(pl.multiple_of(row - RIM, 16), 16), :] = grad.astype(BF16)

    inner_norm_back(0, 1, n16, keep_dhid1, r.acc1, True)

    big[...] = jnp.dot(dhid1[...], first_weight(), preferred_element_type=F32)

    def first_norm_back(i, carry):
        row = pl.multiple_of(i * 16, 16)
        wide = pl.multiple_of(row + RIM, 16)
        scale = cells(r.scale0, wide, 16)
        xhat = (cells(xe, wide, 16).astype(F32) - cells(r.mean0, wide, 16)) * scale
        dpre = cells(big, row, 16) * cells(r.slope0, wide, 16)
        dgain = dpre * xhat
        r.acc0[...] += dgain[0:8] + dgain[8:16]
        dx = dpre * r.g1[0:1, :]
        plain = jnp.sum(dx, axis=1, keepdims=True) / D
        cross = jnp.sum(dx * xhat, axis=1, keepdims=True) / D
        grad = scale * (dx - plain - xhat * cross)
        r.gi_own[pl.ds(row, 16), :] = (cells(cote, wide, 16).astype(F32) + grad).astype(BF16)
        return carry

    lax.fori_loop(0, n16, first_norm_back, 0)

    gi, gi_own = r.gi, r.gi_own
    own_row = move(gi_own, gi.at[t])
    to_core = push(gi_own, gi.at[t], partner)
    parts = 2
    part = N // parts
    chain = {}
    for q in range(parts):
        for way in (1, -1):
            for h in range(Z):
                row = t - 2 * way * h
                span = pl.ds(q * part, part)
                src = gi_own.at[span] if h == 0 else gi.at[row, span]
                onward = remote(src, gi.at[row, span], (s, t + 2 * way)) if h < Z - 1 else None
                sideways = remote(src, gi.at[row, span], partner) if h else None
                chain[q, way, h] = (onward, sideways)

    def has(way, h):
        return layer - h >= 0 if way == 1 else layer + h < Z

    def goes(way):
        return layer + 1 < Z if way == 1 else layer >= 1

    def chain_start(q):
        for way in (1, -1):

            @pl.when(goes(way))
            def _():
                chain[q, way, 0][0].start()

    def chain_step(q, h):
        for way in (1, -1):

            @pl.when(has(way, h))
            def _():
                chain[q, way, h - 1][0].wait_recv()
                chain[q, way, h][1].start()

            if h < Z - 1:

                @pl.when(has(way, h) & goes(way))
                def _():
                    chain[q, way, h][0].start()

    def chain_end():
        for q in range(parts):
            for way in (1, -1):
                for h in range(Z):
                    if h == 0:

                        @pl.when(goes(way))
                        def _():
                            chain[q, way, 0][0].wait_send()

                    else:

                        @pl.when(has(way, h))
                        def _():
                            chain[q, way, h][1].wait()

                        if h < Z - 1:

                            @pl.when(has(way, h) & goes(way))
                            def _():
                                chain[q, way, h][0].wait_send()

    for q in range(parts):
        chain_start(q)

    vec = r.vec
    sum0 = jnp.sum(r.acc0[...], axis=0, keepdims=True)
    sum1 = jnp.sum(r.acc1[...], axis=0, keepdims=True)
    sum2 = jnp.sum(r.acc2[...], axis=0, keepdims=True)
    vec[...] = jnp.zeros_like(vec)
    for j in range(z.nd):
        vec[j : j + 1, :] = sum0[:, j * LANES : (j + 1) * LANES]
    for j in range(z.nh):
        vec[z.nd + j : z.nd + j + 1, :] = sum1[:, j * LANES : (j + 1) * LANES]
        vec[z.nd + z.nh + j : z.nd + z.nh + j + 1, :] = sum2[:, j * LANES : (j + 1) * LANES]
    vec_plane = [push(vec, r.vec_plane.at[i], (seq_at(i), t)) for i in range(1, S)]

    g = r.g

    def grad_units(first, lhs, rhs, count):
        for j in range(0, count, 2):
            width = min(2, count - j)
            block = jnp.dot(
                lhs, rhs(j * LANES, width * LANES), preferred_element_type=F32
            ).astype(BF16)
            for i in range(width):
                u = first + j + i
                g[u % S, u // S] = block[:, i * LANES : (i + 1) * LANES].reshape(T, Hp, LANES)

    rc = r.rc
    swaps, plane1, plane2, along_back, spread_out = {}, {}, {}, {}, {}

    def swap(k):
        a, b = z.chunks[k]
        span = pl.ds(a, b - a)
        swaps[k] = push(g.at[:, span, pl.ds(theirs, Z)], rc.at[:, span], partner)

    low, high = pl.ds(0, Z // 2), pl.ds(Z // 2, Z // 2)

    def to_plane(k):
        a, b = z.chunks[k]
        span = pl.ds(a, b - a)
        swaps[k].wait_recv()
        for q in range(S):
            for n in range(a, b):
                g[q, n, pl.ds(mine, Z)] = (
                    g[q, n, pl.ds(mine, Z)].astype(F32) + rc[q, n].astype(F32)
                ).astype(BF16)
        if z.square:
            near, far = pl.ds(mine, Z // 2), pl.ds(mine + Z // 2, Z // 2)
            plane1[k] = [
                push(g.at[sx, span, near], r.rx.at[0, span], x_side),
                push(g.at[sd, span, near], r.rx.at[1, span], x_side),
                push(g.at[sy, span, far], r.ry.at[0, span], y_side),
                push(g.at[sd, span, far], r.ry.at[1, span], y_side),
            ]
        else:
            plane1[k] = [
                push(g.at[seq_at(i), span, pl.ds(mine, Z)], r.rd.at[i, span], (seq_at(i), t))
                for i in range(1, S)
            ]

    def add_into(q, n, where, count, other):
        g[q, n, pl.ds(where, count)] = (
            g[q, n, pl.ds(where, count)].astype(F32) + other.astype(F32)
        ).astype(BF16)

    def turn_plane(k):
        a, b = z.chunks[k]
        span = pl.ds(a, b - a)
        for copy in plane1[k]:
            copy.wait_recv()
        if not z.square:
            return
        half = Z // 2
        near, far = mine, mine + half
        for n in range(a, b):
            add_into(sy, n, near, half, r.rx[1, n])
            add_into(sx, n, far, half, r.ry[1, n])
        plane2[k] = [
            push(g.at[sy, span, pl.ds(near, half)], r.ry2.at[span], y_side),
            push(g.at[sx, span, pl.ds(far, half)], r.rx2.at[span], x_side),
        ]
        for n in range(a, b):
            add_into(s, n, near, half, r.rx[0, n])
            add_into(s, n, far, half, r.ry[0, n])

    def to_z(k):
        a, b = z.chunks[k]
        span = pl.ds(a, b - a)
        half = Z // 2
        if z.square:
            for copy in plane2[k]:
                copy.wait_recv()
            for n in range(a, b):
                add_into(s, n, mine, half, r.ry2[n])
                add_into(s, n, mine + half, half, r.rx2[n])
        else:
            for n in range(a, b):
                sums = g[s, n, pl.ds(mine, Z)].astype(F32)
                for i in range(1, S):
                    sums = sums + r.rd[i, n].astype(F32)
                g[s, n, pl.ds(mine, Z)] = sums.astype(BF16)
        along_back[k] = [
            push(g.at[s, span, mine + z_at(i)], r.rz.at[i, span], dev_z(i))
            for i in range(1, Z)
        ]

    ff = r.ff

    def to_all(k):
        a, b = z.chunks[k]
        span = pl.ds(a, b - a)
        for copy in along_back[k]:
            copy.wait_recv()
        for n in range(a, b):
            sums = g[s, n, slot].astype(F32)
            for i in range(1, Z):
                sums = sums + r.rz[i, n].astype(F32)
            ff[s, n] = sums.astype(BF16)
        spread_out[k] = [
            push(ff.at[s, span], ff.at[s, span], (seq_at(i), t)) for i in range(1, S)
        ]

    def all_here(k):
        for copy in spread_out[k]:
            copy.wait_recv()

    for u in range(z.units, S * NR):
        g[u % S, u // S] = jnp.zeros((T, Hp, LANES), BF16)
    own = slice(RIM, RIM + N)
    act2_t = act2[own, :].astype(F32).T.astype(BF16)
    grad_units(z.nd + TAPS * z.nh, act2_t, lambda c, w: cote[own, c : c + w], z.nd)
    swap(3)
    dhid2_t = dhid2[PAD + RIM : PAD + RIM + N, :].T.astype(BF16)
    grad_units(z.nd, dhid2_t, lambda c, w: taps[own, c : c + w], TAPS * z.nh)
    swap(2)
    swap(1)
    to_plane(3)
    dhid1_t = dhid1[...].astype(F32).T.astype(BF16)
    grad_units(0, dhid1_t, lambda c, w: r.act0[own, c : c + w], z.nd)
    swap(0)
    to_plane(2)

    chain_step(0, 1)
    turn_plane(3)
    to_plane(1)
    chain_step(1, 1)

    for copy in vec_plane:
        copy.wait_recv()
    vec_sum = r.vec_sum
    vec_sum[...] = sum((r.vec_plane[i] for i in range(1, S)), vec[...])
    vec_z = [push(vec_sum, r.vec_z.at[i - 1], dev_z(i)) for i in range(1, Z)]

    turn_plane(2)
    to_z(3)
    to_plane(0)
    if Z > 2:
        chain_step(0, 2)
    turn_plane(1)
    to_z(2)
    to_all(3)
    if Z > 2:
        chain_step(1, 2)

    for copy in vec_z:
        copy.wait_recv()
    vec_pair = r.vec_pair
    vec_pair[0] = sum((r.vec_z[i - 1] for i in range(1, Z)), vec_sum[...])
    vec_core = push(vec_pair.at[0], vec_pair.at[1], partner)

    turn_plane(0)
    to_z(1)
    to_all(2)
    for h in range(3, Z):
        chain_step(0, h)
    to_z(0)
    to_all(1)
    all_here(3)
    for h in range(3, Z):
        chain_step(1, h)
    to_all(0)
    for k in range(3):
        all_here(k)

    vec_core.wait_recv()
    gain_sums = vec_pair[0] + vec_pair[1]

    def line(first, count):
        return jnp.concatenate([gain_sums[j : j + 1, :] for j in range(first, first + count)], axis=1)

    def picked(row, width, step, index, count):
        return sum(
            jnp.where(index == j, row[:, j * step : j * step + width], 0.0) for j in range(count)
        )

    r.grad_gain[...] = picked(line(0, z.nd), z.Dt, z.Dt, t, T)
    r.grad_gain1[...] = picked(line(z.nd, z.nh), z.Hs, Hp, slot, T)
    r.grad_gain2[...] = picked(line(z.nd + z.nh, z.nh), z.Hs, Hp, slot, T)

    def summed(first, count):
        return jnp.concatenate(
            [ff[u % S, u // S].astype(F32) for u in range(first, first + count)], axis=1
        )

    r.grad_first[...] = summed(0, z.nd).T[:, : z.Hs]
    r.grad_last[...] = summed(z.nd + TAPS * z.nh, z.nd)[: z.Hs]
    for k in range(TAPS):
        turned = summed(z.nd + k * z.nh, z.nh).T[:, : z.Hs]
        for j in range(T):
            to = 2 * (j % Z) + j // Z
            r.grad_conv[k, to * z.Hs : (to + 1) * z.Hs, :] = turned[j * Hp : j * Hp + z.Hs, :]

    for copy in out_local:
        copy.wait()
    for copy in out_copies:
        copy.wait_recv()
    for row in range(T):
        if z.wide:
            r.out[row, :, 0 : z.wide] = r.got_wide[row]
        if z.rem:
            r.out[row, :, z.wide : z.Dt] = unfold_narrow(z, r.got_fold[row])

    to_core.wait_recv()
    own_row.wait()
    chain_end()
    for copy in sent:
        copy.wait_send()


def packed_weights(z, first_proj, dilated_conv, last_proj):
    more = z.Hp - z.Hs

    def rows(cells_):
        return jnp.pad(cells_, ((0, more), (0, 0)))

    first = rows(first_proj.T)
    conv = dilated_conv.reshape(TAPS, z.Z, 2, z.Hs, z.Hs).transpose(0, 4, 2, 1, 3)
    conv = jnp.pad(conv, ((0, 0), (0, more), (0, 0), (0, 0), (0, more)))
    conv = conv.reshape(TAPS, z.Hp, z.nh, LANES).transpose(0, 2, 1, 3)
    units = jnp.concatenate(
        [
            first.reshape(z.Hp, z.nd, LANES).transpose(1, 0, 2),
            conv.reshape(TAPS * z.nh, z.Hp, LANES),
            rows(last_proj).reshape(z.Hp, z.nd, LANES).transpose(1, 0, 2),
            jnp.zeros((z.S * z.NR - z.units, z.Hp, LANES), BF16),
        ]
    )
    return units.reshape(z.NR, z.S, z.Hp, LANES).transpose(1, 0, 2, 3)


def shards(
    mesh,
    inputs,
    starts,
    first_proj,
    dilated_conv,
    last_proj,
    first_norm_gain,
    second_norm_gain,
    third_norm_gain,
    cotangent,
):
    z = Sizes(mesh, inputs, starts, first_proj, cotangent)
    S, T, Z, N, D, E, HP, Hp, NR = z.S, z.T, z.Z, z.N, z.D, z.E, z.HP, z.Hp, z.NR
    pack = packed_weights(z, first_proj, dilated_conv, last_proj)
    gains = jnp.pad(
        jnp.stack([second_norm_gain, third_norm_gain]), ((0, 6), (0, LANES - z.Hs))
    )
    vm, anywhere = pltpu.VMEM, pl.ANY
    ins = dict(
        x=(inputs, anywhere),
        starts=(starts, vm),
        pack=(pack, anywhere),
        gl=(gains, vm),
        g1=(first_norm_gain.reshape(1, D), vm),
        cot=(cotangent, vm),
    )
    outs = dict(
        out=((z.R, N, z.Dt), BF16, vm),
        gi=((z.R, N, D), BF16, anywhere),
        grad_first=((D, z.Hs), F32, vm),
        grad_conv=((TAPS, z.H, z.Hs), F32, vm),
        grad_last=((z.Hs, D), F32, vm),
        grad_gain=((1, z.Dt), F32, vm),
        grad_gain1=((1, z.Hs), F32, vm),
        grad_gain2=((1, z.Hs), F32, vm),
    )
    fold_rows, fold_cols = N // z.fold, max(z.rem * z.fold, 1)
    wide = max(z.wide, 1)
    scratch = dict(
        send=pltpu.SemaphoreType.DMA((400,)),
        recv=pltpu.SemaphoreType.DMA((400,)),
        local=pltpu.SemaphoreType.DMA((16,)),
        xe=vm((E, D), BF16),
        cote=vm((E, D), BF16),
        act0=vm((E, D), BF16),
        slope0=vm((E, D), F32),
        mean0=vm((E, 1), F32),
        scale0=vm((E, 1), F32),
        mask=vm((E, LANES), F32),
        flags_left=vm((z.R, N), jnp.int32),
        flags_right=vm((z.R, N), jnp.int32),
        gslots=vm((T, 8, LANES), F32),
        gains=vm((8, HP), F32),
        wg=vm((S, NR, T, Hp, LANES), BF16),
        hid=vm((E, HP), F32),
        xhat1=vm((E, HP), F32),
        slope1=vm((E, HP), F32),
        scale1=vm((E, 1), F32),
        xhat2=vm((E, HP), F32),
        slope2=vm((E, HP), F32),
        scale2=vm((E, 1), F32),
        act1=vm((E + 2 * PAD, HP), F32),
        dhid2=vm((E + 2 * PAD, HP), F32),
        taps=vm((E, TAPS * HP), BF16),
        back=vm((N, TAPS * HP), BF16),
        act2=vm((E, HP), BF16),
        dhid1=vm((N, HP), BF16),
        big=vm((N, D), F32),
        gi_own=vm((N, D), BF16),
        acc0=vm((8, D), F32),
        acc1=vm((8, HP), F32),
        acc2=vm((8, HP), F32),
        cot_fold=vm((T, fold_rows, fold_cols), BF16),
        cot_wide=vm((T, N, wide), BF16),
        cot_narrow=vm((T, fold_rows, fold_cols), BF16),
        out_wide=vm((T, N, wide), BF16),
        out_fold=vm((T, fold_rows, fold_cols), BF16),
        got_wide=vm((T, N, wide), BF16),
        got_fold=vm((T, fold_rows, fold_cols), BF16),
        g=vm((S, NR, T, Hp, LANES), BF16),
        rc=vm((S, NR, Z, Hp, LANES), BF16),
        rz=vm((Z, NR, Hp, LANES), BF16),
        ff=vm((S, NR, Hp, LANES), BF16),
        vec=vm((24, LANES), F32),
        vec_sum=vm((24, LANES), F32),
        vec_plane=vm((S, 24, LANES), F32),
        vec_z=vm((Z, 24, LANES), F32),
        vec_pair=vm((2, 24, LANES), F32),
    )
    if z.square:
        scratch.update(rx=vm((2, NR, Z // 2, Hp, LANES), BF16))
        scratch.update(ry=vm((2, NR, Z // 2, Hp, LANES), BF16))
        scratch.update(rx2=vm((NR, Z // 2, Hp, LANES), BF16))
        scratch.update(ry2=vm((NR, Z // 2, Hp, LANES), BF16))
    else:
        scratch.update(rd=vm((S, NR, Z, Hp, LANES), BF16))
    names = [*ins, *outs, *scratch]
    results = pl.pallas_call(
        functools.partial(kernel, z, names),
        out_shape=[jax.ShapeDtypeStruct(shape, kind) for shape, kind, _ in outs.values()],
        in_specs=[pl.BlockSpec(memory_space=space) for _, space in ins.values()],
        out_specs=[pl.BlockSpec(memory_space=space) for *_, space in outs.values()],
        scratch_shapes=list(scratch.values()),
        compiler_params=pltpu.CompilerParams(
            collective_id=0, has_side_effects=True, vmem_limit_bytes=63 * 2**20
        ),
    )(*[array for array, _ in ins.values()])
    out, gi, grad_first, grad_conv, grad_last, grad_gain, grad_gain1, grad_gain2 = results
    return (
        out,
        gi,
        grad_first,
        grad_conv,
        grad_last,
        grad_gain.reshape(-1),
        grad_gain1.reshape(-1),
        grad_gain2.reshape(-1),
    )


def solution(mesh):
    placed = (
        P(None, "seq", None),
        P(None, "seq"),
        P(None, "tp"),
        P(None, None, "tp"),
        P("tp", None),
        P(),
        P("tp"),
        P("tp"),
        P(None, "seq", "tp"),
    )
    return jax.shard_map(
        functools.partial(shards, mesh),
        mesh=mesh,
        in_specs=placed,
        out_specs=(
            P(None, "seq", "tp"),
            P(None, "seq", None),
            P(None, "tp"),
            P(None, None, "tp"),
            P("tp", None),
            P("tp"),
            P("tp"),
            P("tp"),
        ),
        check_vma=False,
    )
```

time: 743 us -> 175 us (0.24)
  waiting for transfers between devices: 438 us -> 0 us
  Pallas kernels: 0 us -> 147 us
  blocking collectives: 110 us -> 0 us
  other arithmetic: 80.8 us -> 1.52 us
  matrix products: 45.9 us -> 0 us
  starting transfers between devices: 16.8 us -> 0 us
  between operations: 15 us -> 0.72 us
    psum x2 -> x0, waiting for transfers between devices: 269 us -> none  [the longest x1 215 us: shards(): dact_full = lax.psum(dact_outer, 'tp')]
    pallas_call x0 -> x1, Pallas kernels: none -> 147 us  [shards(): pl.pallas_call(functools.partial(kernel, z, names), out_shape=[jax.ShapeD...]
    reduce_scatter x2 -> x0, waiting for transfers between devices: 115 us -> none  [the longest x1 71.3 us: shards(): mixed = lax.psum_scatter(partial_out, 'tp', scatter_dimension=2, tiled=True)]
    psum x5 -> x0, blocking collectives: 110 us -> none  [the longest x1 30.3 us: shards(): lax.psum((jnp.sum(second_hidden, -1), jnp.sum(second_hidden * second_hidd...]
    convert_element_type x10 -> x0, other arithmetic: 47.7 us -> none  [the longest x1 27.5 us: first_norm_fn(): exact_gelu_fn(pre_norm_input).astype(jnp.bfloat16)]
    dot_general x9 -> x0, matrix products: 45.9 us -> none  [the longest x1 8.76 us: shards(): jnp.einsum('bpc,bph->ch', taps, dhidden_last, preferred_element_type=jnp....]
    all_gather x2 -> x0, waiting for transfers between devices: 42 us -> none  [the longest x1 31.1 us: shards(): wide_active = lax.all_gather(rim_active, 'tp', axis=2, tiled=True)]
    reduce_sum x3 -> x0, other arithmetic: 19.5 us -> none  [the longest x1 13.8 us: shards(): jnp.sum(first_pre_gradient * first_normed, axis=(0, 1))]
  transfers between devices with their start and end apart: 12 -> 0, of which waited for: 10 -> 0; matrix products, arithmetic and copies ran while one was open for 11% -> 0% of each run, Pallas kernels for 0% -> 0%
where the time goes in v1:
time: 175 us
  Pallas kernels  147 us (84%)
  local copies, waits for them, and re-layouts  25.5 us (15%)
    pallas_call x1, Pallas kernels, shards(): pl.pallas_call(functools.partial(kernel, z, names), out_shape=[jax.ShapeD...  147 us
    unnamed x21, local copies, waits for them, and re-layouts  16 us
    reshape x2, local copies, waits for them, and re-layouts, packed_weights(): dilated_conv.reshape(TAPS, z.Z, 2, z.Hs, z.Hs).transpose(0, 4, 2, 1, 3)  5.58 us

profile of v1, /device:TPU:0, one launch (start us, length us, event | category | flops | bytes accessed | tf_op | source)
XLA Modules:
  0.0 174.7 jit_solution(10375289248198204545)
XLA Ops:
  0.6 0.0 copy-start
  0.6 0.0 copy-start.1
  0.7 0.1 pad.10.clone
  0.7 1.4 select_maximum_fusion.refs_3_
  2.1 1.3 reshape.52.refs_4_
  3.4 0.0 copy-done
  3.4 1.1 reshape.46
  4.5 0.1 copy.26
  4.6 4.3 %reshape.47 = bf16[5,4,2,80,80]{3,2,1,4,0:T(2,128)(2,1)S(1)} reshape(bf16[5,640,80]{1,2,0:T(8,128)(2,1)} %param.12) | data formatting | bytes 1024000 | tf_op jit(solution)/shard_map/reshape | solution.py:775
  8.9 1.3 copy.23
  10.2 0.4 copy.24
  10.5 0.2 maximum_maximum_fusion
  10.7 1.0 copy.35
  11.7 0.0 copy-done.1
  11.7 1.3 copy.28.refs_5_
  13.0 147.0 %shard_map.152 = (bf16[8,256,160]{2,1,0:T(8,128)(2,1)}, bf16[8,256,1280]{2,1,0:T(8,128)(2,1)}, f32[1280,80]{1,0:T(8,128)}, f32[5,640,80]{2,1,0:T(8,128)}, f32[80...) custom-call(bf16[8,256,1280]{2,1,0:T(8,128)(2,1)} %refs_0_.1, s32[8,256]{1,0:T(8,128)} %refs_1_.1, ...), custom_call_target="tpu_custom_call" | custom-call | tf_op jit(solution)/shard_map/pallas_call | solution.py:887
  160.0 2.2 %copy.29 = bf16[8,256,160]{1,2,0:T(8,128)(2,1)} copy(bf16[8,256,160]{2,1,0:T(8,128)(2,1)} %get-tuple-element.32) | data formatting | bytes 1310720
  162.2 2.1 %copy.30 = f32[1280,80]{0,1:T(8,128)} copy(f32[1280,80]{1,0:T(8,128)} %get-tuple-element.34) | data formatting | bytes 819200
  164.2 2.9 %copy.31 = f32[5,640,80]{1,2,0:T(8,128)} copy(f32[5,640,80]{2,1,0:T(8,128)} %get-tuple-element.35) | data formatting | bytes 2048000
  167.1 0.0 copy-start.2
  167.1 0.0 copy-start.3
  167.1 0.0 copy-start.5
  167.1 0.0 copy-start.4
  167.1 5.2 %copy.41 = bf16[8,256,1280]{2,1,0:T(8,128)(2,1)} copy(bf16[8,256,1280]{2,1,0:T(8,128)(2,1)} %get-tuple-element.49) | data formatting | bytes 10485760
  172.4 0.0 copy-done.2
  172.4 0.8 copy.42
  173.1 0.0 copy-done.3
  173.1 0.6 copy.43
  173.7 0.0 copy-done.5
  173.7 0.5 copy.44
  174.2 0.0 copy-done.4
  174.2 0.5 copy.45
  (2 shorter events, 0.0 us)
Async XLA Ops:
  0.6 2.8 %copy-start = (bf16[80,1280]{1,0:T(8,128)(2,1)S(1)}, bf16[80,1280]{1,0:T(8,128)(2,1)}, u32[]{:S(2)}) copy-start(bf16[80,1280]{1,0:T(8,128)(2,1)} %param.13) | copy-start | bytes 614404
  0.6 11.1 %copy-start.1 = (bf16[8,256,160]{1,2,0:T(8,128)(2,1)S(1)}, bf16[8,256,160]{1,2,0:T(8,128)(2,1)}, u32[]{:S(2)}) copy-start(bf16[8,256,160]{1,2,0:T(8,128)(2,1)} %param.17) | copy-start | bytes 1966084
  167.1 5.3 %copy-start.2 = (f32[80,1280]{1,0:T(8,128)S(1)}, f32[80,1280]{1,0:T(8,128)}, u32[]{:S(2)}) copy-start(f32[80,1280]{1,0:T(8,128)} %get-tuple-element.52) | copy-start | bytes 1228804
  167.1 6.0 %copy-start.3 = (f32[1,160]{1,0:T(1,128)S(1)}, f32[1,160]{1,0:T(1,128)}, u32[]{:S(2)}) copy-start(f32[1,160]{1,0:T(1,128)} %get-tuple-element.21) | copy-start | bytes 1924
  167.1 6.6 %copy-start.5 = (f32[1,80]{1,0:T(1,128)S(1)}, f32[1,80]{1,0:T(1,128)}, u32[]{:S(2)}) copy-start(f32[1,80]{1,0:T(1,128)} %get-tuple-element.22) | copy-start | bytes 964
  167.1 7.1 %copy-start.4 = (f32[1,80]{1,0:T(1,128)S(1)}, f32[1,80]{1,0:T(1,128)}, u32[]{:S(2)}) copy-start(f32[1,80]{1,0:T(1,128)} %get-tuple-element.23) | copy-start | bytes 964

commit v2 on v1

v2 whole, which is shorter than its diff:
```python
import functools
from types import SimpleNamespace

import jax
import jax.numpy as jnp
from jax import lax
from jax.experimental import pallas as pl
from jax.experimental.pallas import tpu as pltpu
from jax.sharding import PartitionSpec as P

MESH = pl.DeviceIdType.MESH
F32 = jnp.float32
BF16 = jnp.bfloat16

TAPS = 5
STEP = 2
REACH = 4
EPS = 1e-05
LANES = 128
RIM = 16
PAD = 8
STAGES = 4
BLOCK = 32
HALF_ROOT = 0.7071067811865476
PEAK = 0.3989422804014327

NT = (((1,), (1,)), ((), ()))
OFFSETS = [STEP * k - REACH for k in range(TAPS)]


class Sizes:
    def __init__(self, mesh, inputs, starts, first_proj, cotangent):
        self.S = mesh.shape["seq"]
        self.T = mesh.shape["tp"]
        self.Z = self.T // 2
        self.R, self.N, self.D = inputs.shape
        assert self.R == self.T and self.N % LANES == 0
        self.Hs = first_proj.shape[1]
        self.H = self.Hs * self.T
        self.Hp = -(-self.Hs // 16) * 16
        self.HP = self.Hp * self.T
        assert self.HP % LANES == 0 and self.D % LANES == 0
        self.E = self.N + 2 * RIM
        self.nd = self.D // LANES
        self.nh = self.HP // LANES
        self.units = 2 * self.nd + TAPS * self.nh
        self.NR = -(-self.units // self.S)
        self.Dt = cotangent.shape[2]
        assert self.Dt % 16 == 0
        cuts = [round(i * self.NR / STAGES) for i in range(STAGES + 1)]
        self.chunks = list(zip(cuts[:-1], cuts[1:]))
        self.square = self.S == 4
        self.line = self.Z == 4


def cells(ref, row, count):
    return ref[pl.ds(row, count), :]


def gelu_parts(v):
    whole = 0.5 * (1.0 + lax.erf(v * HALF_ROOT))
    slope = whole + v * (PEAK * jnp.exp(-0.5 * v * v))
    return v * whole, slope


def kernel(z, names, *refs):
    r = SimpleNamespace(**dict(zip(names, refs, strict=True)))
    S, T, Z, N, D, E, H, Hp, HP, NR = z.S, z.T, z.Z, z.N, z.D, z.E, z.H, z.Hp, z.HP, z.NR
    s, t = lax.axis_index("seq"), lax.axis_index("tp")
    core, layer = lax.rem(t, 2), t // 2
    partner = (s, t + 1 - 2 * core)

    send, recv, local = r.send, r.recv, r.local
    counts = [0, 0, 0]
    sent, sent_if = [], []

    def remote(src, dst, device, arrival=None):
        counts[0] += 1
        return pltpu.make_async_remote_copy(
            src_ref=src,
            dst_ref=dst,
            send_sem=send.at[counts[0] - 1],
            recv_sem=recv.at[arrivals(1) if arrival is None else arrival],
            device_id=device,
            device_id_type=MESH,
        )

    def arrivals(count):
        counts[1] += count
        return counts[1] - count

    def arrived(arrival, place):
        pltpu.make_async_remote_copy(
            src_ref=place,
            dst_ref=place,
            send_sem=send.at[0],
            recv_sem=recv.at[arrival],
            device_id=partner,
            device_id_type=MESH,
        ).wait_recv()

    def push(src, dst, device, arrival=None):
        copy = remote(src, dst, device, arrival)
        copy.start()
        sent.append(copy)
        return copy

    def push_if(when, copy):
        @pl.when(when)
        def _():
            copy.start()

        sent_if.append((when, copy))

    def move(src, dst):
        counts[2] += 1
        copy = pltpu.make_async_copy(src, dst, local.at[counts[2] - 1])
        copy.start()
        return copy

    def z_at(i):
        return lax.rem(layer + i + Z, Z)

    def dev_z(i):
        return (s, 2 * z_at(i) + core)

    def seq_at(i):
        return lax.rem(s + i + S, S)

    steps = range(1, Z)
    if z.line:
        upper = layer // 2
        inner = lax.rem((layer + 1) // 2, 2)
        end, middle = 3 * upper, 1 + upper
        first = inner * (3 - layer) + (1 - inner) * middle
        second = inner * end + (1 - inner) * (3 - middle)
        origins = [None, first, second, 3 - end]
        own_to = [(first, 2 - inner), (second, 3 - 2 * inner)]
        passed = {1: (end, 2), 3: (end, 3)}
        passed_all = {**passed, 2: (3 - layer, 3)}
    else:
        origins = [None] + [z_at(-i) for i in steps]
        own_to = [(z_at(i), i) for i in steps]
        passed, passed_all, inner = {}, {}, 0

    def at_layer(to):
        return (s, 2 * to + core)

    def take(base, j, place, onward, at_end, passing):
        if base + j not in onwards:
            extra = None
            if j in passing:
                to, then = passing[j]
                extra = remote(place, place, at_layer(to), base + then)
                sent_if.append((inner == 1, extra))
            onwards[base + j] = (extra, onward(j, place))
            sent.extend(onwards[base + j][1])

        def go():
            extra, copies = onwards[base + j]
            arrived(base + j, place)
            if extra is not None and not at_end:
                extra.start()
            for copy in copies:
                copy.start()

        if z.line:
            pl.when(inner == 1 - at_end)(go)
        elif at_end:
            go()

    onwards = {}
    right, left = (seq_at(1), t), (seq_at(-1), t)
    if z.square:
        sx, sy, sd = s ^ 1, s ^ 2, s ^ 3
        x_side, y_side = (sx, t), (sy, t)

    xe, cot, cot_t = r.xe, r.cot, r.cot_t

    def features(who):
        return pl.ds(pl.multiple_of(who * z.Dt, 16), z.Dt)

    weights_in = [move(r.w1, r.w1_in), move(r.wc, r.wc_in), move(r.w3, r.w3_in)]
    row_in = move(r.x.at[t], xe.at[pl.ds(RIM, N)])
    cot_own = move(cot.at[t], cot_t.at[features(t)])

    barrier = pltpu.get_barrier_semaphore()
    for i in range(1, T):
        pl.semaphore_signal(barrier, inc=1, device_id=(s, lax.rem(t + i, T)), device_id_type=MESH)
    for i in range(1, S):
        pl.semaphore_signal(barrier, inc=1, device_id=(seq_at(i), t), device_id_type=MESH)
    pl.semaphore_wait(barrier, T + S - 2)

    rim_r = push(r.x.at[t, pl.ds(N - RIM, RIM)], xe.at[pl.ds(0, RIM)], right)
    rim_l = push(r.x.at[t, pl.ds(0, RIM)], xe.at[pl.ds(RIM + N, RIM)], left)
    flags_r = push(r.starts, r.flags_left, right)
    flags_l = push(r.starts, r.flags_right, left)
    r.gl[0:1, : z.Hs] = r.g2[...]
    r.gl[1:2, : z.Hs] = r.g3[...]
    gain_copies = [push(r.gl, r.gslots.at[t], (s, lax.rem(t + i, T))) for i in range(1, T)]
    gain_own = move(r.gl, r.gslots.at[t])

    wg = r.wg
    bases, own_core = {}, {}
    plane_x, plane_y, plane_d, plane_any, across = {}, {}, {}, {}, {}

    def unit_in(u):
        if u < z.nd:
            return r.w1_in[:, u * LANES : (u + 1) * LANES]
        u -= z.nd
        if u < TAPS * z.nh:
            return r.wc_in[u // z.nh, :, u % z.nh * LANES : (u % z.nh + 1) * LANES]
        u -= TAPS * z.nh
        if u < z.nd:
            return r.w3_in[:, u * LANES : (u + 1) * LANES]
        return jnp.zeros((Hp, LANES), BF16)

    def rounds(k):
        a, b = z.chunks[k]
        return pl.ds(a, b - a)

    def weights_own(k):
        for q in range(S):
            for n in range(*z.chunks[k]):
                wg[q, n, layer, core] = unit_in(n * S + q)
        place = wg.at[s, rounds(k), layer, core]
        bases[k] = arrivals(Z)
        for to, j in own_to:
            push(place, place, at_layer(to), bases[k] + j)
        place = wg.at[:, rounds(k), layer, core]
        own_core[k] = push(place, place, partner)

    def weights_along(k, at_end, js=steps):
        def onward(j, place):
            if not z.square:
                plane_any[k, j] = [remote(place, place, (seq_at(i), t)) for i in range(1, S)]
                return plane_any[k, j]
            plane_x[k, j] = remote(place, place, x_side)
            plane_y[k, j] = remote(place, place, y_side)
            return [plane_x[k, j], plane_y[k, j]]

        for j in js:
            take(bases[k], j, wg.at[s, rounds(k), origins[j], core], onward, at_end, passed)

    def weights_corner(k):
        if not z.square:
            return
        for j in steps:
            across[k, j] = []
            over_y = (k + j) % 2
            place = wg.at[sx if over_y else sy, rounds(k), origins[j], core]
            plane_x[k, j].wait_recv()
            plane_y[k, j].wait_recv()
            plane_d[k, j] = push(place, place, y_side if over_y else x_side)
            for q in (s, sx, sy):
                place = wg.at[q, rounds(k), origins[j], core]
                across[k, j].append(push(place, place, partner))

    def weights_across(k):
        for j in steps:
            if z.square:
                plane_d[k, j].wait_recv()
                place = wg.at[sd, rounds(k), origins[j], core]
                across[k, j].append(push(place, place, partner))
            else:
                for copy in plane_any[k, j]:
                    copy.wait_recv()
                place = wg.at[:, rounds(k), origins[j], core]
                across[k, j] = [push(place, place, partner)]

    def weights_ready(k):
        own_core[k].wait_recv()
        for j in steps:
            for copy in across[k, j]:
                copy.wait_recv()

    cot_copies = []

    def cotangent_out():
        for i in range(1, T):
            to = lax.rem(t + i, T)
            cot_copies.append(push(cot.at[to], cot_t.at[features(t)], (s, to)))

    weights_in[0].wait()
    weights_in[1].wait()
    weights_own(0)
    weights_own(1)
    weights_in[2].wait()
    weights_own(2)
    weights_own(3)
    for k in range(STAGES):
        weights_along(k, False)
        weights_along(k, True, [1])

    def unit(ref, u):
        return ref[u % S, u // S].reshape(HP, LANES)

    def weights(first, count):
        return jnp.concatenate([unit(wg, u) for u in range(first, first + count)], axis=1)

    def first_weight():
        return weights(0, z.nd)

    def tap_weight(k):
        return weights(z.nd + k * z.nh, z.nh)

    def last_weight():
        return weights(z.nd + TAPS * z.nh, z.nd)

    row_in.wait()
    rim_r.wait_recv()
    rim_l.wait_recv()

    gain0 = jnp.concatenate([r.g1[j : j + 1, :] for j in range(z.nd)], axis=1)

    def first_norm(i, carry):
        row = pl.multiple_of(i * BLOCK, BLOCK)
        v = cells(xe, row, BLOCK).astype(F32)
        mean = jnp.sum(v, axis=1, keepdims=True) / D
        spread = jnp.sum(v * v, axis=1, keepdims=True) / D - mean * mean
        scale = lax.rsqrt(spread + EPS)
        act, slope = gelu_parts((v - mean) * scale * gain0)
        r.act0[pl.ds(row, BLOCK), :] = act.astype(BF16)
        r.slope0[pl.ds(row, BLOCK), :] = slope
        r.mean0[pl.ds(row, BLOCK), :] = mean
        r.scale0[pl.ds(row, BLOCK), :] = scale
        return carry

    lax.fori_loop(0, E // BLOCK, first_norm, 0)

    gain_own.wait()
    for copy in gain_copies:
        copy.wait_recv()
    for j in range(T):
        r.gains[0:2, j * Hp : (j + 1) * Hp] = r.gslots[j, 0:2, :Hp]

    flags_r.wait_recv()
    flags_l.wait_recv()
    here = r.starts[pl.ds(t, 1), :]
    before = r.flags_left[pl.ds(t, 1), :]
    after = r.flags_right[pl.ds(t, 1), :]
    window = jnp.concatenate([before[:, N - LANES :], here, after[:, :LANES]], axis=1).astype(F32)
    window = jnp.broadcast_to(window, (E, N + 2 * LANES))
    at = lax.broadcasted_iota(jnp.int32, window.shape, 1) - LANES
    place = lax.broadcasted_iota(jnp.int32, window.shape, 0) - RIM
    rows = lax.broadcasted_iota(jnp.int32, (E, 1), 0) - RIM + s * N
    for k, offset in enumerate(OFFSETS):
        low, high = min(offset, 0), max(offset, 0)
        begun = jnp.sum(
            jnp.where((at > place + low) & (at <= place + high), window, 0.0), axis=1, keepdims=True
        )
        moved = rows + offset
        inside = (begun == 0.0) & (moved >= 0) & (moved < S * N)
        r.mask[:, k : k + 1] = inside.astype(F32)

    weights_along(0, True, steps[1:])
    weights_along(1, True, steps[1:])
    weights_corner(0)
    weights_along(2, True, steps[1:])
    weights_corner(1)
    cotangent_out()
    weights_along(3, True, steps[1:])
    weights_corner(2)
    weights_across(0)
    weights_corner(3)

    weights_ready(0)
    r.hid[...] = lax.dot_general(r.act0[...], first_weight(), NT, preferred_element_type=F32)
    weights_across(1)

    def inner_norm(which, act_store):
        gain = r.gains[which : which + 1, :]
        xhat_ref, slope_ref, scale_ref = (
            (r.xhat1, r.slope1, r.scale1),
            (r.xhat2, r.slope2, r.scale2),
        )[which]

        def body(i, carry):
            row = pl.multiple_of(i * BLOCK, BLOCK)
            v = cells(r.hid, row, BLOCK)
            mean = jnp.sum(v, axis=1, keepdims=True) / H
            spread = jnp.sum(v * v, axis=1, keepdims=True) / H - mean * mean
            scale = lax.rsqrt(spread + EPS)
            xhat = (v - mean) * scale
            act, slope = gelu_parts(xhat * gain)
            act_store(row, act)
            xhat_ref[pl.ds(row, BLOCK), :] = xhat
            slope_ref[pl.ds(row, BLOCK), :] = slope
            scale_ref[pl.ds(row, BLOCK), :] = scale
            return carry

        lax.fori_loop(0, E // BLOCK, body, 0)

    act1, taps = r.act1, r.taps
    act1[0:PAD, :] = jnp.zeros((PAD, HP), F32)
    act1[PAD + E :, :] = jnp.zeros((PAD, HP), F32)

    def keep_act1(row, act):
        act1[pl.ds(pl.multiple_of(row + PAD, 8), BLOCK), :] = act.astype(BF16).astype(F32)

    inner_norm(0, keep_act1)
    for k, offset in enumerate(OFFSETS):
        taps[:, k * HP : (k + 1) * HP] = (
            act1[PAD + offset : PAD + offset + E, :] * r.mask[:, k : k + 1]
        ).astype(BF16)

    weights_across(2)

    weights_ready(1)
    weights_ready(2)
    total = None
    for k in range(TAPS):
        if k == TAPS - 2:
            weights_across(3)
        term = lax.dot_general(
            taps[:, k * HP : (k + 1) * HP], tap_weight(k), NT, preferred_element_type=F32
        )
        total = term if total is None else total + term
    r.hid[...] = total

    cot_own.wait()
    for copy in cot_copies:
        copy.wait_recv()
    cote = r.cote
    cote[RIM : RIM + N, :] = cot_t[...].T
    edge_r = push(cote.at[pl.ds(N, RIM)], cote.at[pl.ds(0, RIM)], right)
    edge_l = push(cote.at[pl.ds(RIM, RIM)], cote.at[pl.ds(RIM + N, RIM)], left)

    act2 = r.act2

    def keep_act2(row, act):
        act2[pl.ds(row, BLOCK), :] = act.astype(BF16)

    inner_norm(1, keep_act2)

    weights_ready(3)
    big = r.big
    big[...] = jnp.dot(act2[RIM : RIM + N, :], last_weight(), preferred_element_type=F32)
    out_t = r.out_t
    out_t[...] = (big[...] + xe[RIM : RIM + N, :].astype(F32)).astype(BF16).T
    out_copies = []
    for i in range(1, T):
        to = lax.rem(t + i, T)
        out_copies.append(push(out_t.at[features(to)], r.out.at[t], (s, to)))
    out_own = move(out_t.at[features(t)], r.out.at[t])

    g = r.g

    def grad_units(first, lhs, rhs, count):
        for j in range(0, count, 2):
            width = min(2, count - j)
            block = jnp.dot(
                lhs, rhs(j * LANES, width * LANES), preferred_element_type=F32
            ).astype(BF16)
            for i in range(width):
                u = first + j + i
                g[u % S, u // S] = block[:, i * LANES : (i + 1) * LANES].reshape(Z, 2, Hp, LANES)

    rc = r.rc
    swaps, plane1, plane2, along_back, spread_out = {}, {}, {}, {}, {}
    beside, over, own_sums = {}, {}, []

    def swap(k):
        a, b = z.chunks[k]
        span = pl.ds(a, b - a)
        swaps[k] = push(g.at[:, span, :, 1 - core], rc.at[:, span], partner)

    near, far = pl.ds(0, Z // 2), pl.ds(Z // 2, Z // 2)

    def to_plane(k):
        a, b = z.chunks[k]
        span = pl.ds(a, b - a)
        swaps[k].wait_recv()
        for q in range(S):
            for n in range(a, b):
                g[q, n, :, core] = (g[q, n, :, core].astype(F32) + rc[q, n].astype(F32)).astype(BF16)
        if z.square:
            plane1[k] = [
                push(g.at[sx, span, near, core], r.rx.at[0, span], x_side),
                push(g.at[sd, span, near, core], r.rx.at[1, span], x_side),
                push(g.at[sy, span, far, core], r.ry.at[0, span], y_side),
                push(g.at[sd, span, far, core], r.ry.at[1, span], y_side),
            ]
        else:
            plane1[k] = [
                push(g.at[seq_at(i), span, :, core], r.rd.at[i, span], (seq_at(i), t))
                for i in range(1, S)
            ]

    def add_into(q, n, where, other):
        g[q, n, where, core] = (g[q, n, where, core].astype(F32) + other.astype(F32)).astype(BF16)

    def turn_plane(k):
        a, b = z.chunks[k]
        span = pl.ds(a, b - a)
        for copy in plane1[k]:
            copy.wait_recv()
        if not z.square:
            return
        for n in range(a, b):
            add_into(sy, n, near, r.rx[1, n])
            add_into(sx, n, far, r.ry[1, n])
        plane2[k] = [
            push(g.at[sy, span, near, core], r.ry2.at[span], y_side),
            push(g.at[sx, span, far, core], r.rx2.at[span], x_side),
        ]
        for n in range(a, b):
            add_into(s, n, near, r.rx[0, n])
            add_into(s, n, far, r.ry[0, n])

    def to_z(k):
        a, b = z.chunks[k]
        span = pl.ds(a, b - a)
        if z.square:
            for copy in plane2[k]:
                copy.wait_recv()
            for n in range(a, b):
                add_into(s, n, near, r.ry2[n])
                add_into(s, n, far, r.rx2[n])
        else:
            for n in range(a, b):
                sums = g[s, n, :, core].astype(F32)
                for i in range(1, S):
                    sums = sums + r.rd[i, n].astype(F32)
                g[s, n, :, core] = sums.astype(BF16)

    def z_start(k):
        if z.line:
            beside[k] = arrivals(1)
            copy = remote(
                g.at[s, rounds(k), pl.ds(1 - upper, 3), core],
                r.rz_end.at[rounds(k)],
                at_layer(middle),
                beside[k],
            )
            push_if(inner == 0, copy)
        else:
            along_back[k] = [
                push(g.at[s, rounds(k), z_at(i), core], r.rz.at[i, rounds(k)], dev_z(i))
                for i in steps
            ]

    def z_over(k):
        if z.line:
            over[k] = arrivals(1)
            pair = pl.ds(2 - 2 * upper, 2)
            copy = remote(
                g.at[s, rounds(k), pair, core], r.rz_pair.at[rounds(k)], at_layer(3 - layer), over[k]
            )
            sent_if.append((inner == 1, copy))

            @pl.when(inner == 1)
            def _():
                arrived(beside[k], r.rz_end.at[rounds(k)])
                for n in range(*z.chunks[k]):
                    add_into(s, n, pair, r.rz_end[n, pl.ds(1 - upper, 2)])
                copy.start()

    def z_middle(k):
        if z.line:
            along_back[k] = remote(
                g.at[s, rounds(k), end, core], r.rz_one.at[rounds(k)], at_layer(end)
            )
            sent_if.append((inner == 1, along_back[k]))

            @pl.when(inner == 1)
            def _():
                arrived(over[k], r.rz_pair.at[rounds(k)])
                for n in range(*z.chunks[k]):
                    add_into(s, n, pl.ds(2 * upper, 2), r.rz_pair[n])
                along_back[k].start()
                for n in range(*z.chunks[k]):
                    sums = g[s, n, layer, core].astype(F32) + r.rz_end[n, 2 * upper].astype(F32)
                    r.ff_own[n] = sums.astype(BF16)

    def to_all(k):
        a, b = z.chunks[k]
        span = pl.ds(a, b - a)
        if z.line:

            @pl.when(inner == 0)
            def _():
                along_back[k].wait_recv()
                for n in range(a, b):
                    sums = g[s, n, layer, core].astype(F32) + r.rz_one[n].astype(F32)
                    r.ff_own[n] = sums.astype(BF16)
        else:
            for copy in along_back[k]:
                copy.wait_recv()
            for n in range(a, b):
                sums = g[s, n, layer, core].astype(F32)
                for i in steps:
                    sums = sums + r.rz[i, n].astype(F32)
                r.ff_own[n] = sums.astype(BF16)
        spread_out[k] = [
            push(r.ff_own.at[span], r.ff.at[s, span], (seq_at(i), t)) for i in range(1, S)
        ]
        own_sums.append(move(r.ff_own.at[span], r.ff.at[s, span]))

    def all_here(k):
        for copy in spread_out[k]:
            copy.wait_recv()

    for u in range(z.units, S * NR):
        g[u % S, u // S] = jnp.zeros((Z, 2, Hp, LANES), BF16)
    own = slice(RIM, RIM + N)
    act2_t = act2[own, :].astype(F32).T.astype(BF16)
    grad_units(z.nd + TAPS * z.nh, act2_t, lambda c, w: cote[own, c : c + w], z.nd)
    swap(3)
    edge_r.wait_recv()
    edge_l.wait_recv()
    r.hid[...] = lax.dot_general(cote[...], last_weight(), NT, preferred_element_type=F32)
    r.acc1[...] = jnp.zeros_like(r.acc1)
    r.acc2[...] = jnp.zeros_like(r.acc2)
    r.acc0[...] = jnp.zeros_like(r.acc0)

    def inner_norm_back(which, first, count, size, grad_store, acc_ref=None):
        gain = r.gains[which : which + 1, :]
        xhat_ref, slope_ref, scale_ref = (
            (r.xhat1, r.slope1, r.scale1),
            (r.xhat2, r.slope2, r.scale2),
        )[which]

        def body(i, carry):
            row = pl.multiple_of(first + i * size, 16)
            xhat = cells(xhat_ref, row, size)
            dpre = cells(r.hid, row, size) * cells(slope_ref, row, size)
            if acc_ref is not None:
                dgain = dpre * xhat
                acc_ref[...] += sum(dgain[n : n + 8] for n in range(0, size, 8))
            dx = dpre * gain
            plain = jnp.sum(dx, axis=1, keepdims=True) / H
            cross = jnp.sum(dx * xhat, axis=1, keepdims=True) / H
            grad_store(row, cells(scale_ref, row, size) * (dx - plain - xhat * cross))
            return carry

        lax.fori_loop(0, count, body, 0)

    dhid2 = r.dhid2
    dhid2[0:PAD, :] = jnp.zeros((PAD, HP), F32)
    dhid2[PAD + E :, :] = jnp.zeros((PAD, HP), F32)

    def keep_dhid2(row, grad):
        dhid2[pl.ds(pl.multiple_of(row + PAD, 8), grad.shape[0]), :] = grad.astype(BF16).astype(F32)

    inner_norm_back(1, 0, 1, RIM, keep_dhid2)
    inner_norm_back(1, RIM, N // BLOCK, BLOCK, keep_dhid2, r.acc2)
    inner_norm_back(1, RIM + N, 1, RIM, keep_dhid2)

    back = r.back
    for j, offset in enumerate(OFFSETS):
        first = PAD + RIM + offset
        back[:, j * HP : (j + 1) * HP] = (
            dhid2[first : first + N, :] * r.mask[RIM : RIM + N, j : j + 1]
        ).astype(BF16)
    total = None
    for j in range(TAPS):
        term = jnp.dot(
            back[:, j * HP : (j + 1) * HP], tap_weight(TAPS - 1 - j), preferred_element_type=F32
        )
        total = term if total is None else total + term
    r.hid[RIM : RIM + N, :] = total

    to_plane(3)
    dhid1 = r.dhid1

    def keep_dhid1(row, grad):
        dhid1[pl.ds(pl.multiple_of(row - RIM, 16), grad.shape[0]), :] = grad.astype(BF16)

    inner_norm_back(0, RIM, N // BLOCK, BLOCK, keep_dhid1, r.acc1)

    big[...] = jnp.dot(dhid1[...], first_weight(), preferred_element_type=F32)

    def first_norm_back(i, carry):
        row = pl.multiple_of(i * BLOCK, BLOCK)
        wide = pl.multiple_of(row + RIM, 16)
        scale = cells(r.scale0, wide, BLOCK)
        xhat = (cells(xe, wide, BLOCK).astype(F32) - cells(r.mean0, wide, BLOCK)) * scale
        dpre = cells(big, row, BLOCK) * cells(r.slope0, wide, BLOCK)
        dgain = dpre * xhat
        r.acc0[...] += sum(dgain[n : n + 8] for n in range(0, BLOCK, 8))
        dx = dpre * gain0
        plain = jnp.sum(dx, axis=1, keepdims=True) / D
        cross = jnp.sum(dx * xhat, axis=1, keepdims=True) / D
        grad = scale * (dx - plain - xhat * cross)
        r.gi_own[pl.ds(row, BLOCK), :] = (cells(cote, wide, BLOCK).astype(F32) + grad).astype(BF16)
        return carry

    gi, gi_own = r.gi, r.gi_own
    parts = 4
    part = N // parts
    per_part = part // BLOCK
    row_bases, to_core = {}, {}

    def rows_along(qs, js, at_end):
        def onward(j, place):
            to_core[q, j] = remote(place, place, partner)
            return [to_core[q, j]]

        for j in js:
            for q in qs:
                span = pl.ds(q * part, part)
                place = gi.at[2 * origins[j] + core, span]
                take(row_bases[q], j, place, onward, at_end, passed_all)

    def rows_own(q):
        span = pl.ds(q * part, part)
        copies = [
            remote(gi_own.at[span], gi.at[t, span], at_layer(to), row_bases[q] + j)
            for to, j in own_to
        ]
        if z.line:
            sent.append(copies[0])
            push_if(inner == 1, copies[1])
            copies[0].start()
        else:
            sent.extend(copies)
            for copy in copies:
                copy.start()

    own_pair = []
    for q in range(parts):
        lax.fori_loop(q * per_part, (q + 1) * per_part, first_norm_back, 0)
        span = pl.ds(q * part, part)
        row_bases[q] = arrivals(Z)
        rows_own(q)
        own_pair.append(push(gi_own.at[span], gi.at[t, span], partner))
    own_row = move(gi_own, gi.at[t])

    vec = r.vec
    sum0 = jnp.sum(r.acc0[...], axis=0, keepdims=True)
    sum1 = jnp.sum(r.acc1[...], axis=0, keepdims=True)
    sum2 = jnp.sum(r.acc2[...], axis=0, keepdims=True)
    vec[...] = jnp.zeros_like(vec)
    for j in range(z.nd):
        vec[j : j + 1, :] = sum0[:, j * LANES : (j + 1) * LANES]
    for j in range(z.nh):
        vec[z.nd + j : z.nd + j + 1, :] = sum1[:, j * LANES : (j + 1) * LANES]
        vec[z.nd + z.nh + j : z.nd + z.nh + j + 1, :] = sum2[:, j * LANES : (j + 1) * LANES]
    vec_plane = [push(vec, r.vec_plane.at[i], (seq_at(i), t)) for i in range(1, S)]

    dhid2_t = dhid2[PAD + RIM : PAD + RIM + N, :].T.astype(BF16)
    grad_units(z.nd, dhid2_t, lambda c, w: taps[own, c : c + w], TAPS * z.nh)
    swap(2)
    swap(1)
    dhid1_t = dhid1[...].astype(F32).T.astype(BF16)
    grad_units(0, dhid1_t, lambda c, w: r.act0[own, c : c + w], z.nd)
    swap(0)
    to_plane(2)
    turn_plane(3)
    to_plane(1)
    rows_along([0], [1, 2], False)
    rows_along([1], [1, 2], False)
    turn_plane(2)
    to_plane(0)
    to_z(3)
    z_start(3)
    rows_along([2], [1, 2], False)
    turn_plane(1)
    rows_along([3], [1, 2], False)

    for copy in vec_plane:
        copy.wait_recv()
    vec_sum = r.vec_sum
    vec_sum[...] = sum((r.vec_plane[i] for i in range(1, S)), vec[...])
    vec_z = [push(vec_sum, r.vec_z.at[i - 1], dev_z(i)) for i in range(1, Z)]

    z_over(3)
    to_z(2)
    z_start(2)
    rows_along([0], [3], False)
    rows_along([0, 1, 2, 3], [1], True)
    turn_plane(0)
    rows_along([1], [3], False)
    z_middle(3)
    z_over(2)
    to_z(1)
    z_start(1)
    rows_along([2], [3], False)
    to_z(0)
    z_start(0)
    z_middle(2)
    z_over(1)
    rows_along([3], [3], False)
    to_all(3)
    rows_along([0, 1], [2], True)
    z_over(0)
    z_middle(1)
    to_all(2)
    rows_along([2, 3], [2], True)
    z_middle(0)
    to_all(1)
    rows_along([0], range(3, Z), True)
    to_all(0)
    rows_along([1], range(3, Z), True)

    for copy in vec_z:
        copy.wait_recv()
    vec_half = r.vec_half
    vec_half[...] = sum((r.vec_z[i - 1] for i in range(1, Z)), vec_sum[...])
    vec_core = push(vec_half, r.gain_sums.at[1], partner)
    own_sums.append(move(vec_half, r.gain_sums.at[0]))
    rows_along([2, 3], range(3, Z), True)
    for k in reversed(range(STAGES)):
        all_here(k)

    vec_core.wait_recv()
    for copy in own_sums:
        copy.wait()
    out_own.wait()
    for copy in out_copies:
        copy.wait_recv()
    own_row.wait()
    for copy in own_pair:
        copy.wait_recv()
    for copy in to_core.values():
        copy.wait_recv()
    assert all(n <= sems.shape[0] for n, sems in zip(counts, (send, recv, local)))
    for copy in sent:
        copy.wait_send()
    for when, copy in sent_if:

        @pl.when(when)
        def _():
            copy.wait_send()


def finish(z, *refs):
    got, gi_got, ff, gain_sums = refs[:4]
    out, gi, grad_first, grad_conv, grad_last, grad_gain, grad_gain1, grad_gain2, *refs = refs[4:]
    first, conv, last, gains, sems = refs
    t = lax.axis_index("tp")
    copies = []

    def move(src, dst):
        copy = pltpu.make_async_copy(src, dst, sems.at[len(copies)])
        copy.start()
        copies.append(copy)

    half = z.R // 2
    for i in range(2):
        move(gi_got.at[pl.ds(i * half, half)], gi.at[pl.ds(i * half, half)])
    move(got, out)

    def summed(start, count):
        return jnp.concatenate(
            [ff[u % z.S, u // z.S].astype(F32) for u in range(start, start + count)], axis=1
        )

    first[...] = summed(0, z.nd)
    move(first, grad_first)
    for k in range(TAPS):
        conv[k] = summed(z.nd + k * z.nh, z.nh)
    move(conv, grad_conv)
    last[...] = summed(z.nd + TAPS * z.nh, z.nd)
    move(last, grad_last)
    sums = gain_sums[0] + gain_sums[1]

    def line(start, count):
        return jnp.concatenate([sums[j : j + 1, :] for j in range(start, start + count)], axis=1)

    def picked(row, width, step):
        return sum(
            jnp.where(t == j, row[:, j * step : j * step + width], 0.0) for j in range(z.T)
        )

    grad_gain[...] = picked(line(0, z.nd), z.Dt, z.Dt)
    grad_gain1[...] = picked(line(z.nd, z.nh), z.Hs, z.Hp)
    grad_gain2[...] = picked(line(z.nd + z.nh, z.nh), z.Hs, z.Hp)
    for copy in copies:
        copy.wait()


def shards(
    mesh,
    inputs,
    starts,
    first_proj,
    dilated_conv,
    last_proj,
    first_norm_gain,
    second_norm_gain,
    third_norm_gain,
    cotangent,
):
    z = Sizes(mesh, inputs, starts, first_proj, cotangent)
    S, T, Z, N, D, E, HP, Hp, NR = z.S, z.T, z.Z, z.N, z.D, z.E, z.HP, z.Hp, z.NR
    more = Hp - z.Hs
    first, last = first_proj.T, last_proj
    conv = dilated_conv.transpose(0, 2, 1)
    if more:
        first, last = (jnp.pad(part, ((0, more), (0, 0))) for part in (first, last))
        conv = jnp.pad(
            conv.reshape(TAPS, z.Hs, T, z.Hs), ((0, 0), (0, more), (0, 0), (0, more))
        ).reshape(TAPS, Hp, HP)
    vm, anywhere = pltpu.VMEM, pl.ANY
    ins = dict(
        x=(inputs, anywhere),
        starts=(starts, vm),
        w1=(first, anywhere),
        wc=(conv, anywhere),
        w3=(last, anywhere),
        g1=(first_norm_gain.reshape(z.nd, LANES), vm),
        g2=(second_norm_gain.reshape(1, z.Hs), vm),
        g3=(third_norm_gain.reshape(1, z.Hs), vm),
        cot=(cotangent.transpose(0, 2, 1), anywhere),
    )
    outs = dict(
        out=((z.R, z.Dt, N), BF16),
        gi=((z.R, N, D), BF16),
        ff=((S, NR, Hp, LANES), BF16),
        gain_sums=((2, 24, LANES), F32),
    )
    near = vm if z.line else jax.ShapeDtypeStruct
    scratch = dict(
        send=pltpu.SemaphoreType.DMA((226 if z.line else 800,)),
        recv=pltpu.SemaphoreType.DMA((222 if z.line else 800,)),
        local=pltpu.SemaphoreType.DMA((13,)),
        xe=vm((E, D), BF16),
        cote=vm((E, D), BF16),
        act0=vm((E, D), BF16),
        slope0=vm((E, D), F32),
        mean0=vm((E, 1), F32),
        scale0=vm((E, 1), F32),
        mask=vm((E, LANES), F32),
        flags_left=vm((z.R, N), jnp.int32),
        flags_right=vm((z.R, N), jnp.int32),
        gslots=vm((T, 8, LANES), F32),
        gains=vm((8, HP), F32),
        wg=vm((S, NR, Z, 2, Hp, LANES), BF16),
        hid=vm((E, HP), F32),
        xhat1=vm((E, HP), F32),
        slope1=vm((E, HP), F32),
        scale1=vm((E, 1), F32),
        xhat2=vm((E, HP), F32),
        slope2=vm((E, HP), F32),
        scale2=vm((E, 1), F32),
        act1=vm((E + 2 * PAD, HP), F32),
        dhid2=vm((E + 2 * PAD, HP), F32),
        taps=vm((E, TAPS * HP), BF16),
        back=vm((N, TAPS * HP), BF16),
        act2=vm((E, HP), BF16),
        dhid1=vm((N, HP), BF16),
        big=vm((N, D), F32),
        gi_own=vm((N, D), BF16),
        acc0=vm((8, D), F32),
        acc1=vm((8, HP), F32),
        acc2=vm((8, HP), F32),
        cot_t=vm((D, N), BF16),
        out_t=vm((D, N), BF16),
        w1_in=vm((Hp, D), BF16),
        wc_in=vm((TAPS, Hp, HP), BF16),
        w3_in=vm((Hp, D), BF16),
        gl=vm((8, LANES), F32),
        g=vm((S, NR, Z, 2, Hp, LANES), BF16),
        rc=vm((S, NR, Z, Hp, LANES), BF16),
        ff_own=vm((NR, Hp, LANES), BF16),
        vec=vm((24, LANES), F32),
        vec_sum=vm((24, LANES), F32),
        vec_plane=vm((S, 24, LANES), F32),
        vec_z=vm((Z, 24, LANES), F32),
        vec_half=vm((24, LANES), F32),
    )
    if z.line:
        scratch.update(rz_end=vm((NR, 3, Hp, LANES), BF16))
        scratch.update(rz_pair=vm((NR, 2, Hp, LANES), BF16), rz_one=vm((NR, Hp, LANES), BF16))
    else:
        scratch.update(rz=vm((Z, NR, Hp, LANES), BF16))
    if z.square:
        scratch.update(rx=vm((2, NR, Z // 2, Hp, LANES), BF16))
        scratch.update(ry=vm((2, NR, Z // 2, Hp, LANES), BF16))
        scratch.update(rx2=vm((NR, Z // 2, Hp, LANES), BF16))
        scratch.update(ry2=vm((NR, Z // 2, Hp, LANES), BF16))
    else:
        scratch.update(rd=vm((S, NR, Z, Hp, LANES), BF16))
    names = [*ins, *outs, *scratch]
    results = pl.pallas_call(
        functools.partial(kernel, z, names),
        out_shape=[near(shape, kind) for shape, kind in outs.values()],
        in_specs=[pl.BlockSpec(memory_space=space) for _, space in ins.values()],
        out_specs=[pl.BlockSpec(memory_space=anywhere)] * len(outs),
        scratch_shapes=list(scratch.values()),
        compiler_params=pltpu.CompilerParams(
            collective_id=0, has_side_effects=True, vmem_limit_bytes=(50 if z.line else 63) * 2**20
        ),
    )(*[array for array, _ in ins.values()])
    if z.line:
        results = [pltpu.with_memory_space_constraint(part, vm) for part in results]
    shape = jax.ShapeDtypeStruct
    out, gi, grad_first, grad_conv, grad_last, grad_gain, grad_gain1, grad_gain2 = pl.pallas_call(
        functools.partial(finish, z),
        out_shape=[
            shape((z.R, z.Dt, N), BF16),
            shape((z.R, N, D), BF16),
            shape((Hp, D), F32),
            shape((TAPS, Hp, HP), F32),
            shape((Hp, D), F32),
            shape((1, z.Dt), F32),
            shape((1, z.Hs), F32),
            shape((1, z.Hs), F32),
        ],
        in_specs=[pl.BlockSpec(memory_space=space) for space in (anywhere, anywhere, vm, vm)],
        out_specs=[pl.BlockSpec(memory_space=space) for space in [anywhere] * 5 + [vm] * 3],
        scratch_shapes=[
            vm((Hp, D), F32),
            vm((TAPS, Hp, HP), F32),
            vm((Hp, D), F32),
            vm((8, LANES), F32),
            pltpu.SemaphoreType.DMA((6,)),
        ],
        compiler_params=pltpu.CompilerParams(vmem_limit_bytes=12 * 2**20),
    )(*results)
    if more:
        grad_first, grad_last = grad_first[: z.Hs], grad_last[: z.Hs]
        grad_conv = grad_conv.reshape(TAPS, Hp, T, Hp)[:, : z.Hs, :, : z.Hs]
        grad_conv = grad_conv.reshape(TAPS, z.Hs, z.H)
    return (
        out.transpose(0, 2, 1),
        gi,
        grad_first.T,
        grad_conv.transpose(0, 2, 1),
        grad_last,
        grad_gain.reshape(-1),
        grad_gain1.reshape(-1),
        grad_gain2.reshape(-1),
    )


def solution(mesh):
    placed = (
        P(None, "seq", None),
        P(None, "seq"),
        P(None, "tp"),
        P(None, None, "tp"),
        P("tp", None),
        P(),
        P("tp"),
        P("tp"),
        P(None, "seq", "tp"),
    )
    return jax.shard_map(
        functools.partial(shards, mesh),
        mesh=mesh,
        in_specs=placed,
        out_specs=(
            P(None, "seq", "tp"),
            P(None, "seq", None),
            P(None, "tp"),
            P(None, None, "tp"),
            P("tp", None),
            P("tp"),
            P("tp"),
            P("tp"),
        ),
        check_vma=False,
    )
```

time: 175 us -> 118 us (0.67)
  Pallas kernels: 147 us -> 117 us
  local copies, waits for them, and re-layouts: 25.5 us -> 0 us
    pallas_call x1 -> x2, Pallas kernels: 147 us -> 117 us  [the longest x1 113 us: shards(): pl.pallas_call(functools.partial(kernel, z, names), out_shape=[near(shape...]
    unnamed x21 -> x0, local copies, waits for them, and re-layouts: 16 us -> none
    reshape x5 -> x0, local copies, waits for them, and re-layouts: 8.95 us -> none  [the longest x2 5.58 us: packed_weights(): dilated_conv.reshape(TAPS, z.Z, 2, z.Hs, z.Hs).transpose(0, 4, 2, 1, 3)]
where the time goes in v2:
time: 118 us; the launch traced here: 117 us
  Pallas kernels  117 us (99%)
    pallas_call x1, Pallas kernels, shards(): pl.pallas_call(functools.partial(kernel, z, names), out_shape=[near(shape...  113 us
    pallas_call x1, Pallas kernels, shards(): pl.pallas_call(functools.partial(finish, z), out_shape=[shape((z.R, z.Dt,...  3.73 us

profile of v2, /device:TPU:0, one launch (start us, length us, event | category | flops | bytes accessed | tf_op | source)
XLA Modules:
  0.0 117.5 jit_solution(7977504001779080879)
XLA Ops:
  0.6 112.9 %shard_map.152 = (bf16[8,160,256]{2,1,0:T(8,128)(2,1)S(1)}, bf16[8,256,1280]{2,1,0:T(8,128)(2,1)S(1)}, bf16[4,12,80,128]{3,2,1,0:T(8,128)(2,1)S(1)}, f32[2,24,128]{2,1,0:T(8,128)S(1)}) custom-call(bf16[8,256,1280]{2,1,0:T(8,128)(2,1)} %refs_0_.1, s32[8,256]{1,0:T(8,128)} %refs_1_.1, bf16[80,1280]{1,0:T(8,128)(2,1)} %bitcast.14, ...), custom_call_target="tpu_custom_call" | custom-call | tf_op jit(solution)/shard_map/pallas_call | solution.py:977
  113.6 3.7 %shard_map.153 = (bf16[8,160,256]{2,1,0:T(8,128)(2,1)}, bf16[8,256,1280]{2,1,0:T(8,128)(2,1)}, f32[80,1280]{1,0:T(8,128)}, f32[5,80,640]{2,1,0:T(8,128)}, f32[80...) custom-call(bf16[8,160,256]{2,1,0:T(8,128)(2,1)S(1)} %get-tuple-element.20.refs_0_, ...), custom_call_target="tpu_custom_call" | custom-call | tf_op jit(solution)/shard_map/pallas_call | solution.py:990

commit v3 on v2

--- a/solution.py
+++ b/solution.py
@@ -20,7 +20,8 @@
 RIM = 16
 PAD = 8
 STAGES = 4
-BLOCK = 32
+REST = STAGES
+BLOCK = 64
 HALF_ROOT = 0.7071067811865476
 PEAK = 0.3989422804014327
 
@@ -44,11 +45,14 @@
         self.nd = self.D // LANES
         self.nh = self.HP // LANES
         self.units = 2 * self.nd + TAPS * self.nh
-        self.NR = -(-self.units // self.S)
+        one, two = -(-self.nd // self.S), -(-(self.nd + TAPS * self.nh) // self.S)
+        whole = self.units // self.S
+        self.rest = self.units % self.S if whole > two else 0
+        self.NF = whole if self.rest else -(-self.units // self.S)
+        self.NR = self.NF + (self.rest > 0)
+        self.chunks = [(0, one), (one, (one + two) // 2), ((one + two) // 2, two), (two, self.NF)]
         self.Dt = cotangent.shape[2]
         assert self.Dt % 16 == 0
-        cuts = [round(i * self.NR / STAGES) for i in range(STAGES + 1)]
-        self.chunks = list(zip(cuts[:-1], cuts[1:]))
         self.square = self.S == 4
         self.line = self.Z == 4
 
@@ -72,37 +76,39 @@
 
     send, recv, local = r.send, r.recv, r.local
     counts = [0, 0, 0]
-    sent, sent_if = [], []
-
-    def remote(src, dst, device, arrival=None):
-        counts[0] += 1
+    sent, sent_if, together = [], [], []
+
+    def remote(src, dst, device, arrival=None, sends=None):
         return pltpu.make_async_remote_copy(
             src_ref=src,
             dst_ref=dst,
-            send_sem=send.at[counts[0] - 1],
+            send_sem=send.at[sendings() if sends is None else sends],
             recv_sem=recv.at[arrivals(1) if arrival is None else arrival],
             device_id=device,
             device_id_type=MESH,
         )
 
+    def sendings():
+        counts[0] += 1
+        return counts[0] - 1
+
     def arrivals(count):
         counts[1] += count
         return counts[1] - count
 
+    def shared(place):
+        pair = (arrivals(1), sendings())
+        together.append((pair[1], place))
+        return pair
+
     def arrived(arrival, place):
-        pltpu.make_async_remote_copy(
-            src_ref=place,
-            dst_ref=place,
-            send_sem=send.at[0],
-            recv_sem=recv.at[arrival],
-            device_id=partner,
-            device_id_type=MESH,
-        ).wait_recv()
-
-    def push(src, dst, device, arrival=None):
-        copy = remote(src, dst, device, arrival)
+        remote(place, place, partner, arrival, 0).wait_recv()
+
+    def push(src, dst, device, arrival=None, sends=None):
+        copy = remote(src, dst, device, arrival, sends)
         copy.start()
-        sent.append(copy)
+        if sends is None:
+            sent.append(copy)
         return copy
 
     def push_if(when, copy):
@@ -135,39 +141,54 @@
         first = inner * (3 - layer) + (1 - inner) * middle
         second = inner * end + (1 - inner) * (3 - middle)
         origins = [None, first, second, 3 - end]
-        own_to = [(first, 2 - inner), (second, 3 - 2 * inner)]
-        passed = {1: (end, 2), 3: (end, 3)}
-        passed_all = {**passed, 2: (3 - layer, 3)}
+        own_to = [(first, 2 - inner), (end, 1)]
+        passed = {1: (end, 2), 2: (3 - layer, 3), 3: (end, 3)}
     else:
         origins = [None] + [z_at(-i) for i in steps]
         own_to = [(z_at(i), i) for i in steps]
-        passed, passed_all, inner = {}, {}, 0
+        passed, inner = {}, 0
 
     def at_layer(to):
         return (s, 2 * to + core)
 
-    def take(base, j, place, onward, at_end, passing):
+    def only(at_end, go):
+        if z.line:
+            pl.when(inner == 1 - at_end)(go)
+        elif at_end:
+            go()
+
+    def send_own(base, src, place, later=False):
+        copies = [remote(src, place, at_layer(to), base + j) for to, j in own_to]
+        if z.line:
+            push_if(inner == 1, copies.pop())
+        sent.extend(copies)
+        later = later and z.line
+        for copy in copies:
+            if later:
+                pl.when(inner == 1)(copy.start)
+            else:
+                copy.start()
+        return (lambda: pl.when(inner == 0)(copies[0].start)) if later else (lambda: None)
+
+    def take(base, j, place, onward, at_end, start=True):
         if base + j not in onwards:
             extra = None
-            if j in passing:
-                to, then = passing[j]
+            if j in passed:
+                to, then = passed[j]
                 extra = remote(place, place, at_layer(to), base + then)
                 sent_if.append((inner == 1, extra))
             onwards[base + j] = (extra, onward(j, place))
-            sent.extend(onwards[base + j][1])
 
         def go():
             extra, copies = onwards[base + j]
             arrived(base + j, place)
             if extra is not None and not at_end:
                 extra.start()
-            for copy in copies:
-                copy.start()
-
-        if z.line:
-            pl.when(inner == 1 - at_end)(go)
-        elif at_end:
-            go()
+            if start:
+                for copy in copies:
+                    copy.start()
+
+        only(at_end, go)
 
     onwards = {}
     right, left = (seq_at(1), t), (seq_at(-1), t)
@@ -197,11 +218,14 @@
     flags_l = push(r.starts, r.flags_right, left)
     r.gl[0:1, : z.Hs] = r.g2[...]
     r.gl[1:2, : z.Hs] = r.g3[...]
-    gain_copies = [push(r.gl, r.gslots.at[t], (s, lax.rem(t + i, T))) for i in range(1, T)]
+    some_gains = r.gslots.at[pl.ds(0, T - 1)]
+    for_gains = shared(some_gains)
+    for i in range(1, T):
+        push(r.gl, r.gslots.at[t], (s, lax.rem(t + i, T)), *for_gains)
     gain_own = move(r.gl, r.gslots.at[t])
 
     wg = r.wg
-    bases, own_core = {}, {}
+    bases, plane = {}, {}
     plane_x, plane_y, plane_d, plane_any, across = {}, {}, {}, {}, {}
 
     def unit_in(u):
@@ -219,67 +243,106 @@
         a, b = z.chunks[k]
         return pl.ds(a, b - a)
 
+    def carried(ref, k, which, c):
+        if k == REST:
+            return ref.at[pl.ds(0, z.rest), z.NF, which, c]
+        return ref.at[s, rounds(k), which, c]
+
+    def every(ref, k, which, c):
+        return carried(ref, k, which, c) if k == REST else ref.at[:, rounds(k), which, c]
+
+    every_chip = pl.ds(0, Z)
+
     def weights_own(k):
-        for q in range(S):
-            for n in range(*z.chunks[k]):
-                wg[q, n, layer, core] = unit_in(n * S + q)
-        place = wg.at[s, rounds(k), layer, core]
+        if k == REST:
+            for q in range(z.rest):
+                wg[q, z.NF, layer, core] = unit_in(z.NF * S + q)
+        else:
+            for q in range(S):
+                for n in range(*z.chunks[k]):
+                    wg[q, n, layer, core] = unit_in(n * S + q)
+        place = carried(wg, k, layer, core)
         bases[k] = arrivals(Z)
-        for to, j in own_to:
-            push(place, place, at_layer(to), bases[k] + j)
-        place = wg.at[:, rounds(k), layer, core]
-        own_core[k] = push(place, place, partner)
-
-    def weights_along(k, at_end, js=steps):
+        send_own(bases[k], place, place)
+        across[k] = shared(every(wg, k, every_chip, core))
+        place = every(wg, k, layer, core)
+        push(place, place, partner, *across[k])
+        if k != REST:
+            copies = S if z.square else S - 1
+            plane[k] = sendings()
+            together.append(
+                (plane[k], wg.at[pl.ds(0, copies - z.square), rounds(k), pl.ds(0, Z - 1), core])
+            )
+
+    def weights_along(k, at_end, js=steps, start=True):
         def onward(j, place):
+            if k == REST:
+                return [remote(place, place, partner, *across[k])]
             if not z.square:
-                plane_any[k, j] = [remote(place, place, (seq_at(i), t)) for i in range(1, S)]
+                plane_any[k, j] = [
+                    remote(place, place, (seq_at(i), t), None, plane[k]) for i in range(1, S)
+                ]
                 return plane_any[k, j]
-            plane_x[k, j] = remote(place, place, x_side)
-            plane_y[k, j] = remote(place, place, y_side)
+            plane_x[k, j] = remote(place, place, x_side, None, plane[k])
+            plane_y[k, j] = remote(place, place, y_side, None, plane[k])
             return [plane_x[k, j], plane_y[k, j]]
 
         for j in js:
-            take(bases[k], j, wg.at[s, rounds(k), origins[j], core], onward, at_end, passed)
-
-    def weights_corner(k):
+            take(bases[k], j, carried(wg, k, origins[j], core), onward, at_end, start)
+
+    def weights_spread(k, js=steps):
+        def go():
+            for j in js:
+                for copy in onwards[bases[k] + j][1]:
+                    copy.start()
+
+        only(False, go)
+
+    def weights_corner(k, at_end):
         if not z.square:
             return
         for j in steps:
-            across[k, j] = []
-            over_y = (k + j) % 2
-            place = wg.at[sx if over_y else sy, rounds(k), origins[j], core]
-            plane_x[k, j].wait_recv()
-            plane_y[k, j].wait_recv()
-            plane_d[k, j] = push(place, place, y_side if over_y else x_side)
-            for q in (s, sx, sy):
-                place = wg.at[q, rounds(k), origins[j], core]
-                across[k, j].append(push(place, place, partner))
-
-    def weights_across(k):
-        for j in steps:
+            if (k, j) not in plane_d:
+                over_y = (k + j) % 2
+                place = wg.at[sx if over_y else sy, rounds(k), origins[j], core]
+                side = y_side if over_y else x_side
+                plane_d[k, j] = remote(place, place, side, None, plane[k])
+
+        def go():
+            for j in steps:
+                plane_x[k, j].wait_recv()
+                plane_y[k, j].wait_recv()
+                plane_d[k, j].start()
+                for q in (s, sx, sy):
+                    place = wg.at[q, rounds(k), origins[j], core]
+                    push(place, place, partner, *across[k])
+
+        only(at_end, go)
+
+    def weights_across(k, js=steps):
+        for j in js:
             if z.square:
                 plane_d[k, j].wait_recv()
                 place = wg.at[sd, rounds(k), origins[j], core]
-                across[k, j].append(push(place, place, partner))
             else:
                 for copy in plane_any[k, j]:
                     copy.wait_recv()
                 place = wg.at[:, rounds(k), origins[j], core]
-                across[k, j] = [push(place, place, partner)]
+            push(place, place, partner, *across[k])
 
     def weights_ready(k):
-        own_core[k].wait_recv()
-        for j in steps:
-            for copy in across[k, j]:
-                copy.wait_recv()
-
-    cot_copies = []
-
-    def cotangent_out():
-        for i in range(1, T):
-            to = lax.rem(t + i, T)
-            cot_copies.append(push(cot.at[to], cot_t.at[features(t)], (s, to)))
+        arrived(across[k][0], every(wg, k, every_chip, 1 - core))
+
+    some_cot = cot_t.at[pl.ds(0, (T - 1) * z.Dt)]
+    for_cot = shared(some_cot)
+
+    def cotangent_out(at_end):
+        def go():
+            for i in range(1, T):
+                to = lax.rem(t + i, T)
+                push(cot.at[to], cot_t.at[features(t)], (s, to), *for_cot)
+
+        only(at_end, go)
 
     weights_in[0].wait()
     weights_in[1].wait()
@@ -288,10 +351,9 @@
     weights_in[2].wait()
     weights_own(2)
     weights_own(3)
-    for k in range(STAGES):
-        weights_along(k, False)
-        weights_along(k, True, [1])
-
+    some_rest = [REST] if z.rest else []
+    for k in some_rest:
+        weights_own(k)
     def unit(ref, u):
         return ref[u % S, u // S].reshape(HP, LANES)
 
@@ -308,29 +370,40 @@
         return weights(z.nd + TAPS * z.nh, z.nd)
 
     row_in.wait()
+
+    gain0 = jnp.concatenate([r.g1[j : j + 1, :] for j in range(z.nd)], axis=1)
+
+    def first_norm(first, count, size):
+        def body(i, carry):
+            row = pl.multiple_of(first + i * size, 16)
+            v = cells(xe, row, size).astype(F32)
+            mean = jnp.sum(v, axis=1, keepdims=True) / D
+            spread = jnp.sum(v * v, axis=1, keepdims=True) / D - mean * mean
+            scale = lax.rsqrt(spread + EPS)
+            act, slope = gelu_parts((v - mean) * scale * gain0)
+            r.act0[pl.ds(row, size), :] = act.astype(BF16)
+            r.slope0[pl.ds(row, size), :] = slope
+            r.mean0[pl.ds(row, size), :] = mean
+            r.scale0[pl.ds(row, size), :] = scale
+            return carry
+
+        lax.fori_loop(0, count, body, 0)
+
+    first_norm(RIM, N // BLOCK, BLOCK)
+
+    for k in range(STAGES):
+        weights_along(k, False, steps[:2], k < 2)
+        weights_along(k, True, steps[:1])
+    for k in some_rest:
+        weights_along(k, False, steps[:2])
+        weights_along(k, True, steps[:1])
     rim_r.wait_recv()
     rim_l.wait_recv()
-
-    gain0 = jnp.concatenate([r.g1[j : j + 1, :] for j in range(z.nd)], axis=1)
-
-    def first_norm(i, carry):
-        row = pl.multiple_of(i * BLOCK, BLOCK)
-        v = cells(xe, row, BLOCK).astype(F32)
-        mean = jnp.sum(v, axis=1, keepdims=True) / D
-        spread = jnp.sum(v * v, axis=1, keepdims=True) / D - mean * mean
-        scale = lax.rsqrt(spread + EPS)
-        act, slope = gelu_parts((v - mean) * scale * gain0)
-        r.act0[pl.ds(row, BLOCK), :] = act.astype(BF16)
-        r.slope0[pl.ds(row, BLOCK), :] = slope
-        r.mean0[pl.ds(row, BLOCK), :] = mean
-        r.scale0[pl.ds(row, BLOCK), :] = scale
-        return carry
-
-    lax.fori_loop(0, E // BLOCK, first_norm, 0)
+    first_norm(0, 1, RIM)
+    first_norm(RIM + N, 1, RIM)
 
     gain_own.wait()
-    for copy in gain_copies:
-        copy.wait_recv()
+    arrived(for_gains[0], some_gains)
     for j in range(T):
         r.gains[0:2, j * Hp : (j + 1) * Hp] = r.gslots[j, 0:2, :Hp]
 
@@ -353,22 +426,41 @@
         inside = (begun == 0.0) & (moved >= 0) & (moved < S * N)
         r.mask[:, k : k + 1] = inside.astype(F32)
 
-    weights_along(0, True, steps[1:])
-    weights_along(1, True, steps[1:])
-    weights_corner(0)
-    weights_along(2, True, steps[1:])
-    weights_corner(1)
-    cotangent_out()
-    weights_along(3, True, steps[1:])
-    weights_corner(2)
-    weights_across(0)
-    weights_corner(3)
+    third = steps[2:]
+    weights_along(0, False, third)
+    weights_along(0, True, [2])
+    weights_along(1, False, third)
+    weights_along(1, True, [2])
+    weights_along(2, False, third, False)
+    weights_along(2, True, [2])
+    weights_along(3, False, third, False)
+    for k in some_rest:
+        weights_along(k, False, third)
+    weights_corner(0, False)
+    weights_spread(2)
+    weights_along(0, True, third)
+    weights_along(1, True, third)
+    weights_along(3, True, [2])
+    weights_along(2, True, third)
+    cotangent_out(True)
+    weights_corner(0, True)
+    weights_corner(1, False)
+    weights_along(3, True, third)
+    for k in some_rest:
+        weights_along(k, True, steps[1:])
+    weights_corner(1, True)
+    weights_spread(3)
+    weights_across(0, steps[:1])
+    cotangent_out(False)
+    weights_across(0, steps[1:])
 
     weights_ready(0)
     r.hid[...] = lax.dot_general(r.act0[...], first_weight(), NT, preferred_element_type=F32)
+    weights_corner(2, False)
+    weights_corner(2, True)
     weights_across(1)
 
-    def inner_norm(which, act_store):
+    def inner_norm(which, act_store, first, count, size):
         gain = r.gains[which : which + 1, :]
         xhat_ref, slope_ref, scale_ref = (
             (r.xhat1, r.slope1, r.scale1),
@@ -376,51 +468,55 @@
         )[which]
 
         def body(i, carry):
-            row = pl.multiple_of(i * BLOCK, BLOCK)
-            v = cells(r.hid, row, BLOCK)
+            row = pl.multiple_of(first + i * size, 16)
+            v = cells(r.hid, row, size)
             mean = jnp.sum(v, axis=1, keepdims=True) / H
             spread = jnp.sum(v * v, axis=1, keepdims=True) / H - mean * mean
             scale = lax.rsqrt(spread + EPS)
             xhat = (v - mean) * scale
             act, slope = gelu_parts(xhat * gain)
             act_store(row, act)
-            xhat_ref[pl.ds(row, BLOCK), :] = xhat
-            slope_ref[pl.ds(row, BLOCK), :] = slope
-            scale_ref[pl.ds(row, BLOCK), :] = scale
+            xhat_ref[pl.ds(row, size), :] = xhat
+            slope_ref[pl.ds(row, size), :] = slope
+            scale_ref[pl.ds(row, size), :] = scale
             return carry
 
-        lax.fori_loop(0, E // BLOCK, body, 0)
+        lax.fori_loop(0, count, body, 0)
 
     act1, taps = r.act1, r.taps
     act1[0:PAD, :] = jnp.zeros((PAD, HP), F32)
     act1[PAD + E :, :] = jnp.zeros((PAD, HP), F32)
 
     def keep_act1(row, act):
-        act1[pl.ds(pl.multiple_of(row + PAD, 8), BLOCK), :] = act.astype(BF16).astype(F32)
-
-    inner_norm(0, keep_act1)
+        act1[pl.ds(pl.multiple_of(row + PAD, 8), act.shape[0]), :] = act.astype(BF16).astype(F32)
+
+    inner_norm(0, keep_act1, RIM, N // BLOCK, BLOCK)
+    inner_norm(0, keep_act1, 0, 1, RIM)
+    inner_norm(0, keep_act1, RIM + N, 1, RIM)
     for k, offset in enumerate(OFFSETS):
         taps[:, k * HP : (k + 1) * HP] = (
             act1[PAD + offset : PAD + offset + E, :] * r.mask[:, k : k + 1]
         ).astype(BF16)
 
-    weights_across(2)
-
-    weights_ready(1)
-    weights_ready(2)
-    total = None
-    for k in range(TAPS):
-        if k == TAPS - 2:
-            weights_across(3)
-        term = lax.dot_general(
+
+    def tap_term(k):
+        return lax.dot_general(
             taps[:, k * HP : (k + 1) * HP], tap_weight(k), NT, preferred_element_type=F32
         )
-        total = term if total is None else total + term
+
+    weights_ready(1)
+    total = tap_term(0) + tap_term(1)
+    weights_corner(3, False)
+    weights_corner(3, True)
+    weights_across(2)
+    weights_ready(2)
+    for k in range(2, TAPS):
+        total = total + tap_term(k)
     r.hid[...] = total
+    weights_across(3)
 
     cot_own.wait()
-    for copy in cot_copies:
-        copy.wait_recv()
+    arrived(for_cot[0], some_cot)
     cote = r.cote
     cote[RIM : RIM + N, :] = cot_t[...].T
     edge_r = push(cote.at[pl.ds(N, RIM)], cote.at[pl.ds(0, RIM)], right)
@@ -429,19 +525,35 @@
     act2 = r.act2
 
     def keep_act2(row, act):
-        act2[pl.ds(row, BLOCK), :] = act.astype(BF16)
-
-    inner_norm(1, keep_act2)
-
-    weights_ready(3)
-    big = r.big
-    big[...] = jnp.dot(act2[RIM : RIM + N, :], last_weight(), preferred_element_type=F32)
-    out_t = r.out_t
-    out_t[...] = (big[...] + xe[RIM : RIM + N, :].astype(F32)).astype(BF16).T
-    out_copies = []
-    for i in range(1, T):
-        to = lax.rem(t + i, T)
-        out_copies.append(push(out_t.at[features(to)], r.out.at[t], (s, to)))
+        act2[pl.ds(row, act.shape[0]), :] = act.astype(BF16)
+
+    inner_norm(1, keep_act2, RIM, N // BLOCK, BLOCK)
+
+    for k in [3, *some_rest]:
+        weights_ready(k)
+    big, out_t = r.big, r.out_t
+    some_out = r.out.at[pl.ds(0, T - 1)]
+    for_out = shared(some_out)
+    half_units = z.nd // 2
+    own_half = layer // (Z // 2)
+    for n in range(2):
+        half = own_half if n == 0 else 1 - own_half
+        units = [z.nd + TAPS * z.nh + half * half_units + j for j in range(half_units)]
+        span = pl.ds(pl.multiple_of(half * half_units * LANES, LANES), half_units * LANES)
+        rows = jnp.dot(
+            act2[RIM : RIM + N, :],
+            jnp.concatenate([unit(wg, u) for u in units], axis=1),
+            preferred_element_type=F32,
+        )
+        rows = rows + xe[RIM : RIM + N, span].astype(F32)
+        out_t[span, :] = rows.astype(BF16).T
+        for i in range(T // 2):
+            to = half * (T // 2) + lax.rem(t + i, T // 2)
+
+            @pl.when(to != t)
+            def _():
+                push(out_t.at[features(to)], r.out.at[t], (s, to), *for_out)
+
     out_own = move(out_t.at[features(t)], r.out.at[t])
 
     g = r.g
@@ -457,35 +569,43 @@
                 g[u % S, u // S] = block[:, i * LANES : (i + 1) * LANES].reshape(Z, 2, Hp, LANES)
 
     rc = r.rc
-    swaps, plane1, plane2, along_back, spread_out = {}, {}, {}, {}, {}
+    swaps, plane1, plane2, along_back = {}, {}, {}, {}
+    some_sums = r.ff.at[pl.ds(0, S - 1), pl.ds(0, z.NF)]
+    spread_out = shared(some_sums)
     beside, over, own_sums = {}, {}, []
 
     def swap(k):
-        a, b = z.chunks[k]
-        span = pl.ds(a, b - a)
-        swaps[k] = push(g.at[:, span, :, 1 - core], rc.at[:, span], partner)
+        place = every(g, k, every_chip, 1 - core)
+        to = rc.at[pl.ds(0, z.rest), z.NF] if k == REST else rc.at[:, rounds(k)]
+        swaps[k] = push(place, to, partner)
+
+    def add_swapped(k):
+        swaps[k].wait_recv()
+        at_ = [(q, z.NF) for q in range(z.rest)]
+        if k != REST:
+            at_ = [(q, n) for q in range(S) for n in range(*z.chunks[k])]
+        for q, n in at_:
+            g[q, n, :, core] = (g[q, n, :, core].astype(F32) + rc[q, n].astype(F32)).astype(BF16)
 
     near, far = pl.ds(0, Z // 2), pl.ds(Z // 2, Z // 2)
 
     def to_plane(k):
         a, b = z.chunks[k]
         span = pl.ds(a, b - a)
-        swaps[k].wait_recv()
-        for q in range(S):
-            for n in range(a, b):
-                g[q, n, :, core] = (g[q, n, :, core].astype(F32) + rc[q, n].astype(F32)).astype(BF16)
+        add_swapped(k)
         if z.square:
-            plane1[k] = [
-                push(g.at[sx, span, near, core], r.rx.at[0, span], x_side),
-                push(g.at[sd, span, near, core], r.rx.at[1, span], x_side),
-                push(g.at[sy, span, far, core], r.ry.at[0, span], y_side),
-                push(g.at[sd, span, far, core], r.ry.at[1, span], y_side),
-            ]
+            over_x, over_y = shared(r.rx.at[:, span]), shared(r.ry.at[:, span])
+            push(g.at[sx, span, near, core], r.rx.at[0, span], x_side, *over_x)
+            push(g.at[sd, span, near, core], r.rx.at[1, span], x_side, *over_x)
+            push(g.at[sy, span, far, core], r.ry.at[0, span], y_side, *over_y)
+            push(g.at[sd, span, far, core], r.ry.at[1, span], y_side, *over_y)
+            plane1[k] = [(over_x[0], r.rx.at[:, span]), (over_y[0], r.ry.at[:, span])]
         else:
-            plane1[k] = [
-                push(g.at[seq_at(i), span, :, core], r.rd.at[i, span], (seq_at(i), t))
-                for i in range(1, S)
-            ]
+            others = r.rd.at[pl.ds(1, S - 1), span]
+            over = shared(others)
+            for i in range(1, S):
+                push(g.at[seq_at(i), span, :, core], r.rd.at[i, span], (seq_at(i), t), *over)
+            plane1[k] = [(over[0], others)]
 
     def add_into(q, n, where, other):
         g[q, n, where, core] = (g[q, n, where, core].astype(F32) + other.astype(F32)).astype(BF16)
@@ -493,8 +613,8 @@
     def turn_plane(k):
         a, b = z.chunks[k]
         span = pl.ds(a, b - a)
-        for copy in plane1[k]:
-            copy.wait_recv()
+        for arrival, place in plane1[k]:
+            arrived(arrival, place)
         if not z.square:
             return
         for n in range(a, b):
@@ -524,20 +644,27 @@
                     sums = sums + r.rd[i, n].astype(F32)
                 g[s, n, :, core] = sums.astype(BF16)
 
+    def sums_of(k):
+        if k == REST:
+            return [(q, z.NF, z.NF + q) for q in range(z.rest)]
+        return [(s, n, n) for n in range(*z.chunks[k])]
+
+    def rows_of(k):
+        return pl.ds(z.NF, z.rest) if k == REST else rounds(k)
+
     def z_start(k):
         if z.line:
             beside[k] = arrivals(1)
             copy = remote(
-                g.at[s, rounds(k), pl.ds(1 - upper, 3), core],
-                r.rz_end.at[rounds(k)],
+                carried(g, k, pl.ds(1 - upper, 3), core),
+                r.rz_end.at[rows_of(k)],
                 at_layer(middle),
                 beside[k],
             )
             push_if(inner == 0, copy)
         else:
             along_back[k] = [
-                push(g.at[s, rounds(k), z_at(i), core], r.rz.at[i, rounds(k)], dev_z(i))
-                for i in steps
+                push(carried(g, k, z_at(i), core), r.rz.at[i, rows_of(k)], dev_z(i)) for i in steps
             ]
 
     def z_over(k):
@@ -545,68 +672,83 @@
             over[k] = arrivals(1)
             pair = pl.ds(2 - 2 * upper, 2)
             copy = remote(
-                g.at[s, rounds(k), pair, core], r.rz_pair.at[rounds(k)], at_layer(3 - layer), over[k]
+                carried(g, k, pair, core), r.rz_pair.at[rows_of(k)], at_layer(3 - layer), over[k]
             )
             sent_if.append((inner == 1, copy))
 
             @pl.when(inner == 1)
             def _():
-                arrived(beside[k], r.rz_end.at[rounds(k)])
-                for n in range(*z.chunks[k]):
-                    add_into(s, n, pair, r.rz_end[n, pl.ds(1 - upper, 2)])
+                arrived(beside[k], r.rz_end.at[rows_of(k)])
+                for q, n, b in sums_of(k):
+                    add_into(q, n, pair, r.rz_end[b, pl.ds(1 - upper, 2)])
                 copy.start()
 
     def z_middle(k):
         if z.line:
             along_back[k] = remote(
-                g.at[s, rounds(k), end, core], r.rz_one.at[rounds(k)], at_layer(end)
+                carried(g, k, end, core), r.rz_one.at[rows_of(k)], at_layer(end)
             )
             sent_if.append((inner == 1, along_back[k]))
 
             @pl.when(inner == 1)
             def _():
-                arrived(over[k], r.rz_pair.at[rounds(k)])
-                for n in range(*z.chunks[k]):
-                    add_into(s, n, pl.ds(2 * upper, 2), r.rz_pair[n])
+                arrived(over[k], r.rz_pair.at[rows_of(k)])
+                for q, n, b in sums_of(k):
+                    add_into(q, n, pl.ds(2 * upper, 2), r.rz_pair[b])
                 along_back[k].start()
-                for n in range(*z.chunks[k]):
-                    sums = g[s, n, layer, core].astype(F32) + r.rz_end[n, 2 * upper].astype(F32)
-                    r.ff_own[n] = sums.astype(BF16)
+                for q, n, b in sums_of(k):
+                    sums = g[q, n, layer, core].astype(F32) + r.rz_end[b, 2 * upper].astype(F32)
+                    r.ff_own[b] = sums.astype(BF16)
 
     def to_all(k):
-        a, b = z.chunks[k]
-        span = pl.ds(a, b - a)
         if z.line:
 
             @pl.when(inner == 0)
             def _():
                 along_back[k].wait_recv()
-                for n in range(a, b):
-                    sums = g[s, n, layer, core].astype(F32) + r.rz_one[n].astype(F32)
-                    r.ff_own[n] = sums.astype(BF16)
+                for q, n, b in sums_of(k):
+                    sums = g[q, n, layer, core].astype(F32) + r.rz_one[b].astype(F32)
+                    r.ff_own[b] = sums.astype(BF16)
         else:
             for copy in along_back[k]:
                 copy.wait_recv()
-            for n in range(a, b):
-                sums = g[s, n, layer, core].astype(F32)
+            for q, n, b in sums_of(k):
+                sums = g[q, n, layer, core].astype(F32)
                 for i in steps:
-                    sums = sums + r.rz[i, n].astype(F32)
-                r.ff_own[n] = sums.astype(BF16)
-        spread_out[k] = [
-            push(r.ff_own.at[span], r.ff.at[s, span], (seq_at(i), t)) for i in range(1, S)
-        ]
-        own_sums.append(move(r.ff_own.at[span], r.ff.at[s, span]))
-
-    def all_here(k):
-        for copy in spread_out[k]:
-            copy.wait_recv()
-
-    for u in range(z.units, S * NR):
+                    sums = sums + r.rz[i, b].astype(F32)
+                r.ff_own[b] = sums.astype(BF16)
+        place = r.ff_own.at[rows_of(k)]
+        for i in range(1, S):
+            if k == REST:
+                push(place, r.others.at[i], (seq_at(i), t), *for_others)
+            else:
+                push(place, r.ff.at[s, rounds(k)], (seq_at(i), t), *spread_out)
+        if k != REST:
+            own_sums.append(move(place, r.ff.at[s, rounds(k)]))
+
+    def rest_end():
+        arrived(for_others[0], some_others)
+        for q in range(z.rest):
+            sums = r.ff_own[z.NF + q].astype(F32)
+            for i in range(1, S):
+                sums = sums + r.others[i, q].astype(F32)
+            r.rest_sum[q] = sums.astype(BF16)
+        own_sums.append(move(r.rest_sum, r.ff.at[pl.ds(0, z.rest), z.NF]))
+
+    if z.rest:
+        some_others = r.others.at[pl.ds(1, S - 1)]
+        for_others = shared(some_others)
+    for u in [] if z.rest else range(z.units, S * NR):
         g[u % S, u // S] = jnp.zeros((Z, 2, Hp, LANES), BF16)
     own = slice(RIM, RIM + N)
     act2_t = act2[own, :].astype(F32).T.astype(BF16)
     grad_units(z.nd + TAPS * z.nh, act2_t, lambda c, w: cote[own, c : c + w], z.nd)
     swap(3)
+    for k in some_rest:
+        swap(k)
+    inner_norm(1, keep_act2, 0, 1, RIM)
+    inner_norm(1, keep_act2, RIM + N, 1, RIM)
+
     edge_r.wait_recv()
     edge_l.wait_recv()
     r.hid[...] = lax.dot_general(cote[...], last_weight(), NT, preferred_element_type=F32)
@@ -646,6 +788,16 @@
     inner_norm_back(1, 0, 1, RIM, keep_dhid2)
     inner_norm_back(1, RIM, N // BLOCK, BLOCK, keep_dhid2, r.acc2)
     inner_norm_back(1, RIM + N, 1, RIM, keep_dhid2)
+
+    to_plane(3)
+    for k in some_rest:
+        add_swapped(k)
+        z_start(k)
+
+    dhid2_t = dhid2[PAD + RIM : PAD + RIM + N, :].T.astype(BF16)
+    grad_units(z.nd, dhid2_t, lambda c, w: taps[own, c : c + w], TAPS * z.nh)
+    swap(2)
+    swap(1)
 
     back = r.back
     for j, offset in enumerate(OFFSETS):
@@ -661,7 +813,7 @@
         total = term if total is None else total + term
     r.hid[RIM : RIM + N, :] = total
 
-    to_plane(3)
+    to_plane(2)
     dhid1 = r.dhid1
 
     def keep_dhid1(row, grad):
@@ -689,43 +841,34 @@
     gi, gi_own = r.gi, r.gi_own
     parts = 4
     part = N // parts
-    per_part = part // BLOCK
-    row_bases, to_core = {}, {}
+    per_part = part // min(part, BLOCK)
+    row_bases = {}
+    core_rows = gi.at[pl.ds(0, Z)]
+    for_rows = shared(core_rows)
 
     def rows_along(qs, js, at_end):
         def onward(j, place):
-            to_core[q, j] = remote(place, place, partner)
-            return [to_core[q, j]]
+            return [remote(place, place, partner, *for_rows)]
 
         for j in js:
             for q in qs:
                 span = pl.ds(q * part, part)
                 place = gi.at[2 * origins[j] + core, span]
-                take(row_bases[q], j, place, onward, at_end, passed_all)
+                take(row_bases[q], j, place, onward, at_end)
 
     def rows_own(q):
         span = pl.ds(q * part, part)
-        copies = [
-            remote(gi_own.at[span], gi.at[t, span], at_layer(to), row_bases[q] + j)
-            for to, j in own_to
-        ]
-        if z.line:
-            sent.append(copies[0])
-            push_if(inner == 1, copies[1])
-            copies[0].start()
-        else:
-            sent.extend(copies)
-            for copy in copies:
-                copy.start()
-
-    own_pair = []
+        return send_own(row_bases[q], gi_own.at[span], gi.at[t, span], q >= 2)
+
+    later = []
     for q in range(parts):
         lax.fori_loop(q * per_part, (q + 1) * per_part, first_norm_back, 0)
         span = pl.ds(q * part, part)
         row_bases[q] = arrivals(Z)
-        rows_own(q)
-        own_pair.append(push(gi_own.at[span], gi.at[t, span], partner))
+        later.append(rows_own(q))
+        push(gi_own.at[span], gi.at[t, span], partner, *for_rows)
     own_row = move(gi_own, gi.at[t])
+    turn_plane(3)
 
     vec = r.vec
     sum0 = jnp.sum(r.acc0[...], axis=0, keepdims=True)
@@ -737,87 +880,92 @@
     for j in range(z.nh):
         vec[z.nd + j : z.nd + j + 1, :] = sum1[:, j * LANES : (j + 1) * LANES]
         vec[z.nd + z.nh + j : z.nd + z.nh + j + 1, :] = sum2[:, j * LANES : (j + 1) * LANES]
-    vec_plane = [push(vec, r.vec_plane.at[i], (seq_at(i), t)) for i in range(1, S)]
-
-    dhid2_t = dhid2[PAD + RIM : PAD + RIM + N, :].T.astype(BF16)
-    grad_units(z.nd, dhid2_t, lambda c, w: taps[own, c : c + w], TAPS * z.nh)
-    swap(2)
-    swap(1)
+    vec_plane = shared(r.vec_plane.at[pl.ds(1, S - 1)])
+    for i in range(1, S):
+        push(vec, r.vec_plane.at[i], (seq_at(i), t), *vec_plane)
+
     dhid1_t = dhid1[...].astype(F32).T.astype(BF16)
     grad_units(0, dhid1_t, lambda c, w: r.act0[own, c : c + w], z.nd)
     swap(0)
-    to_plane(2)
-    turn_plane(3)
     to_plane(1)
-    rows_along([0], [1, 2], False)
-    rows_along([1], [1, 2], False)
     turn_plane(2)
     to_plane(0)
     to_z(3)
     z_start(3)
-    rows_along([2], [1, 2], False)
+    later[2]()
+    rows_along([0, 1], [1], False)
+    for k in some_rest:
+        z_over(k)
+    z_over(3)
     turn_plane(1)
-    rows_along([3], [1, 2], False)
-
-    for copy in vec_plane:
-        copy.wait_recv()
+    to_z(2)
+    z_start(2)
+    later[3]()
+    rows_along([0], [2], False)
+    rows_along([2], [1], False)
+    rows_along([1], [2], False)
+
+    arrived(vec_plane[0], r.vec_plane.at[pl.ds(1, S - 1)])
     vec_sum = r.vec_sum
     vec_sum[...] = sum((r.vec_plane[i] for i in range(1, S)), vec[...])
-    vec_z = [push(vec_sum, r.vec_z.at[i - 1], dev_z(i)) for i in range(1, Z)]
-
-    z_over(3)
-    to_z(2)
-    z_start(2)
-    rows_along([0], [3], False)
-    rows_along([0, 1, 2, 3], [1], True)
+    vec_z = shared(r.vec_z.at[pl.ds(0, Z - 1)])
+    for i in range(1, Z):
+        push(vec_sum, r.vec_z.at[i - 1], dev_z(i), *vec_z)
+
     turn_plane(0)
-    rows_along([1], [3], False)
+    z_over(2)
+    rows_along([2], [2], False)
+    for k in some_rest:
+        z_middle(k)
     z_middle(3)
-    z_over(2)
+    rows_along([3], [1], False)
     to_z(1)
     z_start(1)
-    rows_along([2], [3], False)
+    rows_along([0], [3], False)
     to_z(0)
     z_start(0)
+    z_over(1)
     z_middle(2)
-    z_over(1)
+    rows_along([1], [3], False)
+    for k in some_rest:
+        to_all(k)
+    to_all(3)
+    z_over(0)
+    rows_along([3], [2], False)
+    z_middle(1)
+    rows_along([2], [3], False)
+    rows_along([0, 1, 2, 3], [1], True)
+    rows_along([0, 1], [2], True)
+    z_middle(0)
+    to_all(2)
+    to_all(1)
+    to_all(0)
     rows_along([3], [3], False)
-    to_all(3)
-    rows_along([0, 1], [2], True)
-    z_over(0)
-    z_middle(1)
-    to_all(2)
     rows_along([2, 3], [2], True)
-    z_middle(0)
-    to_all(1)
-    rows_along([0], range(3, Z), True)
-    to_all(0)
-    rows_along([1], range(3, Z), True)
-
-    for copy in vec_z:
-        copy.wait_recv()
+    rows_along([0, 1], range(3, Z), True)
+
+    arrived(vec_z[0], r.vec_z.at[pl.ds(0, Z - 1)])
     vec_half = r.vec_half
     vec_half[...] = sum((r.vec_z[i - 1] for i in range(1, Z)), vec_sum[...])
     vec_core = push(vec_half, r.gain_sums.at[1], partner)
     own_sums.append(move(vec_half, r.gain_sums.at[0]))
     rows_along([2, 3], range(3, Z), True)
-    for k in reversed(range(STAGES)):
-        all_here(k)
+    arrived(spread_out[0], some_sums)
 
     vec_core.wait_recv()
+    if z.rest:
+        rest_end()
     for copy in own_sums:
         copy.wait()
     out_own.wait()
-    for copy in out_copies:
-        copy.wait_recv()
+    arrived(for_out[0], some_out)
     own_row.wait()
-    for copy in own_pair:
-        copy.wait_recv()
-    for copy in to_core.values():
-        copy.wait_recv()
+    arrived(for_rows[0], core_rows)
     assert all(n <= sems.shape[0] for n, sems in zip(counts, (send, recv, local)))
     for copy in sent:
         copy.wait_send()
+    for sends, place in together:
+        remote(place, place, partner, 0, sends).wait_send()
     for when, copy in sent_if:
 
         @pl.when(when)
@@ -837,9 +985,8 @@
         copy.start()
         copies.append(copy)
 
-    half = z.R // 2
-    for i in range(2):
-        move(gi_got.at[pl.ds(i * half, half)], gi.at[pl.ds(i * half, half)])
+    for i in range(z.R):
+        move(gi_got.at[i], gi.at[i])
     move(got, out)
 
     def summed(start, count):
@@ -911,11 +1058,12 @@
         ff=((S, NR, Hp, LANES), BF16),
         gain_sums=((2, 24, LANES), F32),
     )
+    NB = z.NF + z.rest
     near = vm if z.line else jax.ShapeDtypeStruct
     scratch = dict(
-        send=pltpu.SemaphoreType.DMA((226 if z.line else 800,)),
-        recv=pltpu.SemaphoreType.DMA((222 if z.line else 800,)),
-        local=pltpu.SemaphoreType.DMA((13,)),
+        send=pltpu.SemaphoreType.DMA((105 if z.line else 800,)),
+        recv=pltpu.SemaphoreType.DMA((128 if z.line else 800,)),
+        local=pltpu.SemaphoreType.DMA((14,)),
         xe=vm((E, D), BF16),
         cote=vm((E, D), BF16),
         act0=vm((E, D), BF16),
@@ -954,7 +1102,7 @@
         gl=vm((8, LANES), F32),
         g=vm((S, NR, Z, 2, Hp, LANES), BF16),
         rc=vm((S, NR, Z, Hp, LANES), BF16),
-        ff_own=vm((NR, Hp, LANES), BF16),
+        ff_own=vm((NB, Hp, LANES), BF16),
         vec=vm((24, LANES), F32),
         vec_sum=vm((24, LANES), F32),
         vec_plane=vm((S, 24, LANES), F32),
@@ -962,10 +1110,13 @@
         vec_half=vm((24, LANES), F32),
     )
     if z.line:
-        scratch.update(rz_end=vm((NR, 3, Hp, LANES), BF16))
-        scratch.update(rz_pair=vm((NR, 2, Hp, LANES), BF16), rz_one=vm((NR, Hp, LANES), BF16))
+        scratch.update(rz_end=vm((NB, 3, Hp, LANES), BF16))
+        scratch.update(rz_pair=vm((NB, 2, Hp, LANES), BF16), rz_one=vm((NB, Hp, LANES), BF16))
+    if z.rest:
+        scratch.update(others=vm((S, z.rest, Hp, LANES), BF16))
+        scratch.update(rest_sum=vm((z.rest, Hp, LANES), BF16))
     else:
-        scratch.update(rz=vm((Z, NR, Hp, LANES), BF16))
+        scratch.update(rz=vm((Z, NB, Hp, LANES), BF16))
     if z.square:
         scratch.update(rx=vm((2, NR, Z // 2, Hp, LANES), BF16))
         scratch.update(ry=vm((2, NR, Z // 2, Hp, LANES), BF16))
@@ -1006,7 +1157,7 @@
             vm((TAPS, Hp, HP), F32),
             vm((Hp, D), F32),
             vm((8, LANES), F32),
-            pltpu.SemaphoreType.DMA((6,)),
+            pltpu.SemaphoreType.DMA((z.R + 4,)),
         ],
         compiler_params=pltpu.CompilerParams(vmem_limit_bytes=12 * 2**20),
     )(*results)

time: 118 us -> 110 us (0.932)
  Pallas kernels: 117 us -> 109 us
    pallas_call x1, Pallas kernels: 113 us -> 105 us  [shards(): pl.pallas_call(functools.partial(kernel, z, names), out_shape=[near(shape...]
where the time goes in v3:
time: 110 us
  Pallas kernels  109 us (99%)
    pallas_call x1, Pallas kernels, shards(): pl.pallas_call(functools.partial(kernel, z, names), out_shape=[near(shape...  105 us
    pallas_call x1, Pallas kernels, shards(): pl.pallas_call(functools.partial(finish, z), out_shape=[shape((z.R, z.Dt,...  3.76 us

profile of v3, /device:TPU:0, one launch (start us, length us, event | category | flops | bytes accessed | tf_op | source)
XLA Modules:
  0.0 110.0 jit_solution(6940306096352249081)
XLA Ops:
  0.6 105.5 %shard_map.152 = (bf16[8,160,256]{2,1,0:T(8,128)(2,1)S(1)}, bf16[8,256,1280]{2,1,0:T(8,128)(2,1)S(1)}, bf16[4,12,80,128]{3,2,1,0:T(8,128)(2,1)S(1)}, f32[2,24,128]{2,1,0:T(8,128)S(1)}) custom-call(bf16[8,256,1280]{2,1,0:T(8,128)(2,1)} %refs_0_.1, s32[8,256]{1,0:T(8,128)} %refs_1_.1, bf16[80,1280]{1,0:T(8,128)(2,1)} %bitcast.14, ...), custom_call_target="tpu_custom_call" | custom-call | tf_op jit(solution)/shard_map/pallas_call | solution.py:1128
  106.1 3.8 %shard_map.153 = (bf16[8,160,256]{2,1,0:T(8,128)(2,1)}, bf16[8,256,1280]{2,1,0:T(8,128)(2,1)}, f32[80,1280]{1,0:T(8,128)}, f32[5,80,640]{2,1,0:T(8,128)}, f32[80...) custom-call(bf16[8,160,256]{2,1,0:T(8,128)(2,1)S(1)} %get-tuple-element.20.refs_0_, ...), custom_call_target="tpu_custom_call" | custom-call | tf_op jit(solution)/shard_map/pallas_call | solution.py:1141

commit v4 on v3

--- a/solution.py
+++ b/solution.py
@@ -20,7 +20,7 @@
 RIM = 16
 PAD = 8
 STAGES = 4
-REST = STAGES
+REST, FULL = STAGES, STAGES + 1
 BLOCK = 64
 HALF_ROOT = 0.7071067811865476
 PEAK = 0.3989422804014327
@@ -53,6 +53,10 @@
         self.chunks = [(0, one), (one, (one + two) // 2), ((one + two) // 2, two), (two, self.NF)]
         self.Dt = cotangent.shape[2]
         assert self.Dt % 16 == 0
+        self.full = self.NF - 1 if self.rest and self.NF - 1 > two else None
+        self.ahead = list(self.chunks)
+        if self.full is not None:
+            self.ahead[3] = (two, self.full)
         self.square = self.S == 4
         self.line = self.Z == 4
 
@@ -76,7 +80,7 @@
 
     send, recv, local = r.send, r.recv, r.local
     counts = [0, 0, 0]
-    sent, sent_if, together = [], [], []
+    sent, sent_if, together, together_if = [], [], [], []
 
     def remote(src, dst, device, arrival=None, sends=None):
         return pltpu.make_async_remote_copy(
@@ -158,10 +162,9 @@
             go()
 
     def send_own(base, src, place, later=False):
-        copies = [remote(src, place, at_layer(to), base + j) for to, j in own_to]
+        copies = [remote(src, place, at_layer(to), base + j - 1, streams[base]) for to, j in own_to]
         if z.line:
-            push_if(inner == 1, copies.pop())
-        sent.extend(copies)
+            pl.when(inner == 1)(copies.pop().start)
         later = later and z.line
         for copy in copies:
             if later:
@@ -175,13 +178,12 @@
             extra = None
             if j in passed:
                 to, then = passed[j]
-                extra = remote(place, place, at_layer(to), base + then)
-                sent_if.append((inner == 1, extra))
+                extra = remote(place, place, at_layer(to), base + then - 1, streams[base])
             onwards[base + j] = (extra, onward(j, place))
 
         def go():
             extra, copies = onwards[base + j]
-            arrived(base + j, place)
+            arrived(base + j - 1, place)
             if extra is not None and not at_end:
                 extra.start()
             if start:
@@ -190,7 +192,18 @@
 
         only(at_end, go)
 
-    onwards = {}
+    onwards, streams = {}, {}
+
+    def stream(one, most):
+        base = arrivals(Z - 1)
+        streams[base] = sendings()
+        if z.line:
+            together_if.append((inner == 0, streams[base], one))
+            together_if.append((inner == 1, streams[base], most))
+        else:
+            together.append((streams[base], most))
+        return base
+
     right, left = (seq_at(1), t), (seq_at(-1), t)
     if z.square:
         sx, sy, sd = s ^ 1, s ^ 2, s ^ 3
@@ -225,7 +238,7 @@
     gain_own = move(r.gl, r.gslots.at[t])
 
     wg = r.wg
-    bases, plane = {}, {}
+    bases, plane, corner = {}, {}, {}
     plane_x, plane_y, plane_d, plane_any, across = {}, {}, {}, {}, {}
 
     def unit_in(u):
@@ -239,17 +252,21 @@
             return r.w3_in[:, u * LANES : (u + 1) * LANES]
         return jnp.zeros((Hp, LANES), BF16)
 
+    cuts = list(z.ahead)
+
     def rounds(k):
-        a, b = z.chunks[k]
+        a, b = cuts[k]
         return pl.ds(a, b - a)
 
     def carried(ref, k, which, c):
         if k == REST:
             return ref.at[pl.ds(0, z.rest), z.NF, which, c]
+        if k == FULL:
+            return ref.at[:, z.full, which, c]
         return ref.at[s, rounds(k), which, c]
 
     def every(ref, k, which, c):
-        return carried(ref, k, which, c) if k == REST else ref.at[:, rounds(k), which, c]
+        return carried(ref, k, which, c) if k >= REST else ref.at[:, rounds(k), which, c]
 
     every_chip = pl.ds(0, Z)
 
@@ -257,17 +274,25 @@
         if k == REST:
             for q in range(z.rest):
                 wg[q, z.NF, layer, core] = unit_in(z.NF * S + q)
+        elif k == FULL:
+            for q in range(S):
+                wg[q, z.full, layer, core] = unit_in(z.full * S + q)
         else:
             for q in range(S):
-                for n in range(*z.chunks[k]):
+                for n in range(*cuts[k]):
                     wg[q, n, layer, core] = unit_in(n * S + q)
         place = carried(wg, k, layer, core)
-        bases[k] = arrivals(Z)
+        count = place.shape[0]
+        if z.line:
+            most = wg.at[pl.ds(0, count), pl.ds(0, Z + 1), 0, 0]
+        else:
+            most = wg.at[0, pl.ds(0, count), pl.ds(0, Z - 1), 0]
+        bases[k] = stream(place, most)
         send_own(bases[k], place, place)
         across[k] = shared(every(wg, k, every_chip, core))
         place = every(wg, k, layer, core)
         push(place, place, partner, *across[k])
-        if k != REST:
+        if k < REST:
             copies = S if z.square else S - 1
             plane[k] = sendings()
             together.append(
@@ -276,7 +301,7 @@
 
     def weights_along(k, at_end, js=steps, start=True):
         def onward(j, place):
-            if k == REST:
+            if k >= REST:
                 return [remote(place, place, partner, *across[k])]
             if not z.square:
                 plane_any[k, j] = [
@@ -301,12 +326,14 @@
     def weights_corner(k, at_end):
         if not z.square:
             return
+        if k not in corner:
+            corner[k] = arrivals(1)
         for j in steps:
             if (k, j) not in plane_d:
                 over_y = (k + j) % 2
                 place = wg.at[sx if over_y else sy, rounds(k), origins[j], core]
                 side = y_side if over_y else x_side
-                plane_d[k, j] = remote(place, place, side, None, plane[k])
+                plane_d[k, j] = remote(place, place, side, corner[k], plane[k])
 
         def go():
             for j in steps:
@@ -319,15 +346,14 @@
 
         only(at_end, go)
 
-    def weights_across(k, js=steps):
-        for j in js:
-            if z.square:
-                plane_d[k, j].wait_recv()
-                place = wg.at[sd, rounds(k), origins[j], core]
-            else:
+    def weights_across(k):
+        if z.square:
+            arrived(corner[k], wg.at[0, rounds(k), pl.ds(0, Z - 1), core])
+        for j in steps:
+            place = wg.at[sd if z.square else pl.ds(0, S), rounds(k), origins[j], core]
+            if not z.square:
                 for copy in plane_any[k, j]:
                     copy.wait_recv()
-                place = wg.at[:, rounds(k), origins[j], core]
             push(place, place, partner, *across[k])
 
     def weights_ready(k):
@@ -336,11 +362,18 @@
     some_cot = cot_t.at[pl.ds(0, (T - 1) * z.Dt)]
     for_cot = shared(some_cot)
 
-    def cotangent_out(at_end):
+    def cotangent_out(at_end, to_end):
         def go():
             for i in range(1, T):
                 to = lax.rem(t + i, T)
-                push(cot.at[to], cot_t.at[features(t)], (s, to), *for_cot)
+
+                def one():
+                    push(cot.at[to], cot_t.at[features(t)], (s, to), *for_cot)
+
+                if z.line:
+                    pl.when(lax.rem((to // 2 + 1) // 2, 2) == 1 - to_end)(one)
+                elif to_end:
+                    one()
 
         only(at_end, go)
 
@@ -352,8 +385,7 @@
     weights_own(2)
     weights_own(3)
     some_rest = [REST] if z.rest else []
-    for k in some_rest:
-        weights_own(k)
+    by_all = some_rest if z.full is None else [FULL, REST]
     def unit(ref, u):
         return ref[u % S, u // S].reshape(HP, LANES)
 
@@ -394,9 +426,8 @@
     for k in range(STAGES):
         weights_along(k, False, steps[:2], k < 2)
         weights_along(k, True, steps[:1])
-    for k in some_rest:
-        weights_along(k, False, steps[:2])
-        weights_along(k, True, steps[:1])
+    for k in by_all:
+        weights_own(k)
     rim_r.wait_recv()
     rim_l.wait_recv()
     first_norm(0, 1, RIM)
@@ -430,34 +461,34 @@
     weights_along(0, False, third)
     weights_along(0, True, [2])
     weights_along(1, False, third)
+    cotangent_out(False, False)
     weights_along(1, True, [2])
     weights_along(2, False, third, False)
     weights_along(2, True, [2])
     weights_along(3, False, third, False)
-    for k in some_rest:
-        weights_along(k, False, third)
     weights_corner(0, False)
     weights_spread(2)
     weights_along(0, True, third)
+    cotangent_out(True, False)
     weights_along(1, True, third)
     weights_along(3, True, [2])
     weights_along(2, True, third)
-    cotangent_out(True)
     weights_corner(0, True)
     weights_corner(1, False)
     weights_along(3, True, third)
-    for k in some_rest:
-        weights_along(k, True, steps[1:])
     weights_corner(1, True)
     weights_spread(3)
-    weights_across(0, steps[:1])
-    cotangent_out(False)
-    weights_across(0, steps[1:])
+    weights_corner(2, True)
+    cotangent_out(True, True)
+    for k in by_all:
+        weights_along(k, False, steps[:2])
+    weights_across(0)
+    cotangent_out(False, True)
 
     weights_ready(0)
     r.hid[...] = lax.dot_general(r.act0[...], first_weight(), NT, preferred_element_type=F32)
     weights_corner(2, False)
-    weights_corner(2, True)
+    weights_corner(3, True)
     weights_across(1)
 
     def inner_norm(which, act_store, first, count, size):
@@ -504,23 +535,37 @@
             taps[:, k * HP : (k + 1) * HP], tap_weight(k), NT, preferred_element_type=F32
         )
 
+    cote = r.cote
+    edge_r = remote(cote.at[pl.ds(N, RIM)], cote.at[pl.ds(0, RIM)], right)
+    edge_l = remote(cote.at[pl.ds(RIM, RIM)], cote.at[pl.ds(RIM + N, RIM)], left)
+    sent.extend([edge_r, edge_l])
+
+    def cotangent_in(at_end):
+        def go():
+            cot_own.wait()
+            arrived(for_cot[0], some_cot)
+            cote[RIM : RIM + N, :] = cot_t[...].T
+            edge_r.start()
+            edge_l.start()
+
+        only(at_end, go)
+
+    cotangent_in(False)
     weights_ready(1)
     total = tap_term(0) + tap_term(1)
     weights_corner(3, False)
-    weights_corner(3, True)
+    for k in by_all:
+        weights_along(k, False, third)
     weights_across(2)
     weights_ready(2)
     for k in range(2, TAPS):
         total = total + tap_term(k)
     r.hid[...] = total
+    for k in by_all:
+        weights_along(k, True)
     weights_across(3)
 
-    cot_own.wait()
-    arrived(for_cot[0], some_cot)
-    cote = r.cote
-    cote[RIM : RIM + N, :] = cot_t[...].T
-    edge_r = push(cote.at[pl.ds(N, RIM)], cote.at[pl.ds(0, RIM)], right)
-    edge_l = push(cote.at[pl.ds(RIM, RIM)], cote.at[pl.ds(RIM + N, RIM)], left)
+    cotangent_in(True)
 
     act2 = r.act2
 
@@ -529,7 +574,7 @@
 
     inner_norm(1, keep_act2, RIM, N // BLOCK, BLOCK)
 
-    for k in [3, *some_rest]:
+    for k in [3, *by_all]:
         weights_ready(k)
     big, out_t = r.big, r.out_t
     some_out = r.out.at[pl.ds(0, T - 1)]
@@ -556,6 +601,8 @@
 
     out_own = move(out_t.at[features(t)], r.out.at[t])
 
+    cuts[:] = z.chunks
+
     g = r.g
 
     def grad_units(first, lhs, rhs, count):
@@ -569,49 +616,60 @@
                 g[u % S, u // S] = block[:, i * LANES : (i + 1) * LANES].reshape(Z, 2, Hp, LANES)
 
     rc = r.rc
-    swaps, plane1, plane2, along_back = {}, {}, {}, {}
+    swaps, plane1, plane2, along_back, first_copies = {}, {}, {}, {}, {}
     some_sums = r.ff.at[pl.ds(0, S - 1), pl.ds(0, z.NF)]
     spread_out = shared(some_sums)
     beside, over, own_sums = {}, {}, []
 
-    def swap(k):
+    for k in [3, *some_rest, 2, 1, 0]:
         place = every(g, k, every_chip, 1 - core)
         to = rc.at[pl.ds(0, z.rest), z.NF] if k == REST else rc.at[:, rounds(k)]
-        swaps[k] = push(place, to, partner)
+        swaps[k] = remote(place, to, partner)
+        sent.append(swaps[k])
 
     def add_swapped(k):
         swaps[k].wait_recv()
         at_ = [(q, z.NF) for q in range(z.rest)]
         if k != REST:
-            at_ = [(q, n) for q in range(S) for n in range(*z.chunks[k])]
+            at_ = [(q, n) for q in range(S) for n in range(*cuts[k])]
         for q, n in at_:
             g[q, n, :, core] = (g[q, n, :, core].astype(F32) + rc[q, n].astype(F32)).astype(BF16)
 
     near, far = pl.ds(0, Z // 2), pl.ds(Z // 2, Z // 2)
 
-    def to_plane(k):
-        a, b = z.chunks[k]
-        span = pl.ds(a, b - a)
-        add_swapped(k)
-        if z.square:
-            over_x, over_y = shared(r.rx.at[:, span]), shared(r.ry.at[:, span])
-            push(g.at[sx, span, near, core], r.rx.at[0, span], x_side, *over_x)
-            push(g.at[sd, span, near, core], r.rx.at[1, span], x_side, *over_x)
-            push(g.at[sy, span, far, core], r.ry.at[0, span], y_side, *over_y)
-            push(g.at[sd, span, far, core], r.ry.at[1, span], y_side, *over_y)
-            plane1[k] = [(over_x[0], r.rx.at[:, span]), (over_y[0], r.ry.at[:, span])]
-        else:
-            others = r.rd.at[pl.ds(1, S - 1), span]
-            over = shared(others)
-            for i in range(1, S):
-                push(g.at[seq_at(i), span, :, core], r.rd.at[i, span], (seq_at(i), t), *over)
-            plane1[k] = [(over[0], others)]
+    def to_plane(k, at_end=None):
+        span = rounds(k)
+        if k not in plane1:
+            if z.square:
+                over_x, over_y = shared(r.rx.at[:, span]), shared(r.ry.at[:, span])
+                plane1[k] = [(over_x[0], r.rx.at[:, span]), (over_y[0], r.ry.at[:, span])]
+                first_copies[k] = [
+                    remote(g.at[sx, span, near, core], r.rx.at[0, span], x_side, *over_x),
+                    remote(g.at[sd, span, near, core], r.rx.at[1, span], x_side, *over_x),
+                    remote(g.at[sy, span, far, core], r.ry.at[0, span], y_side, *over_y),
+                    remote(g.at[sd, span, far, core], r.ry.at[1, span], y_side, *over_y),
+                ]
+            else:
+                others = r.rd.at[pl.ds(1, S - 1), span]
+                over = shared(others)
+                plane1[k] = [(over[0], others)]
+                first_copies[k] = [
+                    remote(g.at[seq_at(i), span, :, core], r.rd.at[i, span], (seq_at(i), t), *over)
+                    for i in range(1, S)
+                ]
+
+        def go():
+            add_swapped(k)
+            for copy in first_copies[k]:
+                copy.start()
+
+        go() if at_end is None else only(at_end, go)
 
     def add_into(q, n, where, other):
         g[q, n, where, core] = (g[q, n, where, core].astype(F32) + other.astype(F32)).astype(BF16)
 
     def turn_plane(k):
-        a, b = z.chunks[k]
+        a, b = cuts[k]
         span = pl.ds(a, b - a)
         for arrival, place in plane1[k]:
             arrived(arrival, place)
@@ -629,7 +687,7 @@
             add_into(s, n, far, r.ry[0, n])
 
     def to_z(k):
-        a, b = z.chunks[k]
+        a, b = cuts[k]
         span = pl.ds(a, b - a)
         if z.square:
             for copy in plane2[k]:
@@ -647,7 +705,7 @@
     def sums_of(k):
         if k == REST:
             return [(q, z.NF, z.NF + q) for q in range(z.rest)]
-        return [(s, n, n) for n in range(*z.chunks[k])]
+        return [(s, n, n) for n in range(*cuts[k])]
 
     def rows_of(k):
         return pl.ds(z.NF, z.rest) if k == REST else rounds(k)
@@ -741,11 +799,30 @@
     for u in [] if z.rest else range(z.units, S * NR):
         g[u % S, u // S] = jnp.zeros((Z, 2, Hp, LANES), BF16)
     own = slice(RIM, RIM + N)
-    act2_t = act2[own, :].astype(F32).T.astype(BF16)
-    grad_units(z.nd + TAPS * z.nh, act2_t, lambda c, w: cote[own, c : c + w], z.nd)
-    swap(3)
-    for k in some_rest:
-        swap(k)
+
+    def last_gradients(at_end):
+        def go():
+            act2_t = act2[own, :].astype(F32).T.astype(BF16)
+            grad_units(z.nd + TAPS * z.nh, act2_t, lambda c, w: cote[own, c : c + w], z.nd)
+            for k in [3, *some_rest]:
+                swaps[k].start()
+
+        only(at_end, go)
+
+    def conv_gradients(at_end):
+        def go():
+            dhid2_t = dhid2[PAD + RIM : PAD + RIM + N, :].T.astype(BF16)
+            grad_units(z.nd, dhid2_t, lambda c, w: taps[own, c : c + w], TAPS * z.nh)
+            for k in (2, 1):
+                swaps[k].start()
+
+        only(at_end, go)
+
+    def add_rest(at_end):
+        for k in some_rest:
+            only(at_end, functools.partial(add_swapped, k))
+
+    last_gradients(True)
     inner_norm(1, keep_act2, 0, 1, RIM)
     inner_norm(1, keep_act2, RIM + N, 1, RIM)
 
@@ -789,15 +866,11 @@
     inner_norm_back(1, RIM, N // BLOCK, BLOCK, keep_dhid2, r.acc2)
     inner_norm_back(1, RIM + N, 1, RIM, keep_dhid2)
 
-    to_plane(3)
+    to_plane(3, True)
+    add_rest(True)
     for k in some_rest:
-        add_swapped(k)
         z_start(k)
-
-    dhid2_t = dhid2[PAD + RIM : PAD + RIM + N, :].T.astype(BF16)
-    grad_units(z.nd, dhid2_t, lambda c, w: taps[own, c : c + w], TAPS * z.nh)
-    swap(2)
-    swap(1)
+    conv_gradients(True)
 
     back = r.back
     for j, offset in enumerate(OFFSETS):
@@ -813,7 +886,7 @@
         total = term if total is None else total + term
     r.hid[RIM : RIM + N, :] = total
 
-    to_plane(2)
+    to_plane(2, True)
     dhid1 = r.dhid1
 
     def keep_dhid1(row, grad):
@@ -823,25 +896,26 @@
 
     big[...] = jnp.dot(dhid1[...], first_weight(), preferred_element_type=F32)
 
-    def first_norm_back(i, carry):
-        row = pl.multiple_of(i * BLOCK, BLOCK)
-        wide = pl.multiple_of(row + RIM, 16)
-        scale = cells(r.scale0, wide, BLOCK)
-        xhat = (cells(xe, wide, BLOCK).astype(F32) - cells(r.mean0, wide, BLOCK)) * scale
-        dpre = cells(big, row, BLOCK) * cells(r.slope0, wide, BLOCK)
+    def first_norm_back(row, size):
+        wide = row + RIM
+        scale = cells(r.scale0, wide, size)
+        xhat = (cells(xe, wide, size).astype(F32) - cells(r.mean0, wide, size)) * scale
+        dpre = cells(big, row, size) * cells(r.slope0, wide, size)
         dgain = dpre * xhat
-        r.acc0[...] += sum(dgain[n : n + 8] for n in range(0, BLOCK, 8))
+        r.acc0[...] += sum(dgain[n : n + 8] for n in range(0, size, 8))
         dx = dpre * gain0
         plain = jnp.sum(dx, axis=1, keepdims=True) / D
         cross = jnp.sum(dx * xhat, axis=1, keepdims=True) / D
         grad = scale * (dx - plain - xhat * cross)
-        r.gi_own[pl.ds(row, BLOCK), :] = (cells(cote, wide, BLOCK).astype(F32) + grad).astype(BF16)
-        return carry
+        r.gi_own[pl.ds(row, size), :] = (cells(cote, wide, size).astype(F32) + grad).astype(BF16)
 
     gi, gi_own = r.gi, r.gi_own
-    parts = 4
-    part = N // parts
-    per_part = part // min(part, BLOCK)
+    marks = [0, N // 4, N // 2, 3 * N // 4, 7 * N // 8, N]
+    parts = len(marks) - 1
+
+    def part_span(q):
+        return pl.ds(marks[q], marks[q + 1] - marks[q])
+
     row_bases = {}
     core_rows = gi.at[pl.ds(0, Z)]
     for_rows = shared(core_rows)
@@ -852,23 +926,25 @@
 
         for j in js:
             for q in qs:
-                span = pl.ds(q * part, part)
+                span = part_span(q)
                 place = gi.at[2 * origins[j] + core, span]
                 take(row_bases[q], j, place, onward, at_end)
 
     def rows_own(q):
-        span = pl.ds(q * part, part)
+        span = part_span(q)
         return send_own(row_bases[q], gi_own.at[span], gi.at[t, span], q >= 2)
 
     later = []
     for q in range(parts):
-        lax.fori_loop(q * per_part, (q + 1) * per_part, first_norm_back, 0)
-        span = pl.ds(q * part, part)
-        row_bases[q] = arrivals(Z)
+        first_norm_back(marks[q], marks[q + 1] - marks[q])
+        span = part_span(q)
+        some = gi.at[pl.ds(0, Z + 1 if z.line else Z - 1), span]
+        row_bases[q] = stream(gi_own.at[span], some)
         later.append(rows_own(q))
         push(gi_own.at[span], gi.at[t, span], partner, *for_rows)
     own_row = move(gi_own, gi.at[t])
-    turn_plane(3)
+    last_gradients(False)
+    conv_gradients(False)
 
     vec = r.vec
     sum0 = jnp.sum(r.acc0[...], axis=0, keepdims=True)
@@ -886,7 +962,11 @@
 
     dhid1_t = dhid1[...].astype(F32).T.astype(BF16)
     grad_units(0, dhid1_t, lambda c, w: r.act0[own, c : c + w], z.nd)
-    swap(0)
+    swaps[0].start()
+    to_plane(3, False)
+    add_rest(False)
+    to_plane(2, False)
+    turn_plane(3)
     to_plane(1)
     turn_plane(2)
     to_plane(0)
@@ -901,6 +981,7 @@
     to_z(2)
     z_start(2)
     later[3]()
+    later[4]()
     rows_along([0], [2], False)
     rows_along([2], [1], False)
     rows_along([1], [2], False)
@@ -913,35 +994,36 @@
         push(vec_sum, r.vec_z.at[i - 1], dev_z(i), *vec_z)
 
     turn_plane(0)
+    rows_along([3], [1], False)
     z_over(2)
     rows_along([2], [2], False)
     for k in some_rest:
         z_middle(k)
     z_middle(3)
-    rows_along([3], [1], False)
+    rows_along([4], [1], False)
     to_z(1)
     z_start(1)
     rows_along([0], [3], False)
     to_z(0)
     z_start(0)
+    rows_along([1], [3], False)
     z_over(1)
     z_middle(2)
-    rows_along([1], [3], False)
+    z_over(0)
+    rows_along([3, 4], [2], False)
     for k in some_rest:
         to_all(k)
     to_all(3)
-    z_over(0)
-    rows_along([3], [2], False)
+    rows_along([2], [3], False)
     z_middle(1)
-    rows_along([2], [3], False)
-    rows_along([0, 1, 2, 3], [1], True)
+    rows_along([0, 1, 2, 3, 4], [1], True)
     rows_along([0, 1], [2], True)
     z_middle(0)
     to_all(2)
     to_all(1)
     to_all(0)
-    rows_along([3], [3], False)
-    rows_along([2, 3], [2], True)
+    rows_along([3, 4], [3], False)
+    rows_along([2, 3, 4], [2], True)
     rows_along([0, 1], range(3, Z), True)
 
     arrived(vec_z[0], r.vec_z.at[pl.ds(0, Z - 1)])
@@ -949,7 +1031,7 @@
     vec_half[...] = sum((r.vec_z[i - 1] for i in range(1, Z)), vec_sum[...])
     vec_core = push(vec_half, r.gain_sums.at[1], partner)
     own_sums.append(move(vec_half, r.gain_sums.at[0]))
-    rows_along([2, 3], range(3, Z), True)
+    rows_along([2, 3, 4], range(3, Z), True)
     arrived(spread_out[0], some_sums)
 
     vec_core.wait_recv()
@@ -966,6 +1048,8 @@
         copy.wait_send()
     for sends, place in together:
         remote(place, place, partner, 0, sends).wait_send()
+    for when, sends, place in together_if:
+        pl.when(when)(remote(place, place, partner, 0, sends).wait_send)
     for when, copy in sent_if:
 
         @pl.when(when)
@@ -976,7 +1060,7 @@
 def finish(z, *refs):
     got, gi_got, ff, gain_sums = refs[:4]
     out, gi, grad_first, grad_conv, grad_last, grad_gain, grad_gain1, grad_gain2, *refs = refs[4:]
-    first, conv, last, gains, sems = refs
+    first, conv, last, gain, gain1, gain2, sems = refs
     t = lax.axis_index("tp")
     copies = []
 
@@ -1011,9 +1095,12 @@
             jnp.where(t == j, row[:, j * step : j * step + width], 0.0) for j in range(z.T)
         )
 
-    grad_gain[...] = picked(line(0, z.nd), z.Dt, z.Dt)
-    grad_gain1[...] = picked(line(z.nd, z.nh), z.Hs, z.Hp)
-    grad_gain2[...] = picked(line(z.nd + z.nh, z.nh), z.Hs, z.Hp)
+    gain[...] = picked(line(0, z.nd), z.Dt, z.Dt)
+    move(gain, grad_gain)
+    gain1[...] = picked(line(z.nd, z.nh), z.Hs, z.Hp)
+    move(gain1, grad_gain1)
+    gain2[...] = picked(line(z.nd + z.nh, z.nh), z.Hs, z.Hp)
+    move(gain2, grad_gain2)
     for copy in copies:
         copy.wait()
 
@@ -1061,8 +1148,8 @@
     NB = z.NF + z.rest
     near = vm if z.line else jax.ShapeDtypeStruct
     scratch = dict(
-        send=pltpu.SemaphoreType.DMA((105 if z.line else 800,)),
-        recv=pltpu.SemaphoreType.DMA((128 if z.line else 800,)),
+        send=pltpu.SemaphoreType.DMA((72 if z.line else 800,)),
+        recv=pltpu.SemaphoreType.DMA((118 if z.line else 800,)),
         local=pltpu.SemaphoreType.DMA((14,)),
         xe=vm((E, D), BF16),
         cote=vm((E, D), BF16),
@@ -1151,13 +1238,15 @@
             shape((1, z.Hs), F32),
         ],
         in_specs=[pl.BlockSpec(memory_space=space) for space in (anywhere, anywhere, vm, vm)],
-        out_specs=[pl.BlockSpec(memory_space=space) for space in [anywhere] * 5 + [vm] * 3],
+        out_specs=[pl.BlockSpec(memory_space=space) for space in [anywhere] * 8],
         scratch_shapes=[
             vm((Hp, D), F32),
             vm((TAPS, Hp, HP), F32),
             vm((Hp, D), F32),
-            vm((8, LANES), F32),
-            pltpu.SemaphoreType.DMA((z.R + 4,)),
+            vm((1, z.Dt), F32),
+            vm((1, z.Hs), F32),
+            vm((1, z.Hs), F32),
+            pltpu.SemaphoreType.DMA((z.R + 7,)),
         ],
         compiler_params=pltpu.CompilerParams(vmem_limit_bytes=12 * 2**20),
     )(*results)

time: 110 us -> 106 us (0.964)
  Pallas kernels: 109 us -> 105 us
    pallas_call x1, Pallas kernels: 105 us -> 102 us  [shards(): pl.pallas_call(functools.partial(kernel, z, names), out_shape=[near(shape...]
where the time goes in v4:
time: 106 us
  Pallas kernels  105 us (99%)
    pallas_call x1, Pallas kernels, shards(): pl.pallas_call(functools.partial(kernel, z, names), out_shape=[near(shape...  102 us
    pallas_call x1, Pallas kernels, shards(): pl.pallas_call(functools.partial(finish, z), out_shape=[shape((z.R, z.Dt,...  3.23 us

profile of v4, /device:TPU:0, one launch (start us, length us, event | category | flops | bytes accessed | tf_op | source)
XLA Modules:
  0.0 105.6 jit_solution(7468743238850215577)
XLA Ops:
  0.6 101.5 %shard_map.152 = (bf16[8,160,256]{2,1,0:T(8,128)(2,1)S(1)}, bf16[8,256,1280]{2,1,0:T(8,128)(2,1)S(1)}, bf16[4,12,80,128]{3,2,1,0:T(8,128)(2,1)S(1)}, f32[2,24,128]{2,1,0:T(8,128)S(1)}) custom-call(bf16[8,256,1280]{2,1,0:T(8,128)(2,1)} %refs_0_.1, s32[8,256]{1,0:T(8,128)} %refs_1_.1, bf16[80,1280]{1,0:T(8,128)(2,1)} %bitcast.14, ...), custom_call_target="tpu_custom_call" | custom-call | tf_op jit(solution)/shard_map/pallas_call | solution.py:1215
  102.2 3.2 %shard_map.153 = (bf16[8,160,256]{2,1,0:T(8,128)(2,1)}, bf16[8,256,1280]{2,1,0:T(8,128)(2,1)}, f32[80,1280]{1,0:T(8,128)}, f32[5,80,640]{2,1,0:T(8,128)}, f32[80...) custom-call(bf16[8,160,256]{2,1,0:T(8,128)(2,1)S(1)} %get-tuple-element.20.refs_0_, ...), custom_call_target="tpu_custom_call" | custom-call | tf_op jit(solution)/shard_map/pallas_call | solution.py:1228

commit v5 on v4

--- a/solution.py
+++ b/solution.py
@@ -346,15 +346,18 @@
 
         only(at_end, go)
 
-    def weights_across(k):
-        if z.square:
-            arrived(corner[k], wg.at[0, rounds(k), pl.ds(0, Z - 1), core])
-        for j in steps:
-            place = wg.at[sd if z.square else pl.ds(0, S), rounds(k), origins[j], core]
-            if not z.square:
-                for copy in plane_any[k, j]:
-                    copy.wait_recv()
-            push(place, place, partner, *across[k])
+    def weights_across(k, at_end=None):
+        def go():
+            if z.square:
+                arrived(corner[k], wg.at[0, rounds(k), pl.ds(0, Z - 1), core])
+            for j in steps:
+                place = wg.at[sd if z.square else pl.ds(0, S), rounds(k), origins[j], core]
+                if not z.square:
+                    for copy in plane_any[k, j]:
+                        copy.wait_recv()
+                push(place, place, partner, *across[k])
+
+        go() if at_end is None else only(at_end, go)
 
     def weights_ready(k):
         arrived(across[k][0], every(wg, k, every_chip, 1 - core))
@@ -487,9 +490,9 @@
 
     weights_ready(0)
     r.hid[...] = lax.dot_general(r.act0[...], first_weight(), NT, preferred_element_type=F32)
-    weights_corner(2, False)
+
     weights_corner(3, True)
-    weights_across(1)
+    weights_across(1, True)
 
     def inner_norm(which, act_store, first, count, size):
         gain = r.gains[which : which + 1, :]
@@ -528,7 +531,9 @@
         taps[:, k * HP : (k + 1) * HP] = (
             act1[PAD + offset : PAD + offset + E, :] * r.mask[:, k : k + 1]
         ).astype(BF16)
-
+    weights_corner(2, False)
+    weights_corner(3, False)
+    weights_across(1, False)
 
     def tap_term(k):
         return lax.dot_general(
@@ -551,21 +556,22 @@
         only(at_end, go)
 
     cotangent_in(False)
+    weights_across(2, True)
     weights_ready(1)
     total = tap_term(0) + tap_term(1)
-    weights_corner(3, False)
     for k in by_all:
         weights_along(k, False, third)
-    weights_across(2)
+    cotangent_in(True)
+    weights_across(2, False)
     weights_ready(2)
     for k in range(2, TAPS):
         total = total + tap_term(k)
+        if k == 3:
+            weights_across(3)
     r.hid[...] = total
     for k in by_all:
         weights_along(k, True)
-    weights_across(3)
-
-    cotangent_in(True)
+
 
     act2 = r.act2
 
@@ -619,13 +625,19 @@
     swaps, plane1, plane2, along_back, first_copies = {}, {}, {}, {}, {}
     some_sums = r.ff.at[pl.ds(0, S - 1), pl.ds(0, z.NF)]
     spread_out = shared(some_sums)
-    beside, over, own_sums = {}, {}, []
-
+    beside, over, z_sends, own_sums = {}, {}, {}, []
+
+    plane_sends = {}
     for k in [3, *some_rest, 2, 1, 0]:
         place = every(g, k, every_chip, 1 - core)
         to = rc.at[pl.ds(0, z.rest), z.NF] if k == REST else rc.at[:, rounds(k)]
-        swaps[k] = remote(place, to, partner)
-        sent.append(swaps[k])
+        if z.square and z.line and k != REST:
+            a, b = cuts[k]
+            plane_sends[k] = sendings()
+            together.append((plane_sends[k], wg.at[pl.ds(0, b - a), pl.ds(0, 7), :, 0]))
+        swaps[k] = remote(place, to, partner, None, plane_sends.get(k))
+        if k not in plane_sends:
+            sent.append(swaps[k])
 
     def add_swapped(k):
         swaps[k].wait_recv()
@@ -641,7 +653,10 @@
         span = rounds(k)
         if k not in plane1:
             if z.square:
-                over_x, over_y = shared(r.rx.at[:, span]), shared(r.ry.at[:, span])
+                if k in plane_sends:
+                    over_x, over_y = ((arrivals(1), plane_sends[k]) for _ in range(2))
+                else:
+                    over_x, over_y = shared(r.rx.at[:, span]), shared(r.ry.at[:, span])
                 plane1[k] = [(over_x[0], r.rx.at[:, span]), (over_y[0], r.ry.at[:, span])]
                 first_copies[k] = [
                     remote(g.at[sx, span, near, core], r.rx.at[0, span], x_side, *over_x),
@@ -679,8 +694,8 @@
             add_into(sy, n, near, r.rx[1, n])
             add_into(sx, n, far, r.ry[1, n])
         plane2[k] = [
-            push(g.at[sy, span, near, core], r.ry2.at[span], y_side),
-            push(g.at[sx, span, far, core], r.rx2.at[span], x_side),
+            push(g.at[sy, span, near, core], r.ry2.at[span], y_side, None, plane_sends.get(k)),
+            push(g.at[sx, span, far, core], r.rx2.at[span], x_side, None, plane_sends.get(k)),
         ]
         for n in range(a, b):
             add_into(s, n, near, r.rx[0, n])
@@ -712,14 +727,21 @@
 
     def z_start(k):
         if z.line:
-            beside[k] = arrivals(1)
-            copy = remote(
-                carried(g, k, pl.ds(1 - upper, 3), core),
-                r.rz_end.at[rows_of(k)],
-                at_layer(middle),
-                beside[k],
-            )
-            push_if(inner == 0, copy)
+            beside[k] = arrivals(2)
+            z_sends[k] = sendings()
+            blocks = len(sums_of(k))
+            together.append((z_sends[k], wg.at[pl.ds(0, blocks), pl.ds(0, 3), 0, 0]))
+            for n, (which, to) in enumerate(
+                [(pl.ds(2 - 2 * upper, 2), pl.ds(1 - upper, 2)), (middle, 2 * upper)]
+            ):
+                copy = remote(
+                    carried(g, k, which, core),
+                    r.rz_end.at[rows_of(k), to],
+                    at_layer(middle),
+                    beside[k] + n,
+                    z_sends[k],
+                )
+                only(True, copy.start)
         else:
             along_back[k] = [
                 push(carried(g, k, z_at(i), core), r.rz.at[i, rows_of(k)], dev_z(i)) for i in steps
@@ -730,13 +752,12 @@
             over[k] = arrivals(1)
             pair = pl.ds(2 - 2 * upper, 2)
             copy = remote(
-                carried(g, k, pair, core), r.rz_pair.at[rows_of(k)], at_layer(3 - layer), over[k]
+                carried(g, k, pair, core), r.rz_pair.at[rows_of(k)], at_layer(3 - layer), over[k], z_sends[k]
             )
-            sent_if.append((inner == 1, copy))
 
             @pl.when(inner == 1)
             def _():
-                arrived(beside[k], r.rz_end.at[rows_of(k)])
+                arrived(beside[k], r.rz_end.at[rows_of(k), pl.ds(1 - upper, 2)])
                 for q, n, b in sums_of(k):
                     add_into(q, n, pair, r.rz_end[b, pl.ds(1 - upper, 2)])
                 copy.start()
@@ -744,9 +765,8 @@
     def z_middle(k):
         if z.line:
             along_back[k] = remote(
-                carried(g, k, end, core), r.rz_one.at[rows_of(k)], at_layer(end)
+                carried(g, k, end, core), r.rz_one.at[rows_of(k)], at_layer(end), None, z_sends[k]
             )
-            sent_if.append((inner == 1, along_back[k]))
 
             @pl.when(inner == 1)
             def _():
@@ -754,35 +774,45 @@
                 for q, n, b in sums_of(k):
                     add_into(q, n, pl.ds(2 * upper, 2), r.rz_pair[b])
                 along_back[k].start()
+                arrived(beside[k] + 1, r.rz_end.at[rows_of(k), 2 * upper])
                 for q, n, b in sums_of(k):
                     sums = g[q, n, layer, core].astype(F32) + r.rz_end[b, 2 * upper].astype(F32)
                     r.ff_own[b] = sums.astype(BF16)
 
-    def to_all(k):
-        if z.line:
-
-            @pl.when(inner == 0)
-            def _():
+    own_copies = {}
+
+    def to_all(k, at_end):
+        place = r.ff_own.at[rows_of(k)]
+        if k != REST and k not in own_copies:
+            counts[2] += 1
+            own_copies[k] = pltpu.make_async_copy(
+                place, r.ff.at[s, rounds(k)], local.at[counts[2] - 1]
+            )
+            own_sums.append(own_copies[k])
+
+        def go():
+            if not z.line:
+                for copy in along_back[k]:
+                    copy.wait_recv()
+                for q, n, b in sums_of(k):
+                    sums = g[q, n, layer, core].astype(F32)
+                    for i in steps:
+                        sums = sums + r.rz[i, b].astype(F32)
+                    r.ff_own[b] = sums.astype(BF16)
+            elif at_end:
                 along_back[k].wait_recv()
                 for q, n, b in sums_of(k):
                     sums = g[q, n, layer, core].astype(F32) + r.rz_one[b].astype(F32)
                     r.ff_own[b] = sums.astype(BF16)
-        else:
-            for copy in along_back[k]:
-                copy.wait_recv()
-            for q, n, b in sums_of(k):
-                sums = g[q, n, layer, core].astype(F32)
-                for i in steps:
-                    sums = sums + r.rz[i, b].astype(F32)
-                r.ff_own[b] = sums.astype(BF16)
-        place = r.ff_own.at[rows_of(k)]
-        for i in range(1, S):
-            if k == REST:
-                push(place, r.others.at[i], (seq_at(i), t), *for_others)
-            else:
-                push(place, r.ff.at[s, rounds(k)], (seq_at(i), t), *spread_out)
-        if k != REST:
-            own_sums.append(move(place, r.ff.at[s, rounds(k)]))
+            for i in range(1, S):
+                if k == REST:
+                    push(place, r.others.at[i], (seq_at(i), t), *for_others)
+                else:
+                    push(place, r.ff.at[s, rounds(k)], (seq_at(i), t), *spread_out)
+            if k != REST:
+                own_copies[k].start()
+
+        only(at_end, go)
 
     def rest_end():
         arrived(for_others[0], some_others)
@@ -871,6 +901,7 @@
     for k in some_rest:
         z_start(k)
     conv_gradients(True)
+    to_plane(2, True)
 
     back = r.back
     for j, offset in enumerate(OFFSETS):
@@ -886,7 +917,6 @@
         total = term if total is None else total + term
     r.hid[RIM : RIM + N, :] = total
 
-    to_plane(2, True)
     dhid1 = r.dhid1
 
     def keep_dhid1(row, grad):
@@ -983,7 +1013,7 @@
     later[3]()
     later[4]()
     rows_along([0], [2], False)
-    rows_along([2], [1], False)
+    rows_along([2, 3, 4], [1], False)
     rows_along([1], [2], False)
 
     arrived(vec_plane[0], r.vec_plane.at[pl.ds(1, S - 1)])
@@ -994,13 +1024,11 @@
         push(vec_sum, r.vec_z.at[i - 1], dev_z(i), *vec_z)
 
     turn_plane(0)
-    rows_along([3], [1], False)
     z_over(2)
     rows_along([2], [2], False)
-    for k in some_rest:
+    for k in [*some_rest, 3]:
         z_middle(k)
-    z_middle(3)
-    rows_along([4], [1], False)
+        to_all(k, False)
     to_z(1)
     z_start(1)
     rows_along([0], [3], False)
@@ -1009,19 +1037,21 @@
     rows_along([1], [3], False)
     z_over(1)
     z_middle(2)
+    to_all(2, False)
     z_over(0)
     rows_along([3, 4], [2], False)
     for k in some_rest:
-        to_all(k)
-    to_all(3)
+        to_all(k, True)
+    to_all(3, True)
     rows_along([2], [3], False)
     z_middle(1)
+    to_all(1, False)
     rows_along([0, 1, 2, 3, 4], [1], True)
     rows_along([0, 1], [2], True)
     z_middle(0)
-    to_all(2)
-    to_all(1)
-    to_all(0)
+    to_all(0, False)
+    for k in (2, 1, 0):
+        to_all(k, True)
     rows_along([3, 4], [3], False)
     rows_along([2, 3, 4], [2], True)
     rows_along([0, 1], range(3, Z), True)
@@ -1148,8 +1178,8 @@
     NB = z.NF + z.rest
     near = vm if z.line else jax.ShapeDtypeStruct
     scratch = dict(
-        send=pltpu.SemaphoreType.DMA((72 if z.line else 800,)),
-        recv=pltpu.SemaphoreType.DMA((118 if z.line else 800,)),
+        send=pltpu.SemaphoreType.DMA((46 if z.line else 800,)),
+        recv=pltpu.SemaphoreType.DMA((123 if z.line else 800,)),
         local=pltpu.SemaphoreType.DMA((14,)),
         xe=vm((E, D), BF16),
         cote=vm((E, D), BF16),

time: 106 us -> 106 us (level)
  no operation moved by 1% of the time
where the time goes in v5:
time: 106 us; the launch traced here: 105 us
  Pallas kernels  105 us (99%)
    pallas_call x1, Pallas kernels, shards(): pl.pallas_call(functools.partial(kernel, z, names), out_shape=[near(shape...  101 us
    pallas_call x1, Pallas kernels, shards(): pl.pallas_call(functools.partial(finish, z), out_shape=[shape((z.R, z.Dt,...  3.23 us

profile of v5, /device:TPU:0, one launch (start us, length us, event | category | flops | bytes accessed | tf_op | source)
XLA Modules:
  0.0 105.5 jit_solution(18085483334864242599)
XLA Ops:
  0.6 101.5 %shard_map.152 = (bf16[8,160,256]{2,1,0:T(8,128)(2,1)S(1)}, bf16[8,256,1280]{2,1,0:T(8,128)(2,1)S(1)}, bf16[4,12,80,128]{3,2,1,0:T(8,128)(2,1)S(1)}, f32[2,24,128]{2,1,0:T(8,128)S(1)}) custom-call(bf16[8,256,1280]{2,1,0:T(8,128)(2,1)} %refs_0_.1, s32[8,256]{1,0:T(8,128)} %refs_1_.1, bf16[80,1280]{1,0:T(8,128)(2,1)} %bitcast.14, ...), custom_call_target="tpu_custom_call" | custom-call | tf_op jit(solution)/shard_map/pallas_call | solution.py:1245
  102.1 3.2 %shard_map.153 = (bf16[8,160,256]{2,1,0:T(8,128)(2,1)}, bf16[8,256,1280]{2,1,0:T(8,128)(2,1)}, f32[80,1280]{1,0:T(8,128)}, f32[5,80,640]{2,1,0:T(8,128)}, f32[80...) custom-call(bf16[8,160,256]{2,1,0:T(8,128)(2,1)S(1)} %get-tuple-element.20.refs_0_, ...), custom_call_target="tpu_custom_call" | custom-call | tf_op jit(solution)/shard_map/pallas_call | solution.py:1258

commit v6 on v5

--- a/solution.py
+++ b/solution.py
@@ -842,9 +842,14 @@
     def conv_gradients(at_end):
         def go():
             dhid2_t = dhid2[PAD + RIM : PAD + RIM + N, :].T.astype(BF16)
-            grad_units(z.nd, dhid2_t, lambda c, w: taps[own, c : c + w], TAPS * z.nh)
-            for k in (2, 1):
-                swaps[k].start()
+            ahead = max(z.chunks[2][0] * S - z.nd, 0)
+            skip = ahead * LANES
+            later_units = TAPS * z.nh - ahead
+            grad_units(z.nd + ahead, dhid2_t, lambda c, w: taps[own, skip + c : skip + c + w], later_units)
+            swaps[2].start()
+            grad_units(z.nd, dhid2_t, lambda c, w: taps[own, c : c + w], ahead)
+            if not at_end:
+                swaps[1].start()
 
         only(at_end, go)
 
@@ -902,6 +907,7 @@
         z_start(k)
     conv_gradients(True)
     to_plane(2, True)
+    only(True, swaps[1].start)
 
     back = r.back
     for j, offset in enumerate(OFFSETS):

time: 106 us -> 106 us (level)
  no operation moved by 1% of the time
where the time goes in v6:
time: 106 us; the launch traced here: 105 us
  Pallas kernels  105 us (99%)
    pallas_call x1, Pallas kernels, shards(): pl.pallas_call(functools.partial(kernel, z, names), out_shape=[near(shape...  101 us
    pallas_call x1, Pallas kernels, shards(): pl.pallas_call(functools.partial(finish, z), out_shape=[shape((z.R, z.Dt,...  3.23 us

profile of v6, /device:TPU:0, one launch (start us, length us, event | category | flops | bytes accessed | tf_op | source)
XLA Modules:
  0.0 105.5 jit_solution(9773042002681608660)
XLA Ops:
  0.6 101.5 %shard_map.152 = (bf16[8,160,256]{2,1,0:T(8,128)(2,1)S(1)}, bf16[8,256,1280]{2,1,0:T(8,128)(2,1)S(1)}, bf16[4,12,80,128]{3,2,1,0:T(8,128)(2,1)S(1)}, f32[2,24,128]{2,1,0:T(8,128)S(1)}) custom-call(bf16[8,256,1280]{2,1,0:T(8,128)(2,1)} %refs_0_.1, s32[8,256]{1,0:T(8,128)} %refs_1_.1, bf16[80,1280]{1,0:T(8,128)(2,1)} %bitcast.14, ...), custom_call_target="tpu_custom_call" | custom-call | tf_op jit(solution)/shard_map/pallas_call | solution.py:1251
  102.1 3.2 %shard_map.153 = (bf16[8,160,256]{2,1,0:T(8,128)(2,1)}, bf16[8,256,1280]{2,1,0:T(8,128)(2,1)}, f32[80,1280]{1,0:T(8,128)}, f32[5,80,640]{2,1,0:T(8,128)}, f32[80...) custom-call(bf16[8,160,256]{2,1,0:T(8,128)(2,1)S(1)} %get-tuple-element.20.refs_0_, ...), custom_call_target="tpu_custom_call" | custom-call | tf_op jit(solution)/shard_map/pallas_call | solution.py:1264
